TPU v7x, 32 devices: a whole 2x2x4 slice. The times are simulated.
32 devices in a mesh: leaf: 8 (over z, y), grid: 4 (over x, core).
Axes of the slice: x: 2, y: 2, z: 4, core: 2. Of those that a mesh axis runs over, the one named last changes fastest.
Arguments:
- rhs: bfloat16 [5, 16, 256, 256], P(None, 'leaf', 'grid'), may hold values from -6 to 6
- fwd_inv: bfloat16 [5, 16, 256, 256], P(None, 'leaf', 'grid')
- bwd_inv: bfloat16 [5, 16, 256, 256], P(None, 'leaf', 'grid')
- upd_t: bfloat16 [4, 16, 256, 512], P(None, 'leaf', 'grid'), may hold values from -0.25 to 0.25
- bwd_t: bfloat16 [4, 16, 512, 256], P(None, 'leaf', 'grid'), may hold values from -0.1875 to 0.1875
- dest_owner: int32 [4, 8, 4, 256, 1], P(None, 'leaf', 'grid'), may hold values from 0 to 7; in each aligned block of 256 rows (0 to 255, 256 to 511, ..., all dimensions but the last counted through in order) at most 85 rows name the same one
- dest_row: int32 [4, 8, 4, 256], P(None, 'leaf', 'grid'), may hold values from 128 to 639, as said below
Outputs:
- solution: bfloat16 [5, 16, 256, 256], P(None, 'leaf', 'grid')
Inputs may be any that keep to these rules, and one draw needn't show every extreme that they name: `dest_owner`: in the rows of one device at one level (one aligned block of 256), no owner is named more than 85 times, a bound that some block reaches. `dest_row`: an entry of level l reaches a row of a later level: it lies from (l + 1) * 2 * 64 to 639.
All inputs are finite; a program needn't handle non-finite values.
Results may differ from a plain program's by a relative error of at most 0.025.
Values may be sent and summed in bfloat16 or wider, within the bound.
No kernel may reach another device: no remote copies, remote signals or barrier semaphores. Data moves between devices by JAX's collectives and lax.ppermute only.
A program may use at most 64 MiB of HBM per device.

v0:
```python
import functools

import jax
import jax.numpy as jnp
from jax import lax
from jax.experimental import pallas as pl
from jax.experimental.pallas import tpu as pltpu
from jax.sharding import PartitionSpec as P

BF = jnp.bfloat16
F32 = jnp.float32
LANES = 128
ROWS_AT_ONCE = 256
VMEM_BYTES = 48 * 1024 * 1024


def nn(a, b):
    return lax.dot_general(a, b, (((1,), (0,)), ((), ())), preferred_element_type=F32)


def nt(a, b):
    return lax.dot_general(a, b, (((1,), (1,)), ((), ())), preferred_element_type=F32)


class Plan:
    def __init__(self, mesh, rhs, upd_t, bwd_t):
        self.levels, self.kept, self.rows, self.columns = rhs.shape
        self.leaves, self.groups = mesh.shape["leaf"], mesh.shape["grid"]
        self.parts = 2 if self.leaves % 2 == 0 else 1
        self.owners = self.leaves // self.parts
        self.supers = self.parts * self.kept
        self.chunk = self.columns // (self.groups * self.parts)
        self.width = self.rows * self.groups
        self.update_rows = upd_t.shape[3]
        self.group_rows = bwd_t.shape[2]
        self.slab = (self.supers * self.chunk, self.width)
        self.targets = self.supers * self.owners * self.rows
        self.sources = self.supers * self.group_rows
        self.blocks = [(dp, dg) for dp in range(self.parts) for dg in range(self.groups)]

    def place(self):
        leaf, grid = lax.axis_index("leaf"), lax.axis_index("grid")
        return leaf // self.parts, leaf % self.parts, grid


def fetch(plan, blocks, pieces, sems):
    _, part, grid = plan.place()
    copies = []
    for slab, make in pieces:
        group = []
        for ref, (dp, dg) in zip(blocks, plan.blocks):
            copy = pltpu.make_async_copy(
                ref.at[slab],
                make(part ^ dp, grid ^ dg),
                sems.at[len(copies) * len(plan.blocks) + len(group)],
            )
            copy.start()
            group.append(copy)
        copies.append(group)
    return copies


def wait(group):
    for copy in group:
        copy.wait()


def matrix(plan, ref, s):
    whole = ref[s // plan.kept, s % plan.kept]
    return whole.reshape(-1, whole.shape[-1])


def pick_columns(plan, ref):
    _, part, grid = plan.place()
    first = (part * plan.groups + grid) * plan.chunk
    shape = (plan.chunk, plan.columns)
    pick = lax.broadcasted_iota(jnp.int32, shape, 1) == first + lax.broadcasted_iota(jnp.int32, shape, 0)
    pick = jnp.where(pick, 1.0, 0.0).astype(BF)
    return jnp.concatenate([nt(pick, matrix(plan, ref, s)) for s in range(plan.supers)], axis=0)


def onehot(keys, first, rows):
    iota = lax.broadcasted_iota(jnp.int32, (rows, keys.shape[1]), 0)
    return jnp.where(iota == keys - first, 1.0, 0.0).astype(BF)


def cross(even, odd):
    half = even.shape[1] // 2
    low = lax.broadcasted_iota(jnp.int32, even.shape, 1) < half
    return (
        jnp.where(low, even, pltpu.roll(odd, half, 1)),
        jnp.where(low, pltpu.roll(even, half, 1), odd),
    )


def scatter(plan, sent, key_ref, level_to, emit):
    c, per = plan.chunk, max(1, ROWS_AT_ONCE // plan.rows)
    per = min(per, plan.owners)
    for pair in range(plan.groups // 2):
        given = []
        for g in (2 * pair, 2 * pair + 1):
            lanes = slice(g * plan.group_rows, (g + 1) * plan.group_rows)
            given.append(
                jnp.concatenate([sent[s * c : (s + 1) * c, lanes] for s in range(plan.supers)], axis=1)
            )
        for s in range(plan.supers):
            for first in range(0, plan.owners, per):
                row = level_to * plan.targets + (s * plan.owners + first) * plan.rows
                even, odd = [
                    nt(given[i], onehot(key_ref[2 * pair + i : 2 * pair + i + 1, :], row, per * plan.rows))
                    for i in range(2)
                ]
                for j in range(0, per, 2):
                    at = slice(j * plan.rows, (j + 2) * plan.rows)
                    one, two = cross(even[:, at], odd[:, at])
                    emit(first + j, s, pair, one)
                    emit(first + j + 1, s, pair, two)


def gather(plan, slabs, key_ref, level_from, g):
    c, pair = plan.chunk, g // 2
    lanes = slice(pair * LANES, (pair + 1) * LANES)
    total = None
    per = min(plan.owners, max(2, 4 * ROWS_AT_ONCE // plan.rows))
    for s in range(plan.supers):
        for first in range(0, plan.owners, per):
            given = []
            for d in range(first, first + per, 2):
                even, odd = [slabs[d + i][s * c : (s + 1) * c, lanes].astype(F32) for i in range(2)]
                given.append(cross(even, odd)[g % 2])
            row = level_from * plan.targets + (s * plan.owners + first) * plan.rows
            term = nn(
                jnp.concatenate(given, axis=1).astype(BF),
                onehot(key_ref[g : g + 1, :], row, per * plan.rows),
            )
            total = term if total is None else total + term
    return total


def forward_kernel(plan, level, part_of, fresh, added, *refs):
    refs = list(refs)
    key_ref = None if level == plan.levels - 1 else refs.pop(0)
    start_ref = None if fresh else refs.pop(0)
    arrived = [] if fresh else [refs.pop(0) for _ in range(plan.owners)]
    more_ref = refs.pop(0) if added else None
    blocks = [refs.pop(0) for _ in plan.blocks]
    out_ref = refs.pop(0)
    last = level == plan.levels - 1
    if last:
        solved_ref = refs.pop(0)
    else:
        sent_ref = refs.pop(0)
        slab_refs = [refs.pop(0) for _ in range(plan.owners)]
    if fresh:
        rhs_ref = refs.pop(0)
    inv_ref = refs.pop(0)
    if last:
        back_ref = refs.pop(0)
    else:
        upd_ref = refs.pop(0)
    sems = refs.pop(0)
    c = plan.chunk

    pieces = []
    if fresh:
        pieces.append((part_of["rhs"], lambda p, g: rhs_ref.at[p, :, g]))
    pieces.append((part_of["fwd"], lambda p, g: inv_ref.at[p, :, g]))
    if last:
        pieces.append((part_of["inv"], lambda p, g: back_ref.at[p, :, g]))
    else:
        for half in range(plan.update_rows // plan.width):
            pieces.append((part_of["upd"] + half, lambda p, g, half=half: upd_ref.at[half, p, :, g]))
    copies = fetch(plan, blocks, pieces, sems)

    if fresh:
        wait(copies.pop(0))
        block = pick_columns(plan, rhs_ref)
    else:
        block = start_ref[...] - arrived[0][...]
        for ref in arrived[1:]:
            block = block - ref[...].astype(F32)
    block = block.astype(BF)
    wait(copies.pop(0))
    solved = jnp.concatenate(
        [nt(block[s * c : (s + 1) * c], matrix(plan, inv_ref, s)) for s in range(plan.supers)], axis=0
    )
    out_ref[...] = solved
    lowered = solved.astype(BF)
    for group in copies:
        wait(group)
    if last:
        for s in range(plan.supers):
            at = slice(s * c, (s + 1) * c)
            solved_ref[at, :] = nt(lowered[at], matrix(plan, back_ref, s)).astype(BF)
        return
    for s in range(plan.supers):
        at = slice(s * c, (s + 1) * c)
        for half in range(plan.update_rows // plan.width):
            sent_ref[at, half * plan.width : (half + 1) * plan.width] = nn(
                lowered[at], matrix(plan, upd_ref.at[half], s)
            ).astype(BF)

    def emit(distance, s, pair, value):
        at, lanes = slice(s * c, (s + 1) * c), slice(pair * LANES, (pair + 1) * LANES)
        if more_ref is not None:
            value = value + more_ref[distance, at, lanes]
        slab_refs[distance][at, lanes] = value.astype(slab_refs[distance].dtype)

    scatter(plan, sent_ref[...], key_ref, level + 1, emit)


def ahead_kernel(plan, level, part_of, *refs):
    refs = list(refs)
    far = level < plan.levels - 1
    sent = [refs.pop(0) for _ in range(level)] if far else []
    key_refs = [refs.pop(0) for _ in sent]
    blocks = [refs.pop(0) for _ in plan.blocks]
    start_ref = refs.pop(0)
    more_ref = refs.pop(0) if far else None
    rhs_ref, sems = refs
    copies = fetch(plan, blocks, [(part_of["rhs"], lambda p, g: rhs_ref.at[p, :, g])], sems)
    c = plan.chunk
    for i, (ref, key_ref) in enumerate(zip(sent, key_refs)):

        def emit(distance, s, pair, value, first=i == 0):
            at, lanes = slice(s * c, (s + 1) * c), slice(pair * LANES, (pair + 1) * LANES)
            if not first:
                value = value + more_ref[distance, at, lanes]
            more_ref[distance, at, lanes] = value

        scatter(plan, ref[...], key_ref, level + 1, emit)
    wait(copies[0])
    start_ref[...] = pick_columns(plan, rhs_ref)


def known_kernel(plan, froms, *refs):
    key_ref, out_ref = refs[0], refs[-1]
    slabs = [refs[1 + i * plan.owners : 1 + (i + 1) * plan.owners] for i in range(len(froms))]
    for g in range(plan.groups):
        total = None
        for level_from, own in zip(froms, slabs):
            term = gather(plan, own, key_ref, level_from, g)
            total = term if total is None else total + term
        out_ref[g] = total.astype(BF)


def backward_kernel(plan, level, part_of, known, *refs):
    refs = list(refs)
    key_ref = refs.pop(0)
    slabs = [refs.pop(0) for _ in range(plan.owners)]
    known_ref = refs.pop(0) if known else None
    forward_ref = refs.pop(0)
    blocks = [refs.pop(0) for _ in plan.blocks]
    solved_ref, upper_ref, inv_ref, sems = refs
    c, half_rows = plan.chunk, plan.rows
    pieces = [
        (
            part_of["upper"] + h,
            lambda p, g, h=h: upper_ref.at[p, :, g, pl.ds(h * half_rows, half_rows)],
        )
        for h in range(plan.group_rows // half_rows)
    ]
    pieces.append((part_of["inv"], lambda p, g: inv_ref.at[p, :, g]))
    copies = fetch(plan, blocks, pieces, sems)
    pulled = []
    for g in range(plan.groups):
        found = gather(plan, slabs, key_ref, level + 1, g)
        if known:
            found = found + known_ref[g].astype(F32)
        pulled.append(found.astype(BF))
    for group in copies:
        wait(group)
    for s in range(plan.supers):
        at = slice(s * c, (s + 1) * c)
        lanes = slice(s * plan.group_rows, (s + 1) * plan.group_rows)
        upper = nn(jnp.concatenate([p[:, lanes] for p in pulled], axis=1), matrix(plan, upper_ref, s))
        reduced = (forward_ref[at, :] - upper).astype(BF)
        solved_ref[at, :] = nt(reduced, matrix(plan, inv_ref, s)).astype(BF)


def pieces_kernel(plan, *refs):
    _, part, grid = plan.place()
    slabs, outs = refs[: plan.levels], refs[plan.levels :]
    rows = plan.kept * plan.chunk
    for out, (dp, dg) in zip(outs, plan.blocks):
        first = pl.multiple_of((part ^ dp) * rows, rows)
        lane = pl.multiple_of((grid ^ dg) * plan.rows // LANES * LANES, LANES)
        for level, slab in enumerate(slabs):
            out[level] = slab[pl.ds(first, rows), pl.ds(lane, LANES)]


def result_kernel(plan, *refs):
    _, part, grid = plan.place()
    refs = list(refs)
    scratch, out = refs.pop(), refs.pop()
    c = plan.chunk
    shape = (plan.rows, LANES)
    lane = lax.broadcasted_iota(jnp.int32, shape, 1) - grid * plan.rows % LANES
    pick = jnp.where(lane == lax.broadcasted_iota(jnp.int32, shape, 0), 1.0, 0.0).astype(BF)
    for level in range(plan.levels):
        for k in range(plan.kept):
            for ref, (dp, dg) in zip(refs, plan.blocks):
                at = ((part ^ dp) * plan.groups + (grid ^ dg)) * c
                scratch[level, k, pl.ds(pl.multiple_of(at, c), c), :] = ref[level, k * c : (k + 1) * c, :]
    for level in range(plan.levels):
        for k in range(plan.kept):
            out[level, k] = nt(pick, scratch[level, k]).astype(BF)


VM = pl.BlockSpec(memory_space=pltpu.VMEM)
ANY = pl.BlockSpec(memory_space=pl.ANY)


def call(body, args, specs, outs, scratch, flops, moved):
    return pl.pallas_call(
        body,
        in_specs=specs,
        out_specs=[VM] * len(outs),
        out_shape=[jax.ShapeDtypeStruct(shape, dtype) for shape, dtype in outs],
        scratch_shapes=scratch,
        compiler_params=pltpu.CompilerParams(vmem_limit_bytes=VMEM_BYTES),
        cost_estimate=pl.CostEstimate(flops=flops, bytes_accessed=moved, transcendentals=0),
    )(*args)


def solve(plan, rhs, fwd_inv, bwd_inv, upd_t, bwd_t, dest_owner, dest_row):
    levels, owners = plan.levels, plan.owners
    owner_at, part, grid = plan.place()

    def over_leaf(x, step):
        return lax.ppermute(x, "leaf", [(i, i ^ step) for i in range(plan.leaves)])

    def over_grid(x, step):
        return lax.ppermute(x, "grid", [(i, i ^ step) for i in range(plan.groups)])

    per_owner = levels * plan.kept * plan.rows
    code = dest_owner.reshape(levels - 1, -1) * per_owner + dest_row.reshape(levels - 1, -1)
    pairs = [[i * plan.parts + j for j in range(plan.parts)] for i in range(owners)]
    code = lax.all_gather(code, "leaf", axis=0, axis_index_groups=pairs)
    code = lax.all_gather(code, "grid", axis=0)
    code = code.reshape(plan.groups, plan.parts, levels - 1, plan.group_rows, plan.kept)
    code = jnp.transpose(code, (2, 0, 1, 4, 3)).reshape(levels - 1, plan.groups, plan.sources)
    leaf_to, row_to = code // per_owner, code % per_owner
    super_to = leaf_to % plan.parts * plan.kept + row_to // plan.rows % plan.kept
    distance = (leaf_to // plan.parts) ^ owner_at
    keys = row_to // (plan.kept * plan.rows) * plan.targets
    keys = keys + (super_to * owners + distance) * plan.rows + row_to % plan.rows

    def cut(x):
        k, r, w = x.shape
        x = x.reshape(k, r // plan.rows, plan.rows, w // plan.width, plan.width)
        return jnp.transpose(x, (1, 3, 0, 2, 4)).reshape(-1, k, plan.rows, plan.width)

    where = {}

    def chunk(number, names):
        slabs, at = [], 0
        for name, level in names:
            array = dict(rhs=rhs, fwd=fwd_inv, inv=bwd_inv, upd=upd_t, upper=bwd_t)[name][level]
            slabs.append(cut(array))
            where[name, level] = (number, at)
            at += slabs[-1].shape[0]
        return jnp.concatenate(slabs, axis=0)

    def spread(own, by_leaf_last):
        got = {(0, 0): own}
        high = [1 << b for b in reversed(range(1, (plan.groups - 1).bit_length()))]
        if plan.parts > 1:
            got[1, 0] = over_leaf(own, 1)
        for step in high:
            for dg in [dg for dp, dg in got if dp == 0]:
                got[0, dg ^ step] = over_grid(got[0, dg], step)
                if plan.parts > 1:
                    if by_leaf_last:
                        got[1, dg ^ step] = over_leaf(got[0, dg ^ step], 1)
                    else:
                        got[1, dg ^ step] = over_grid(got[1, dg], step)
        if plan.groups > 1:
            for dp, dg in list(got):
                got[dp, dg ^ 1] = over_grid(got[dp, dg], 1)
        return [got[block] for block in plan.blocks]

    top = levels - 1
    names = [[("rhs", 0), ("fwd", 0), ("upd", 0)]]
    for level in range(1, top):
        names.append([("rhs", level), ("fwd", level), ("upd", level)])
    names[-1] += [("rhs", top), ("fwd", top), ("inv", top)]
    back = [[("upper", level), ("inv", level)] for level in reversed(range(top))]
    half = len(back) // 2
    names.append(sum(back[:half], []))
    names.append(sum(back[half:], []))
    chunks = [spread(chunk(i, part_names), i % 2 == 1) for i, part_names in enumerate(names)]

    def matrices(level, wanted):
        numbers = {where[name, level][0] for name in wanted}
        (number,) = numbers
        return chunks[number], {name: where[name, level][1] for name in wanted}

    full = (plan.parts, plan.kept, plan.groups, plan.rows, plan.width)
    count = len(plan.blocks)
    halves = plan.update_rows // plan.width
    tall = plan.group_rows // plan.rows
    slab_bytes = plan.slab[0] * plan.slab[1] * 2
    one_pass = 2 * plan.targets * plan.sources * plan.groups * LANES

    forward_out, sent, start, arrived, more = [], [], None, [], None
    for level in range(levels):
        last, fresh = level == top, level == 0
        wanted = ["fwd"] + (["rhs"] if fresh else []) + (["inv"] if last else ["upd"])
        blocks, part_of = matrices(level, wanted)
        args, specs = [], []
        if not last:
            args.append(keys[level])
            specs.append(VM)
        if not fresh:
            args += [start] + arrived
            specs += [VM] * (1 + owners)
        if more is not None and not last:
            args.append(more)
            specs.append(VM)
        args += blocks
        specs += [ANY] * count
        outs = [(plan.slab, F32)]
        if last:
            outs.append((plan.slab, BF))
        else:
            outs.append(((plan.slab[0], plan.update_rows), BF))
            outs += [(plan.slab, F32)] + [(plan.slab, BF)] * (owners - 1)
        scratch = [pltpu.VMEM(full, BF)] * (2 if fresh else 1)
        scratch.append(pltpu.VMEM(full if last else (halves,) + full, BF))
        scratch.append(pltpu.SemaphoreType.DMA((count * (2 + halves),)))
        got = call(
            functools.partial(
                forward_kernel, plan, level, part_of, fresh, more is not None and not last
            ),
            args, specs, outs, scratch, one_pass, 24 * slab_bytes,
        )
        forward_out.append(got[0])
        if last:
            solved = got[1]
            break
        sent.append(got[1])
        arrived = [got[2]] + [over_leaf(got[2 + d], d * plan.parts) for d in range(1, owners)]
        ahead_blocks, ahead_part = matrices(level + 1, ["rhs"])
        ahead = level + 1
        is_far = ahead < top
        args = (sent[:ahead] if is_far else []) + ([keys[i] for i in range(ahead)] if is_far else [])
        outs = [(plan.slab, F32)] + ([((owners,) + plan.slab, F32)] if is_far else [])
        got = call(
            functools.partial(ahead_kernel, plan, ahead, ahead_part),
            args + ahead_blocks, [VM] * len(args) + [ANY] * count, outs,
            [pltpu.VMEM(full, BF), pltpu.SemaphoreType.DMA((count,))],
            one_pass * max(1, len(args) // 2), 16 * slab_bytes,
        )
        start, more = got[0], got[1] if is_far else None

    solutions = {top: solved}
    everywhere = {}
    for level in reversed(range(top)):
        above = solutions[level + 1]
        everywhere[level + 1] = [above] + [over_leaf(above, d * plan.parts) for d in range(1, owners)]
        froms = list(range(level + 2, levels))
        known = []
        if froms:
            slabs = sum([everywhere[f] for f in froms], [])
            known = call(
                functools.partial(known_kernel, plan, froms),
                [keys[level]] + slabs, [VM] * (1 + len(slabs)),
                [((plan.groups, plan.chunk, plan.sources), BF)], [],
                one_pass * len(froms), 16 * slab_bytes,
            )
        blocks, part_of = matrices(level, ["upper", "inv"])
        args = [keys[level]] + everywhere[level + 1] + list(known) + [forward_out[level]]
        (solutions[level],) = call(
            functools.partial(backward_kernel, plan, level, part_of, bool(froms)),
            args + blocks, [VM] * len(args) + [ANY] * count, [(plan.slab, BF)],
            [
                pltpu.VMEM((plan.parts, plan.kept, plan.groups, plan.group_rows, plan.width), BF),
                pltpu.VMEM(full, BF),
                pltpu.SemaphoreType.DMA((count * (1 + tall),)),
            ],
            one_pass, 24 * slab_bytes,
        )

    piece = (levels, plan.kept * plan.chunk, LANES)
    own = call(
        functools.partial(pieces_kernel, plan),
        [solutions[level] for level in range(levels)], [VM] * levels,
        [(piece, BF)] * count, [], 1, 8 * slab_bytes,
    )
    both = ("leaf", "grid")

    def swap(x, dp, dg):
        if (dp, dg) == (0, 0):
            return x
        g = plan.groups
        moves = [(i, ((i // g) ^ dp) * g + ((i % g) ^ dg)) for i in range(plan.leaves * g)]
        return lax.ppermute(x, both, moves)

    theirs = [swap(x, dp, dg) for x, (dp, dg) in zip(own, plan.blocks)]
    (result,) = call(
        functools.partial(result_kernel, plan),
        theirs, [VM] * count, [(rhs.shape, BF)],
        [pltpu.VMEM((levels, plan.kept, plan.columns, LANES), BF)], 1, 8 * slab_bytes,
    )
    return result


def solution(mesh):
    def local(rhs, fwd_inv, bwd_inv, upd_t, bwd_t, dest_owner, dest_row):
        plan = Plan(mesh, rhs, upd_t, bwd_t)
        return solve(plan, rhs, fwd_inv, bwd_inv, upd_t, bwd_t, dest_owner, dest_row)

    rows = P(None, "leaf", "grid", None)
    placed = (rows, rows, rows, rows, rows, P(None, "leaf", "grid", None, None), rows)
    return jax.shard_map(local, mesh=mesh, in_specs=placed, out_specs=rows, check_vma=False)
```

profile of v0, /device:TPU:0, one launch (start us, length us, event | category | flops | bytes accessed | tf_op | source)
XLA Modules:
  0.0 228.1 jit_solution(15987353362350223310)
XLA Ops:
  3.6 3.0 %collective-permute-start.10 = (bf16[4,2,64,256]{3,2,1,0:T(8,128)(2,1)S(1)}, bf16[4,2,64,256]{3,2,1,0:T(8,128)(2,1)}, u32[]{:S(2)}, u32[]{:S(2)}) collective-permute-start(bf16[4,2,64,256]{3,2,1,0:T(8,128)(2,1)S(1)} %pad_maximum_fusion.2.refs_1_), channel_id=1, source_target_pairs={{0,4},{4,0},{8,12},{12,8},{16,20},{20,16},{24,28},{28,24},{1,5},{5... | collective-permute-start | bytes 786440 | tf_op jit(solution)/shard_map/ppermute | solution.py:331
  11.2 2.7 %collective-permute-done.10.refs_5_ = bf16[4,2,64,256]{3,2,1,0:T(8,128)(2,1)} collective-permute-done((bf16[4,2,64,256]{3,2,1,0:T(8,128)(2,1)S(1)}, bf16[4,2,64,256]{3,2,1,0:T(8,128)(2,1)}, u32[]{:S(2)}, u32[]{:S(2)}) %collective-permute-start.10) | collective-permute-done | bytes 262176 | tf_op jit(solution)/shard_map/ppermute | solution.py:331
  28.8 3.8 %collective-permute-done.46.refs_10_.refs_11_ = bf16[6,2,64,256]{3,2,1,0:T(8,128)(2,1)} collective-permute-done((bf16[6,2,64,256]{3,2,1,0:T(8,128)(2,1)S(1)}, bf16[6,2,64,256]{3,2,1,0:T(8,128)(2,1)}, u32[]{:S(2)}, u32[]{:S(2)}) %collective-permute-start.46) | collective-permute-done | bytes 393248 | tf_op jit(solution)/shard_map/ppermute | solution.py:331
  37.0 6.0 %collective-permute-done.57.refs_9_ = bf16[6,2,64,256]{3,2,1,0:T(8,128)(2,1)S(1)} collective-permute-done((bf16[6,2,64,256]{3,2,1,0:T(8,128)(2,1)S(1)}, bf16[6,2,64,256]{3,2,1,0:T(8,128)(2,1)S(1)}, u32[]{:S(2)}, u32[]{:S(2)}) %collective-permute-start.57) | collective-permute-done | bytes 393248 | tf_op jit(solution)/shard_map/ppermute | solution.py:334
  43.0 4.3 %all_gather.10 = s32[2,4,256]{2,1,0:T(4,128)S(1)} all-gather(s32[1,4,256]{2,1,0:T(4,128)S(1)} %bitcast_add_fusion), channel_id=1, replica_groups={{0,4},{8,12},{16,20},{24,28},{1,5},{9,13},{17,21},{25,29},{2,6},{10,14}..., dimensions={0}, use_global_device_ids=true | all-gather | bytes 12288 | tf_op jit(solution)/shard_map/all_gather | solution.py:339
  47.3 11.7 %all-gather = s32[8,4,256]{2,1,0:T(4,128)S(1)} all-gather(s32[2,4,256]{2,1,0:T(4,128)S(1)} %all_gather.10), channel_id=2, replica_groups=mesh['leaf'=8,'grid'=4] {'grid'}, dimensions={0}, use_global_device_ids=true | all-gather | bytes 40960 | tf_op jit(solution)/shard_map/all_gather | solution.py:340
  74.8 3.1 %ne.78 = pred[4,2,4,128,2]{4,3,1,0,2:T(8,128)(4,1)} reshape(pred[8,4,256]{2,0,1:T(8,128)(4,1)S(1)} %sign_compare_fusion) | data formatting | bytes 16384 | tf_op jit(solution)/shard_map/jit(floor_divide)/ne | solution.py:343
  86.8 3.6 %shard_map.74 = (f32[128,256]{1,0:T(8,128)S(1)}, bf16[128,512]{1,0:T(8,128)(2,1)S(1)}, f32[128,256]{1,0:T(8,128)S(1)}, bf16[128,256]{1,0:T(8,128)(2,1)S(1)}, bf1...) custom-call(s32[4,512]{1,0:T(4,128)S(1)} %get-tuple-element.105.refs_0_.refs_1_.refs_2_.refs_3_, ...), custom_call_target="tpu_custom_call" | custom-call | flops 536870912 | bytes 1572864 | tf_op jit(solution)/shard_map/pallas_call | solution.py:315
  92.1 2.6 %collective-permute-start.22 = (bf16[128,256]{1,0:T(8,128)(2,1)S(1)}, bf16[128,256]{1,0:T(8,128)(2,1)S(1)}, u32[]{:S(2)}, u32[]{:S(2)}) collective-permute-start(bf16[128,256]{1,0:T(8,128)(2,1)S(1)} %get-tuple-element.47), channel_id=1, source_target_pairs={{0,16},{4,20},{8,24},{12,28},{16,0},{20,4},{24,8},{28,12},{1,17},{... | collective-permute-start | bytes 196616 | tf_op jit(solution)/shard_map/ppermute | solution.py:331
  94.9 4.8 %collective-permute-done.22.refs_4_ = bf16[128,256]{1,0:T(8,128)(2,1)S(1)} collective-permute-done((bf16[128,256]{1,0:T(8,128)(2,1)S(1)}, bf16[128,256]{1,0:T(8,128)(2,1)S(1)}, u32[]{:S(2)}, u32[]{:S(2)}) %collective-permute-start.22) | collective-permute-done | bytes 65568 | tf_op jit(solution)/shard_map/ppermute | solution.py:331
  103.4 3.4 %shard_map.76 = (f32[128,256]{1,0:T(8,128)S(1)}, bf16[128,512]{1,0:T(8,128)(2,1)S(1)}, f32[128,256]{1,0:T(8,128)S(1)}, bf16[128,256]{1,0:T(8,128)(2,1)S(1)}, bf1...) custom-call(s32[4,512]{1,0:T(4,128)S(1)} %get-tuple-element.104.refs_0_.refs_3_.refs_4_, ...), custom_call_target="tpu_custom_call" | custom-call | flops 536870912 | bytes 1572864 | tf_op jit(solution)/shard_map/pallas_call | solution.py:315
  108.0 3.2 %collective-permute-done.31.refs_3_ = bf16[128,256]{1,0:T(8,128)(2,1)S(1)} collective-permute-done((bf16[128,256]{1,0:T(8,128)(2,1)S(1)}, bf16[128,256]{1,0:T(8,128)(2,1)S(1)}, u32[]{:S(2)}, u32[]{:S(2)}) %collective-permute-start.31) | collective-permute-done | bytes 65568 | tf_op jit(solution)/shard_map/ppermute | solution.py:331
  113.4 3.8 %collective-permute-done.32.refs_4_ = bf16[128,256]{1,0:T(8,128)(2,1)S(1)} collective-permute-done((bf16[128,256]{1,0:T(8,128)(2,1)S(1)}, bf16[128,256]{1,0:T(8,128)(2,1)S(1)}, u32[]{:S(2)}, u32[]{:S(2)}) %collective-permute-start.32) | collective-permute-done | bytes 65568 | tf_op jit(solution)/shard_map/ppermute | solution.py:331
  118.9 3.3 %shard_map.77 = (f32[128,256]{1,0:T(8,128)S(1)}, f32[4,128,256]{2,1,0:T(8,128)S(1)}) custom-call(bf16[128,512]{1,0:T(8,128)(2,1)S(1)} %get-tuple-element.43.refs_0_, bf16[128,512]{1,0:T(8,128)(2,1)S(1)} %get-tuple-element.50.refs_1_, s32[4,512]{1,0:T(4,128)S(1)} %get-tuple-element.105.refs_0_.refs_1_.refs_2_.refs_3_, ...), custom_call_target="tpu_custom_call" | custom-call | flops 1073741824 | bytes 1048576 | tf_op jit(solution)/shard_map/pallas_call | solution.py:315
  124.2 3.5 %shard_map.78 = (f32[128,256]{1,0:T(8,128)S(1)}, bf16[128,512]{1,0:T(8,128)(2,1)S(1)}, f32[128,256]{1,0:T(8,128)S(1)}, bf16[128,256]{1,0:T(8,128)(2,1)S(1)}, bf1...) custom-call(s32[4,512]{1,0:T(4,128)S(1)} %get-tuple-element.103.refs_0_.refs_5_, ...), custom_call_target="tpu_custom_call" | custom-call | flops 536870912 | bytes 1572864 | tf_op jit(solution)/shard_map/pallas_call | solution.py:315
  130.1 3.1 %collective-permute-done.34.refs_3_ = bf16[128,256]{1,0:T(8,128)(2,1)S(1)} collective-permute-done((bf16[128,256]{1,0:T(8,128)(2,1)S(1)}, bf16[128,256]{1,0:T(8,128)(2,1)S(1)}, u32[]{:S(2)}, u32[]{:S(2)}) %collective-permute-start.34) | collective-permute-done | bytes 65568 | tf_op jit(solution)/shard_map/ppermute | solution.py:331
  135.9 3.3 %collective-permute-done.36.refs_5_ = bf16[128,256]{1,0:T(8,128)(2,1)S(1)} collective-permute-done((bf16[128,256]{1,0:T(8,128)(2,1)S(1)}, bf16[128,256]{1,0:T(8,128)(2,1)S(1)}, u32[]{:S(2)}, u32[]{:S(2)}) %collective-permute-start.36) | collective-permute-done | bytes 65568 | tf_op jit(solution)/shard_map/ppermute | solution.py:331
  140.4 4.7 %shard_map.79 = (f32[128,256]{1,0:T(8,128)S(1)}, f32[4,128,256]{2,1,0:T(8,128)S(1)}) custom-call(bf16[128,512]{1,0:T(8,128)(2,1)S(1)} %get-tuple-element.43.refs_0_, bf16[128,512]{1,0:T(8,128)(2,1)S(1)} %get-tuple-element.50.refs_1_, bf16[128,512]{1,0:T(8,128)(2,1)S(1)} %get-tuple-element.57.refs_2_, ...), custom_call_target="tpu_custom_call" | custom-call | flops 1610612736 | bytes 1048576 | tf_op jit(solution)/shard_map/pallas_call | solution.py:315
  145.1 3.3 %shard_map.80 = (f32[128,256]{1,0:T(8,128)S(1)}, bf16[128,512]{1,0:T(8,128)(2,1)}, f32[128,256]{1,0:T(8,128)S(1)}, bf16[128,256]{1,0:T(8,128)(2,1)S(1)}, bf16[12...) custom-call(s32[4,512]{1,0:T(4,128)S(1)} %get-tuple-element.102.refs_0_, f32[128,256]{1,0:T(8,128)S(1)} %get-tuple-element.58.refs_1_, ...), custom_call_target="tpu_custom_call" | custom-call | flops 536870912 | bytes 1572864 | tf_op jit(solution)/shard_map/pallas_call | solution.py:315
  150.7 3.5 %collective-permute-done.37.refs_2_ = bf16[128,256]{1,0:T(8,128)(2,1)S(1)} collective-permute-done((bf16[128,256]{1,0:T(8,128)(2,1)S(1)}, bf16[128,256]{1,0:T(8,128)(2,1)S(1)}, u32[]{:S(2)}, u32[]{:S(2)}) %collective-permute-start.37) | collective-permute-done | bytes 65568 | tf_op jit(solution)/shard_map/ppermute | solution.py:331
  156.5 3.7 %collective-permute-done.39.refs_4_ = bf16[128,256]{1,0:T(8,128)(2,1)S(1)} collective-permute-done((bf16[128,256]{1,0:T(8,128)(2,1)S(1)}, bf16[128,256]{1,0:T(8,128)(2,1)S(1)}, u32[]{:S(2)}, u32[]{:S(2)}) %collective-permute-start.39) | collective-permute-done | bytes 65568 | tf_op jit(solution)/shard_map/ppermute | solution.py:331
  167.9 3.2 %collective-permute-done.41.refs_3_.refs_7_.refs_11_ = bf16[128,256]{1,0:T(8,128)(2,1)S(1)} collective-permute-done((bf16[128,256]{1,0:T(8,128)(2,1)S(1)}, bf16[128,256]{1,0:T(8,128)(2,1)S(1)}, u32[]{:S(2)}, u32[]{:S(2)}) %collective-permute-start.41) | collective-permute-done | bytes 65568 | tf_op jit(solution)/shard_map/ppermute | solution.py:331
  171.0 2.7 %shard_map.82.refs_1_.refs_5_.refs_3_ = bf16[128,256]{1,0:T(8,128)(2,1)S(1)} custom-call(s32[4,512]{1,0:T(4,128)S(1)} %get-tuple-element.102.refs_0_, bf16[128,256]{1,0:T(8,128)(2,1)S(1)} %get-tuple-element.68.refs_1_.refs_5_.refs_9_.refs_4_, bf16[128,256]{1,0:T(8,128)(2,1)S(1)} %collective-permute-done.40.refs_2_.refs_6_.refs_10_, ...), custom_call_target="tpu_custom_call" | custom-call | flops 536870912 | bytes 1572864 | tf_op jit(solution)/shard_map/pallas_call | solution.py:315
  175.3 2.9 %collective-permute-done.50.refs_2_.refs_6_ = bf16[128,256]{1,0:T(8,128)(2,1)S(1)} collective-permute-done((bf16[128,256]{1,0:T(8,128)(2,1)S(1)}, bf16[128,256]{1,0:T(8,128)(2,1)S(1)}, u32[]{:S(2)}, u32[]{:S(2)}) %collective-permute-start.50) | collective-permute-done | bytes 65568 | tf_op jit(solution)/shard_map/ppermute | solution.py:331
  179.7 3.7 %collective-permute-done.51.refs_3_.refs_7_ = bf16[128,256]{1,0:T(8,128)(2,1)S(1)} collective-permute-done((bf16[128,256]{1,0:T(8,128)(2,1)S(1)}, bf16[128,256]{1,0:T(8,128)(2,1)S(1)}, u32[]{:S(2)}, u32[]{:S(2)}) %collective-permute-start.51) | collective-permute-done | bytes 65568 | tf_op jit(solution)/shard_map/ppermute | solution.py:331
  185.9 3.5 %collective-permute-done.52.refs_4_.refs_8_ = bf16[128,256]{1,0:T(8,128)(2,1)S(1)} collective-permute-done((bf16[128,256]{1,0:T(8,128)(2,1)S(1)}, bf16[128,256]{1,0:T(8,128)(2,1)S(1)}, u32[]{:S(2)}, u32[]{:S(2)}) %collective-permute-start.52) | collective-permute-done | bytes 65568 | tf_op jit(solution)/shard_map/ppermute | solution.py:331
  189.5 2.7 %shard_map.84.refs_1_.refs_2_ = bf16[128,256]{1,0:T(8,128)(2,1)S(1)} custom-call(s32[4,512]{1,0:T(4,128)S(1)} %get-tuple-element.103.refs_0_.refs_5_, bf16[128,256]{1,0:T(8,128)(2,1)S(1)} %shard_map.82.refs_1_.refs_5_.refs_3_, bf16[128,256]{1,0:T(8,128)(2,1)S(1)} %collective-permute-done.50.refs_2_.refs_6_, ...), custom_call_target="tpu_custom_call" | custom-call | flops 536870912 | bytes 1572864 | tf_op jit(solution)/shard_map/pallas_call | solution.py:315
  200.4 3.2 %shard_map.86.refs_1_ = bf16[128,256]{1,0:T(8,128)(2,1)S(1)} custom-call(s32[4,512]{1,0:T(4,128)S(1)} %get-tuple-element.104.refs_0_.refs_3_.refs_4_, bf16[128,256]{1,0:T(8,128)(2,1)S(1)} %shard_map.84.refs_1_.refs_2_, bf16[128,256]{1,0:T(8,128)(2,1)S(1)} %collective-permute-done.53.refs_2_, bf16[128,256]{1,0:T(8,128)(2,1)S(1)} %collective-permute-done.54.refs_3_, ...), custom_call_target="tpu_custom_call" | custom-call | flops 536870912 | bytes 1572864 | tf_op jit(solution)/shard_map/pallas_call | solution.py:315
  203.7 2.8 %collective-permute-start.64 = (bf16[128,256]{1,0:T(8,128)(2,1)S(1)}, bf16[128,256]{1,0:T(8,128)(2,1)S(1)}, u32[]{:S(2)}, u32[]{:S(2)}) collective-permute-start(bf16[128,256]{1,0:T(8,128)(2,1)S(1)} %shard_map.86.refs_1_), channel_id=1, source_target_pairs={{0,16},{4,20},{8,24},{12,28},{16,0},{20,4},{24,8},{28,12},{1,17},{... | collective-permute-start | bytes 196616 | tf_op jit(solution)/shard_map/ppermute | solution.py:331
  208.0 2.8 %shard_map.87.refs_5_ = bf16[4,32,512]{2,1,0:T(8,128)(2,1)S(1)} custom-call(s32[4,512]{1,0:T(4,128)S(1)} %get-tuple-element.105.refs_0_.refs_1_.refs_2_.refs_3_, bf16[128,256]{1,0:T(8,128)(2,1)S(1)} %shard_map.84.refs_1_.refs_2_, bf16[128,256]{1,0:T(8,128)(2,1)S(1)} %collective-permute-done.53.refs_2_, bf16[128,256]{1,0:T(8,128)(2,1)S(1)} %collective-permute-done.54.refs_3_, ...), custom_call_target="tpu_custom_call" | custom-call | flops 1610612736 | bytes 1048576 | tf_op jit(solution)/shard_map/pallas_call | solution.py:315
  212.6 2.9 %shard_map.88.refs_0_ = bf16[128,256]{1,0:T(8,128)(2,1)S(1)} custom-call(s32[4,512]{1,0:T(4,128)S(1)} %get-tuple-element.105.refs_0_.refs_1_.refs_2_.refs_3_, bf16[128,256]{1,0:T(8,128)(2,1)S(1)} %shard_map.86.refs_1_, bf16[128,256]{1,0:T(8,128)(2,1)S(1)} %collective-permute-done.63.refs_2_, bf16[128,256]{1,0:T(8,128)(2,1)S(1)} %collective-permute-done.64.refs_3_, ...), custom_call_target="tpu_custom_call" | custom-call | flops 536870912 | bytes 1572864 | tf_op jit(solution)/shard_map/pallas_call | solution.py:315
  222.8 4.1 %collective-permute-done.70.refs_5_ = bf16[5,64,128]{2,1,0:T(8,128)(2,1)S(1)} collective-permute-done((bf16[5,64,128]{2,1,0:T(8,128)(2,1)S(1)}, bf16[5,64,128]{2,1,0:T(8,128)(2,1)S(1)}, u32[]{:S(2)}, u32[]{:S(2)}) %collective-permute-start.70) | collective-permute-done | bytes 81952 | tf_op jit(solution)/shard_map/ppermute | solution.py:498
  (221 shorter events, 108.3 us)
Async XLA Ops:
  3.6 10.3 %collective-permute-start.10 = (bf16[4,2,64,256]{3,2,1,0:T(8,128)(2,1)S(1)}, bf16[4,2,64,256]{3,2,1,0:T(8,128)(2,1)}, u32[]{:S(2)}, u32[]{:S(2)}) collective-permute-start(bf16[4,2,64,256]{3,2,1,0:T(8,128)(2,1)S(1)} %pad_maximum_fusion.2.refs_1_), channel_id=1, source_target_pairs={{0,4},{4,0},{8,12},{12,8},{16,20},{20,16},{24,28},{28,24},{1,5},{5... | collective-permute-start | bytes 786440 | tf_op jit(solution)/shard_map/ppermute | solution.py:331
  8.2 12.3 %collective-permute-start.15 = (bf16[4,2,64,256]{3,2,1,0:T(8,128)(2,1)S(1)}, bf16[4,2,64,256]{3,2,1,0:T(8,128)(2,1)S(1)}, u32[]{:S(2)}, u32[]{:S(2)}) collective-permute-start(bf16[4,2,64,256]{3,2,1,0:T(8,128)(2,1)S(1)} %pad_maximum_fusion.3.refs_2_.refs_7_), channel_id=1, source_target_pairs={{0,2},{1,3},{2,0},{3,1},{4,6},{5,7},{6,4},{7,5},{8,10},{9,11},{10,... | collective-permute-start | bytes 786440 | tf_op jit(solution)/shard_map/ppermute | solution.py:334
  8.8 12.1 %collective-permute-start.17 = (bf16[4,2,64,256]{3,2,1,0:T(8,128)(2,1)S(1)}, bf16[4,2,64,256]{3,2,1,0:T(8,128)(2,1)}, u32[]{:S(2)}, u32[]{:S(2)}) collective-permute-start(bf16[4,2,64,256]{3,2,1,0:T(8,128)(2,1)S(1)} %pad_maximum_fusion.3.refs_2_.refs_7_), channel_id=1, source_target_pairs={{0,4},{4,0},{8,12},{12,8},{16,20},{20,16},{24,28},{28,24},{1,5},{5... | collective-permute-start | bytes 786440 | tf_op jit(solution)/shard_map/ppermute | solution.py:331
  20.5 12.2 %collective-permute-start.46 = (bf16[6,2,64,256]{3,2,1,0:T(8,128)(2,1)S(1)}, bf16[6,2,64,256]{3,2,1,0:T(8,128)(2,1)}, u32[]{:S(2)}, u32[]{:S(2)}) collective-permute-start(bf16[6,2,64,256]{3,2,1,0:T(8,128)(2,1)S(1)} %pad_maximum_fusion.refs_6_.refs_7_), channel_id=1, source_target_pairs={{0,4},{4,0},{8,12},{12,8},{16,20},{20,16},{24,28},{28,24},{1,5},{5... | collective-permute-start | bytes 1179656 | tf_op jit(solution)/shard_map/ppermute | solution.py:331
  21.8 12.8 %collective-permute-start.44 = (bf16[6,2,64,256]{3,2,1,0:T(8,128)(2,1)S(1)}, bf16[6,2,64,256]{3,2,1,0:T(8,128)(2,1)}, u32[]{:S(2)}, u32[]{:S(2)}) collective-permute-start(bf16[6,2,64,256]{3,2,1,0:T(8,128)(2,1)S(1)} %pad_maximum_fusion.refs_6_.refs_7_), channel_id=1, source_target_pairs={{0,2},{1,3},{2,0},{3,1},{4,6},{5,7},{6,4},{7,5},{8,10},{9,11},{10,... | collective-permute-start | bytes 1179656 | tf_op jit(solution)/shard_map/ppermute | solution.py:334
  26.1 16.9 %collective-permute-start.57 = (bf16[6,2,64,256]{3,2,1,0:T(8,128)(2,1)S(1)}, bf16[6,2,64,256]{3,2,1,0:T(8,128)(2,1)S(1)}, u32[]{:S(2)}, u32[]{:S(2)}) collective-permute-start(bf16[6,2,64,256]{3,2,1,0:T(8,128)(2,1)S(1)} %pad_maximum_fusion.1.refs_7_), channel_id=1, source_target_pairs={{0,2},{1,3},{2,0},{3,1},{4,6},{5,7},{6,4},{7,5},{8,10},{9,11},{10,... | collective-permute-start | bytes 1179656 | tf_op jit(solution)/shard_map/ppermute | solution.py:334
  28.4 30.6 %collective-permute-start.1 = (bf16[7,2,64,256]{3,2,1,0:T(8,128)(2,1)S(1)}, bf16[7,2,64,256]{3,2,1,0:T(8,128)(2,1)S(1)}, u32[]{:S(2)}, u32[]{:S(2)}) collective-permute-start(bf16[7,2,64,256]{3,2,1,0:T(8,128)(2,1)S(1)} %get-tuple-element.92.refs_0_.refs_6_.refs_7_.refs_5_), channel_id=1, source_target_pairs={{0,2},{1,3},{2,0},{3,1},{4,6},{5,7},{6,4},{7,5},{8,10},{9,11},{10,... | collective-permute-start | bytes 1376264 | tf_op jit(solution)/shard_map/ppermute | solution.py:334
  32.7 26.7 %collective-permute-start.3 = (bf16[7,2,64,256]{3,2,1,0:T(8,128)(2,1)S(1)}, bf16[7,2,64,256]{3,2,1,0:T(8,128)(2,1)S(1)}, u32[]{:S(2)}, u32[]{:S(2)}) collective-permute-start(bf16[7,2,64,256]{3,2,1,0:T(8,128)(2,1)S(1)} %get-tuple-element.92.refs_0_.refs_6_.refs_7_.refs_5_), channel_id=1, source_target_pairs={{0,4},{4,0},{8,12},{12,8},{16,20},{20,16},{24,28},{28,24},{1,5},{5... | collective-permute-start | bytes 1376264 | tf_op jit(solution)/shard_map/ppermute | solution.py:331
  34.6 26.3 %collective-permute-start = (bf16[7,2,64,256]{3,2,1,0:T(8,128)(2,1)S(1)}, bf16[7,2,64,256]{3,2,1,0:T(8,128)(2,1)S(1)}, u32[]{:S(2)}, u32[]{:S(2)}) collective-permute-start(bf16[7,2,64,256]{3,2,1,0:T(8,128)(2,1)S(1)} %get-tuple-element.92.refs_0_.refs_6_.refs_7_.refs_5_), channel_id=1, source_target_pairs={{0,1},{1,0},{2,3},{3,2},{4,5},{5,4},{6,7},{7,6},{8,9},{9,8},{10,11... | collective-permute-start | bytes 1376264 | tf_op jit(solution)/shard_map/ppermute | solution.py:334
  35.4 25.5 %collective-permute-start.12 = (bf16[4,2,64,256]{3,2,1,0:T(8,128)(2,1)}, bf16[4,2,64,256]{3,2,1,0:T(8,128)(2,1)}, u32[]{:S(2)}, u32[]{:S(2)}) collective-permute-start(bf16[4,2,64,256]{3,2,1,0:T(8,128)(2,1)} %collective-permute-done.10.refs_5_), channel_id=1, source_target_pairs={{0,2},{1,3},{2,0},{3,1},{4,6},{5,7},{6,4},{7,5},{8,10},{9,11},{10,... | collective-permute-start | bytes 786440 | tf_op jit(solution)/shard_map/ppermute | solution.py:334
  43.0 18.5 %collective-permute-start.11 = (bf16[4,2,64,256]{3,2,1,0:T(8,128)(2,1)}, bf16[4,2,64,256]{3,2,1,0:T(8,128)(2,1)S(1)}, u32[]{:S(2)}, u32[]{:S(2)}) collective-permute-start(bf16[4,2,64,256]{3,2,1,0:T(8,128)(2,1)} %collective-permute-done.10.refs_5_), channel_id=1, source_target_pairs={{0,1},{1,0},{2,3},{3,2},{4,5},{5,4},{6,7},{7,6},{8,9},{9,8},{10,11... | collective-permute-start | bytes 786440 | tf_op jit(solution)/shard_map/ppermute | solution.py:334
  59.0 20.6 %collective-permute-start.9 = (bf16[4,2,64,256]{3,2,1,0:T(8,128)(2,1)}, bf16[4,2,64,256]{3,2,1,0:T(8,128)(2,1)}, u32[]{:S(2)}, u32[]{:S(2)}) collective-permute-start(bf16[4,2,64,256]{3,2,1,0:T(8,128)(2,1)} %copy-done.12), channel_id=1, source_target_pairs={{0,1},{1,0},{2,3},{3,2},{4,5},{5,4},{6,7},{7,6},{8,9},{9,8},{10,11... | collective-permute-start | bytes 786440 | tf_op jit(solution)/shard_map/ppermute | solution.py:334
  59.4 21.4 %collective-permute-start.19 = (bf16[4,2,64,256]{3,2,1,0:T(8,128)(2,1)S(1)}, bf16[4,2,64,256]{3,2,1,0:T(8,128)(2,1)}, u32[]{:S(2)}, u32[]{:S(2)}) collective-permute-start(bf16[4,2,64,256]{3,2,1,0:T(8,128)(2,1)S(1)} %collective-permute-done.15.refs_4_.refs_9_), channel_id=1, source_target_pairs={{0,4},{4,0},{8,12},{12,8},{16,20},{20,16},{24,28},{28,24},{1,5},{5... | collective-permute-start | bytes 786440 | tf_op jit(solution)/shard_map/ppermute | solution.py:331
  60.9 20.9 %collective-permute-start.16 = (bf16[4,2,64,256]{3,2,1,0:T(8,128)(2,1)S(1)}, bf16[4,2,64,256]{3,2,1,0:T(8,128)(2,1)}, u32[]{:S(2)}, u32[]{:S(2)}) collective-permute-start(bf16[4,2,64,256]{3,2,1,0:T(8,128)(2,1)S(1)} %collective-permute-done.15.refs_4_.refs_9_), channel_id=1, source_target_pairs={{0,1},{1,0},{2,3},{3,2},{4,5},{5,4},{6,7},{7,6},{8,9},{9,8},{10,11... | collective-permute-start | bytes 786440 | tf_op jit(solution)/shard_map/ppermute | solution.py:334
  60.9 21.4 %collective-permute-start.18 = (bf16[4,2,64,256]{3,2,1,0:T(8,128)(2,1)}, bf16[4,2,64,256]{3,2,1,0:T(8,128)(2,1)}, u32[]{:S(2)}, u32[]{:S(2)}) collective-permute-start(bf16[4,2,64,256]{3,2,1,0:T(8,128)(2,1)} %collective-permute-done.17.refs_6_.refs_11_), channel_id=1, source_target_pairs={{0,1},{1,0},{2,3},{3,2},{4,5},{5,4},{6,7},{7,6},{8,9},{9,8},{10,11... | collective-permute-start | bytes 786440 | tf_op jit(solution)/shard_map/ppermute | solution.py:334
  62.2 20.3 %collective-permute-start.29 = (bf16[4,2,64,256]{3,2,1,0:T(8,128)(2,1)}, bf16[4,2,64,256]{3,2,1,0:T(8,128)(2,1)}, u32[]{:S(2)}, u32[]{:S(2)}) collective-permute-start(bf16[4,2,64,256]{3,2,1,0:T(8,128)(2,1)} %collective-permute-done.27.refs_8_.refs_11_), channel_id=1, source_target_pairs={{0,2},{1,3},{2,0},{3,1},{4,6},{5,7},{6,4},{7,5},{8,10},{9,11},{10,... | collective-permute-start | bytes 786440 | tf_op jit(solution)/shard_map/ppermute | solution.py:334
  79.6 23.7 %collective-permute-start.5 = (bf16[7,2,64,256]{3,2,1,0:T(8,128)(2,1)S(1)}, bf16[7,2,64,256]{3,2,1,0:T(8,128)(2,1)S(1)}, u32[]{:S(2)}, u32[]{:S(2)}) collective-permute-start(bf16[7,2,64,256]{3,2,1,0:T(8,128)(2,1)S(1)} %collective-permute-done.1.refs_2_.refs_8_.refs_9_.refs_7_), channel_id=1, source_target_pairs={{0,4},{4,0},{8,12},{12,8},{16,20},{20,16},{24,28},{28,24},{1,5},{5... | collective-permute-start | bytes 1376264 | tf_op jit(solution)/shard_map/ppermute | solution.py:331
  82.4 12.2 %collective-permute-start.20 = (bf16[4,2,64,256]{3,2,1,0:T(8,128)(2,1)}, bf16[4,2,64,256]{3,2,1,0:T(8,128)(2,1)S(1)}, u32[]{:S(2)}, u32[]{:S(2)}) collective-permute-start(bf16[4,2,64,256]{3,2,1,0:T(8,128)(2,1)} %collective-permute-done.19.refs_8_.refs_13_), channel_id=1, source_target_pairs={{0,1},{1,0},{2,3},{3,2},{4,5},{5,4},{6,7},{7,6},{8,9},{9,8},{10,11... | collective-permute-start | bytes 786440 | tf_op jit(solution)/shard_map/ppermute | solution.py:334
  82.9 23.9 %collective-permute-start.30 = (bf16[4,2,64,256]{3,2,1,0:T(8,128)(2,1)}, bf16[4,2,64,256]{3,2,1,0:T(8,128)(2,1)S(1)}, u32[]{:S(2)}, u32[]{:S(2)}) collective-permute-start(bf16[4,2,64,256]{3,2,1,0:T(8,128)(2,1)} %collective-permute-done.29.refs_10_.refs_13_), channel_id=1, source_target_pairs={{0,1},{1,0},{2,3},{3,2},{4,5},{5,4},{6,7},{7,6},{8,9},{9,8},{10,11... | collective-permute-start | bytes 786440 | tf_op jit(solution)/shard_map/ppermute | solution.py:334
  94.9 32.9 %collective-permute-start.2 = (bf16[7,2,64,256]{3,2,1,0:T(8,128)(2,1)S(1)}, bf16[7,2,64,256]{3,2,1,0:T(8,128)(2,1)S(1)}, u32[]{:S(2)}, u32[]{:S(2)}) collective-permute-start(bf16[7,2,64,256]{3,2,1,0:T(8,128)(2,1)S(1)} %collective-permute-done.1.refs_2_.refs_8_.refs_9_.refs_7_), channel_id=1, source_target_pairs={{0,1},{1,0},{2,3},{3,2},{4,5},{5,4},{6,7},{7,6},{8,9},{9,8},{10,11... | collective-permute-start | bytes 1376264 | tf_op jit(solution)/shard_map/ppermute | solution.py:334
  99.8 28.2 %collective-permute-start.4 = (bf16[7,2,64,256]{3,2,1,0:T(8,128)(2,1)S(1)}, bf16[7,2,64,256]{3,2,1,0:T(8,128)(2,1)S(1)}, u32[]{:S(2)}, u32[]{:S(2)}) collective-permute-start(bf16[7,2,64,256]{3,2,1,0:T(8,128)(2,1)S(1)} %collective-permute-done.3.refs_4_.refs_10_.refs_11_.refs_9_), channel_id=1, source_target_pairs={{0,1},{1,0},{2,3},{3,2},{4,5},{5,4},{6,7},{7,6},{8,9},{9,8},{10,11... | collective-permute-start | bytes 1376264 | tf_op jit(solution)/shard_map/ppermute | solution.py:334
  100.8 27.0 %collective-permute-start.48 = (bf16[6,2,64,256]{3,2,1,0:T(8,128)(2,1)}, bf16[6,2,64,256]{3,2,1,0:T(8,128)(2,1)S(1)}, u32[]{:S(2)}, u32[]{:S(2)}) collective-permute-start(bf16[6,2,64,256]{3,2,1,0:T(8,128)(2,1)} %collective-permute-done.46.refs_10_.refs_11_), channel_id=1, source_target_pairs={{0,2},{1,3},{2,0},{3,1},{4,6},{5,7},{6,4},{7,5},{8,10},{9,11},{10,... | collective-permute-start | bytes 1179656 | tf_op jit(solution)/shard_map/ppermute | solution.py:334
  103.3 37.1 %collective-permute-start.6 = (bf16[7,2,64,256]{3,2,1,0:T(8,128)(2,1)S(1)}, bf16[7,2,64,256]{3,2,1,0:T(8,128)(2,1)S(1)}, u32[]{:S(2)}, u32[]{:S(2)}) collective-permute-start(bf16[7,2,64,256]{3,2,1,0:T(8,128)(2,1)S(1)} %collective-permute-done.5.refs_6_.refs_12_.refs_13_.refs_11_), channel_id=1, source_target_pairs={{0,1},{1,0},{2,3},{3,2},{4,5},{5,4},{6,7},{7,6},{8,9},{9,8},{10,11... | collective-permute-start | bytes 1376264 | tf_op jit(solution)/shard_map/ppermute | solution.py:334
  123.3 25.1 %collective-permute-start.59 = (bf16[6,2,64,256]{3,2,1,0:T(8,128)(2,1)S(1)}, bf16[6,2,64,256]{3,2,1,0:T(8,128)(2,1)S(1)}, u32[]{:S(2)}, u32[]{:S(2)}) collective-permute-start(bf16[6,2,64,256]{3,2,1,0:T(8,128)(2,1)S(1)} %pad_maximum_fusion.1.refs_7_), channel_id=1, source_target_pairs={{0,4},{4,0},{8,12},{12,8},{16,20},{20,16},{24,28},{28,24},{1,5},{5... | collective-permute-start | bytes 1179656 | tf_op jit(solution)/shard_map/ppermute | solution.py:331
  127.9 20.7 %collective-permute-start.47 = (bf16[6,2,64,256]{3,2,1,0:T(8,128)(2,1)}, bf16[6,2,64,256]{3,2,1,0:T(8,128)(2,1)S(1)}, u32[]{:S(2)}, u32[]{:S(2)}) collective-permute-start(bf16[6,2,64,256]{3,2,1,0:T(8,128)(2,1)} %collective-permute-done.46.refs_10_.refs_11_), channel_id=1, source_target_pairs={{0,1},{1,0},{2,3},{3,2},{4,5},{5,4},{6,7},{7,6},{8,9},{9,8},{10,11... | collective-permute-start | bytes 1179656 | tf_op jit(solution)/shard_map/ppermute | solution.py:334
  135.9 26.3 %collective-permute-start.45 = (bf16[6,2,64,256]{3,2,1,0:T(8,128)(2,1)}, bf16[6,2,64,256]{3,2,1,0:T(8,128)(2,1)S(1)}, u32[]{:S(2)}, u32[]{:S(2)}) collective-permute-start(bf16[6,2,64,256]{3,2,1,0:T(8,128)(2,1)} %collective-permute-done.44.refs_8_.refs_9_), channel_id=1, source_target_pairs={{0,1},{1,0},{2,3},{3,2},{4,5},{5,4},{6,7},{7,6},{8,9},{9,8},{10,11... | collective-permute-start | bytes 1179656 | tf_op jit(solution)/shard_map/ppermute | solution.py:334
  139.2 23.1 %collective-permute-start.61 = (bf16[6,2,64,256]{3,2,1,0:T(8,128)(2,1)S(1)}, bf16[6,2,64,256]{3,2,1,0:T(8,128)(2,1)S(1)}, u32[]{:S(2)}, u32[]{:S(2)}) collective-permute-start(bf16[6,2,64,256]{3,2,1,0:T(8,128)(2,1)S(1)} %collective-permute-done.57.refs_9_), channel_id=1, source_target_pairs={{0,4},{4,0},{8,12},{12,8},{16,20},{20,16},{24,28},{28,24},{1,5},{5... | collective-permute-start | bytes 1179656 | tf_op jit(solution)/shard_map/ppermute | solution.py:331
  140.4 24.1 %collective-permute-start.49 = (bf16[6,2,64,256]{3,2,1,0:T(8,128)(2,1)S(1)}, bf16[6,2,64,256]{3,2,1,0:T(8,128)(2,1)S(1)}, u32[]{:S(2)}, u32[]{:S(2)}) collective-permute-start(bf16[6,2,64,256]{3,2,1,0:T(8,128)(2,1)S(1)} %collective-permute-done.48.refs_12_.refs_13_), channel_id=1, source_target_pairs={{0,1},{1,0},{2,3},{3,2},{4,5},{5,4},{6,7},{7,6},{8,9},{9,8},{10,11... | collective-permute-start | bytes 1179656 | tf_op jit(solution)/shard_map/ppermute | solution.py:334
  156.5 35.8 %collective-permute-start.56 = (bf16[6,2,64,256]{3,2,1,0:T(8,128)(2,1)S(1)}, bf16[6,2,64,256]{3,2,1,0:T(8,128)(2,1)S(1)}, u32[]{:S(2)}, u32[]{:S(2)}) collective-permute-start(bf16[6,2,64,256]{3,2,1,0:T(8,128)(2,1)S(1)} %pad_maximum_fusion.1.refs_7_), channel_id=1, source_target_pairs={{0,1},{1,0},{2,3},{3,2},{4,5},{5,4},{6,7},{7,6},{8,9},{9,8},{10,11... | collective-permute-start | bytes 1179656 | tf_op jit(solution)/shard_map/ppermute | solution.py:334
  160.2 34.1 %collective-permute-start.58 = (bf16[6,2,64,256]{3,2,1,0:T(8,128)(2,1)S(1)}, bf16[6,2,64,256]{3,2,1,0:T(8,128)(2,1)S(1)}, u32[]{:S(2)}, u32[]{:S(2)}) collective-permute-start(bf16[6,2,64,256]{3,2,1,0:T(8,128)(2,1)S(1)} %collective-permute-done.57.refs_9_), channel_id=1, source_target_pairs={{0,1},{1,0},{2,3},{3,2},{4,5},{5,4},{6,7},{7,6},{8,9},{9,8},{10,11... | collective-permute-start | bytes 1179656 | tf_op jit(solution)/shard_map/ppermute | solution.py:334
  167.9 30.7 %collective-permute-start.60 = (bf16[6,2,64,256]{3,2,1,0:T(8,128)(2,1)S(1)}, bf16[6,2,64,256]{3,2,1,0:T(8,128)(2,1)S(1)}, u32[]{:S(2)}, u32[]{:S(2)}) collective-permute-start(bf16[6,2,64,256]{3,2,1,0:T(8,128)(2,1)S(1)} %collective-permute-done.59.refs_11_), channel_id=1, source_target_pairs={{0,1},{1,0},{2,3},{3,2},{4,5},{5,4},{6,7},{7,6},{8,9},{9,8},{10,11... | collective-permute-start | bytes 1179656 | tf_op jit(solution)/shard_map/ppermute | solution.py:334
  171.0 27.6 %collective-permute-start.62 = (bf16[6,2,64,256]{3,2,1,0:T(8,128)(2,1)S(1)}, bf16[6,2,64,256]{3,2,1,0:T(8,128)(2,1)S(1)}, u32[]{:S(2)}, u32[]{:S(2)}) collective-permute-start(bf16[6,2,64,256]{3,2,1,0:T(8,128)(2,1)S(1)} %collective-permute-done.61.refs_13_), channel_id=1, source_target_pairs={{0,1},{1,0},{2,3},{3,2},{4,5},{5,4},{6,7},{7,6},{8,9},{9,8},{10,11... | collective-permute-start | bytes 1179656 | tf_op jit(solution)/shard_map/ppermute | solution.py:334
  (67 other events, 461.0 us)
where the time goes:
time: 229 us; the launch traced here: 228 us
  waiting for transfers between devices  71.2 us (31%)
  starting transfers between devices  64.4 us (28%)
  Pallas kernels  44.9 us (20%)
  local copies, waits for them, and re-layouts  29 us (13%)
  blocking collectives  16 us (7%)
    ppermute x33, waiting for transfers between devices, over_leaf(): return lax.ppermute(x, 'leaf', [(i, i ^ step) for i in range(plan.leaves)])  55.1 us
    pallas_call x18, Pallas kernels, call(): pl.pallas_call(body, in_specs=specs, out_specs=[VM] * len(outs), out_shap...  44.9 us
    ppermute x33, starting transfers between devices, over_leaf(): return lax.ppermute(x, 'leaf', [(i, i ^ step) for i in range(plan.leaves)])  44.5 us
    ppermute x33, starting transfers between devices, over_grid(): return lax.ppermute(x, 'grid', [(i, i ^ step) for i in range(plan.groups)])  13.5 us
    all_gather x1, blocking collectives, solve(): code = lax.all_gather(code, 'grid', axis=0)  11.7 us
    ppermute x33, waiting for transfers between devices, over_grid(): return lax.ppermute(x, 'grid', [(i, i ^ step) for i in range(plan.groups)])  11.1 us
    unnamed x55, local copies, waits for them, and re-layouts  10.4 us
    ppermute x7, starting transfers between devices, swap(): return lax.ppermute(x, both, moves)  6.32 us
  transfers between devices with their start and end apart: 73, of which 27 were waited for; matrix products, arithmetic and copies ran while one was open for 8% of the time, Pallas kernels for 16%

commit v1 on v0

v1 whole, which is shorter than its diff:
```python
import functools

import jax
import jax.numpy as jnp
from jax import lax
from jax.experimental import pallas as pl
from jax.experimental.pallas import tpu as pltpu
from jax.sharding import PartitionSpec as P

BF = jnp.bfloat16
F32 = jnp.float32
LANES = 128
ROWS_AT_ONCE = 256
VMEM_BYTES = 16 * 1024 * 1024
PACK_VMEM_BYTES = 60 * 1024 * 1024


def nn(a, b):
    return lax.dot_general(a, b, (((1,), (0,)), ((), ())), preferred_element_type=F32)


def nt(a, b):
    return lax.dot_general(a, b, (((1,), (1,)), ((), ())), preferred_element_type=F32)


class Plan:
    def __init__(self, mesh, rhs, upd_t, bwd_t):
        self.levels, self.kept, self.rows, self.columns = rhs.shape
        self.leaves, self.groups = mesh.shape["leaf"], mesh.shape["grid"]
        self.parts = 2 if self.leaves % 2 == 0 else 1
        self.owners = self.leaves // self.parts
        self.supers = self.parts * self.kept
        self.chunk = self.columns // (self.groups * self.parts)
        self.width = self.rows * self.groups
        self.update_rows = upd_t.shape[3]
        self.group_rows = bwd_t.shape[2]
        self.slab = (self.supers * self.chunk, self.width)
        self.chips = [(dp, dg) for dg in range(0, self.groups, 2) for dp in range(self.parts)]
        self.coded = -(-3 * (self.levels - 1) // 16) * 16
        self.sources = self.supers * self.group_rows
        self.blocks = [(dp, dg) for dp in range(self.parts) for dg in range(self.groups)]

    def place(self):
        leaf, grid = lax.axis_index("leaf"), lax.axis_index("grid")
        return leaf // self.parts, leaf % self.parts, grid


def fetch(plan, blocks, pieces, sems):
    _, part, grid = plan.place()
    copies, k = [], plan.kept
    for slab, make in pieces:
        group = []
        for ref, (dp, dg) in zip(blocks, plan.blocks):
            sem = sems.at[len(copies) * len(plan.blocks) + len(group)]
            source = ref.at[pl.ds(slab * k, k)]
            group.append(pltpu.make_async_copy(source, make(part ^ dp, grid ^ dg), sem))
            group[-1].start()
        copies.append(group)
    return copies


def wait(group):
    for copy in group:
        copy.wait()


def matrix(plan, ref, s):
    whole = ref[s // plan.kept, s % plan.kept]
    return whole.reshape(-1, whole.shape[-1])


def joined(plan, stacks, slab, s, count=1):
    own, other = stacks
    first = lax.axis_index("grid") % 2 == 0
    rows = []
    for x in range(plan.groups // 2):
        at = [(x, s // plan.kept, (slab + i) * plan.kept + s % plan.kept) for i in range(count)]
        rows += [jnp.where(first, own[i], other[i]) for i in at]
        rows += [jnp.where(first, other[i], own[i]) for i in at]
    return jnp.concatenate(rows, axis=0)


def start_slab(plan, pieces, at, upper):
    out = []
    for pair in range(plan.groups // 2):
        out.append(
            jnp.concatenate(
                [
                    cross(*[pieces[p, 2 * pair + i, at].astype(F32) for i in range(2)])[upper]
                    for p in range(plan.parts)
                ],
                axis=0,
            )
        )
    return jnp.concatenate(out, axis=1)


def fetch_pieces(plan, blocks, first, count, target, sems, at):
    _, part, grid = plan.place()
    lanes = pl.ds(pl.multiple_of(grid % 2 * LANES, LANES), LANES)
    copies = []
    for ref, (dp, dg) in zip(blocks, plan.blocks):
        for i in range(count):
            copy = pltpu.make_async_copy(
                ref.at[first + i, :, lanes],
                target.at[part ^ dp, grid ^ dg, i],
                sems.at[at + len(copies)],
            )
            copy.start()
            copies.append(copy)
    return copies


def copy_matrices(plan, sources, layout, target, sems, at):
    copies = []
    for i, (source, index) in enumerate(layout):
        to = target.at[pl.ds(i * plan.kept, plan.kept)]
        copies.append(pltpu.make_async_copy(sources[source].at[index], to, sems.at[at + i]))
        copies[-1].start()
    return copies


def pack_kernel(plan, layouts, *refs):
    sources, targets, sems = refs[:4], refs[-1 - len(layouts) : -1], refs[-1]
    copies = []
    for layout, target in zip(layouts, targets):
        copies += copy_matrices(plan, sources, layout, target, sems, len(copies))
    wait(copies)


def first_kernel(plan, layout, second, pairs, *refs):
    refs = list(refs)
    sources = [refs.pop(0) for _ in range(4)]
    rhs_ref, owner_ref, row_ref = [refs.pop(0) for _ in range(3)]
    firsts, second_ref = [refs.pop(0) for _ in plan.chips], refs.pop(0)
    raw_ref, turned_ref, sent_ref, sems = refs
    owner_at, part, grid = plan.place()
    k, r, c = plan.kept, plan.rows, plan.chunk
    fill = pltpu.make_async_copy(rhs_ref, raw_ref, sems.at[0])
    fill.start()
    copies = []
    for target in firsts:
        copies += copy_matrices(plan, sources, layout, target, sems, 1 + len(copies))
    copies += copy_matrices(plan, sources, second, second_ref, sems, 1 + len(copies))
    first = len(layout) * k
    leaf_to, row_to = [
        jnp.concatenate([ref[level, 0] for level in range(plan.levels - 1)], axis=0) for ref in (owner_ref, row_ref)
    ]
    block_to = row_to // r
    super_to = (block_to // k * plan.parts + leaf_to % plan.parts) * k + block_to % k
    fields = [(leaf_to // plan.parts) ^ owner_at, row_to % r, super_to]
    lines = [x[i : i + 1].astype(F32) for i in range(plan.levels - 1) for x in fields]
    lines.append(jnp.zeros((r - len(lines), plan.width), F32))
    shape = (plan.width, plan.width)
    now, then = lax.broadcasted_iota(jnp.int32, shape, 0), lax.broadcasted_iota(jnp.int32, shape, 1)
    move = jnp.where(now == then % plan.group_rows * k + then // plan.group_rows, 1.0, 0.0).astype(BF)
    lines = nn(jnp.concatenate(lines, axis=0).astype(BF), move).astype(BF)
    for i in range(len(plan.chips)):
        sent_ref[i, len(pairs)] = lines
    shape = (plan.columns, plan.columns)
    same = lax.broadcasted_iota(jnp.int32, shape, 0) == lax.broadcasted_iota(jnp.int32, shape, 1)
    same = jnp.where(same, 1.0, 0.0).astype(BF)
    fill.wait()
    for j, pair in enumerate(pairs):
        for s in range(k):
            two = [raw_ref[level, s] for level in pair]
            two += [jnp.zeros((r, plan.columns), BF)] * (2 - len(two))
            turned_ref[s] = nt(same, jnp.concatenate(two, axis=0)).astype(BF)
        for i, (dp, dg) in enumerate(plan.chips):
            for s in range(k):
                for core in range(2):
                    column = ((part ^ dp) * plan.groups + (grid ^ dg) // 2 * 2 + core) * c
                    piece = turned_ref[s, pl.ds(pl.multiple_of(column, c), c), :]
                    sent_ref[i, j, s * c : (s + 1) * c, core * LANES : (core + 1) * LANES] = piece
    extra = len(pairs) + 1
    for i, target in enumerate(firsts):
        copy = pltpu.make_async_copy(sent_ref.at[i], target.at[pl.ds(first, extra)], sems.at[1 + len(copies)])
        copy.start()
        copies.append(copy)
    wait(copies)


def onehot(keys, first, rows):
    iota = lax.broadcasted_iota(jnp.int32, (rows, keys.shape[1]), 0)
    return jnp.where(iota == keys - first, 1.0, 0.0).astype(BF)


def cross(even, odd):
    half = even.shape[1] // 2
    low = lax.broadcasted_iota(jnp.int32, even.shape, 1) < half
    return (
        jnp.where(low, even, pltpu.roll(odd, half, 1)),
        jnp.where(low, pltpu.roll(even, half, 1), odd),
    )


def owners_at_once(plan):
    return min(plan.owners, max(2, ROWS_AT_ONCE // plan.rows))


def scatter(plan, sent, key_ref, level, levels_to, emit):
    c, per = plan.chunk, owners_at_once(plan)
    for pair in range(plan.groups // 2):
        given = []
        for g in (2 * pair, 2 * pair + 1):
            lanes = slice(g * plan.group_rows, (g + 1) * plan.group_rows)
            whole = jnp.concatenate([sent[s * c : (s + 1) * c, lanes] for s in range(plan.supers)], axis=1)
            super_to = key_ref[1, level, g : g + 1, :]
            given.append(
                jnp.concatenate(
                    [
                        whole * jnp.where(super_to == to * plan.supers + s, 1.0, 0.0).astype(BF)
                        for to in levels_to
                        for s in range(plan.supers)
                    ],
                    axis=0,
                )
            )
        for first in range(0, plan.owners, per):
            even, odd = [
                nt(
                    given[i],
                    onehot(
                        key_ref[0, level, 2 * pair + i : 2 * pair + i + 1, :],
                        first * plan.rows,
                        per * plan.rows,
                    ),
                )
                for i in range(2)
            ]
            for j in range(0, per, 2):
                at = slice(j * plan.rows, (j + 2) * plan.rows)
                one, two = cross(even[:, at], odd[:, at])
                for i, to in enumerate(levels_to):
                    rows = slice(i * plan.slab[0], (i + 1) * plan.slab[0])
                    emit(to, first + j, pair, one[rows])
                    emit(to, first + j + 1, pair, two[rows])


def gather(plan, froms, key_ref, level, done):
    c, per = plan.chunk, owners_at_once(plan)
    for pair in range(plan.groups // 2):
        lanes = slice(pair * LANES, (pair + 1) * LANES)
        total = [None, None]
        for first in range(0, plan.owners, per):
            given = [[], []]
            for _, slabs in froms:
                got = [[], []]
                for d in range(first, first + per, 2):
                    halves = cross(slabs[d][:, lanes].astype(F32), slabs[d + 1][:, lanes].astype(F32))
                    for i in range(2):
                        got[i].append(halves[i])
                for i in range(2):
                    given[i].append(jnp.concatenate(got[i], axis=1).astype(BF))
            for i in range(2):
                g = 2 * pair + i
                keys = key_ref[0, level, g : g + 1, :]
                super_to = key_ref[1, level, g : g + 1, :]
                found = nn(
                    jnp.concatenate(given[i], axis=0), onehot(keys, first * plan.rows, per * plan.rows)
                )
                at = 0
                for level_from, _ in froms:
                    for s in range(plan.supers):
                        term = jnp.where(super_to == level_from * plan.supers + s, found[at : at + c], 0.0)
                        total[i] = term if total[i] is None else total[i] + term
                        at += c
        for i in range(2):
            done(2 * pair + i, total[i])


def gate_kernel(*refs):
    pass


def stack_kernel(plan, counts, *refs):
    _, part, grid = plan.place()
    refs = list(refs)
    given = [[(refs.pop(0), first) for first in firsts] for firsts in counts]
    for parts, out in zip(given, refs[len(refs) - len(counts) :]):
        for i, (ref, first) in enumerate(parts):
            if len(out.shape) > 4 and len(ref.shape) > 3:
                out[(grid // 2) ^ i] = ref[...]
            elif len(out.shape) > 4:
                out[(grid // 2) ^ (i // plan.parts), part ^ (i % plan.parts)] = ref[...]
            else:
                out[part ^ i] = ref[first : first + out.shape[1]]


def forward_kernel(plan, level, part_of, added, *refs):
    refs = list(refs)
    last, fresh = level == plan.levels - 1, level == 0
    c, halves = plan.chunk, plan.update_rows // plan.width
    key_ref = None if last or fresh else refs.pop(0)
    if not fresh:
        start_ref, *arrived = [refs.pop(0) for _ in range(1 + plan.owners)]
    more_ref = refs.pop(0) if added else None
    blocks = [refs.pop(0) for _ in (plan.blocks if fresh else range(2))]
    if fresh:
        del refs[: len(plan.chips)]
    out_ref = refs.pop(0)
    if last:
        solved_ref = refs.pop(0)
    else:
        sent_ref = refs.pop(0)
        slab_refs = [refs.pop(0) for _ in range(plan.owners)]
    if fresh:
        key_ref = refs.pop(0)
        next_refs = [refs.pop(0) for _ in range(plan.levels - 1)]
        coded_ref, piece_ref, inv_ref, upd_ref, sems = refs
        _, part, grid = plan.place()
        pairs, size = piece_ref.shape[2], len(plan.blocks)
        first = blocks[0].shape[0] - 1 - pairs
        arriving = fetch_pieces(plan, blocks, first, pairs, piece_ref, sems, size * (2 + halves))
        pieces = [(part_of["fwd"], lambda p, g: inv_ref.at[p, :, g])]
        for half in range(halves):
            pieces.append((part_of["upd"] + half, lambda p, g, half=half: upd_ref.at[half, p, :, g]))
        copies = fetch(plan, blocks, pieces, sems)
        coded = []
        for i, (ref, (dp, dg)) in enumerate(zip(blocks, plan.blocks)):
            coded.append(
                pltpu.make_async_copy(
                    ref.at[ref.shape[0] - 1, pl.ds(0, plan.coded)],
                    coded_ref.at[part ^ dp, grid ^ dg],
                    sems.at[(1 + halves) * size + i],
                )
            )
            coded[-1].start()
        wait(arriving)
        block = start_slab(plan, piece_ref, 0, 0)
        wait(copies[0])
        lower = lambda s: matrix(plan, inv_ref, s)
        update = lambda s, half: matrix(plan, upd_ref.at[half], s)
    else:
        block = start_ref[...] - arrived[0][...]
        for ref in arrived[1:]:
            block = block - ref[...].astype(F32)
        lower = lambda s: joined(plan, blocks, part_of["fwd"], s)
        update = lambda s, half: joined(plan, blocks, part_of["upd"] + half, s)
    block = block.astype(BF)
    solved = jnp.concatenate(
        [nt(block[s * c : (s + 1) * c], lower(s)) for s in range(plan.supers)], axis=0
    )
    out_ref[...] = solved
    lowered = solved.astype(BF)
    if last:
        for s in range(plan.supers):
            at = slice(s * c, (s + 1) * c)
            solved_ref[at, :] = nt(lowered[at], joined(plan, blocks, part_of["inv"], s)).astype(BF)
        return
    if fresh:
        wait(coded)
        for to in range(plan.levels - 1):
            for g in range(plan.groups):
                distance, row, super_to = [
                    jnp.concatenate(
                        [coded_ref[p, g, 3 * to + i : 3 * to + i + 1, :] for p in range(plan.parts)], axis=1
                    ).astype(F32)
                    for i in range(3)
                ]
                key_ref[0, to, g : g + 1, :] = (distance * plan.rows + row).astype(jnp.int32)
                key_ref[1, to, g : g + 1, :] = super_to.astype(jnp.int32)
        for group in copies[1:]:
            wait(group)
    for s in range(plan.supers):
        at = slice(s * c, (s + 1) * c)
        for half in range(halves):
            lanes = slice(half * plan.width, (half + 1) * plan.width)
            sent_ref[at, lanes] = nn(lowered[at], update(s, half)).astype(BF)

    def emit(to, distance, pair, value):
        lanes = slice(pair * LANES, (pair + 1) * LANES)
        if more_ref is not None:
            value = value + more_ref[distance, :, lanes]
        slab_refs[distance][:, lanes] = value.astype(slab_refs[distance].dtype)

    scatter(plan, sent_ref[...], key_ref, level, [level + 1], emit)
    if fresh:
        for i, ref in enumerate(next_refs):
            ref[...] = start_slab(plan, piece_ref, (i + 1) // 2, (i + 1) % 2)


def ahead_kernel(plan, level, *refs):
    sent, key_ref, more_ref = refs[:level], refs[level], refs[level + 1]
    for i, ref in enumerate(sent):

        def emit(to, distance, pair, value, first=i == 0):
            lanes = slice(pair * LANES, (pair + 1) * LANES)
            if not first:
                value = value + more_ref[distance, :, lanes]
            more_ref[distance, :, lanes] = value

        scatter(plan, ref[...], key_ref, i, [level + 1], emit)


def known_kernel(plan, level, froms, *refs):
    key_ref, out_ref = refs[0], refs[-1]
    slabs = [refs[1 + i * plan.owners : 1 + (i + 1) * plan.owners] for i in range(len(froms))]

    def done(g, value):
        out_ref[g] = value.astype(BF)

    gather(plan, list(zip(froms, slabs)), key_ref, level, done)


def backward_kernel(plan, level, part_of, known, *refs):
    refs = list(refs)
    key_ref = refs.pop(0)
    slabs = [refs.pop(0) for _ in range(plan.owners)]
    known_ref = refs.pop(0) if known else None
    forward_ref, *blocks, solved_ref = refs
    c, tall = plan.chunk, plan.group_rows // plan.rows
    pulled = [None] * plan.groups

    def done(g, value):
        if known:
            value = value + known_ref[g].astype(F32)
        pulled[g] = value.astype(BF)

    gather(plan, [(level + 1, slabs)], key_ref, level, done)
    for s in range(plan.supers):
        at = slice(s * c, (s + 1) * c)
        lanes = slice(s * plan.group_rows, (s + 1) * plan.group_rows)
        whole = jnp.concatenate([p[:, lanes] for p in pulled], axis=1)
        upper = nn(whole, joined(plan, blocks, part_of["upper"], s, tall))
        reduced = (forward_ref[at, :] - upper).astype(BF)
        solved_ref[at, :] = nt(reduced, joined(plan, blocks, part_of["inv"], s)).astype(BF)


def pieces_kernel(plan, *refs):
    _, part, grid = plan.place()
    slabs, outs = refs[: plan.levels], refs[plan.levels :]
    rows, half = plan.kept * plan.chunk, plan.rows
    low = lax.broadcasted_iota(jnp.int32, (rows, LANES), 1) < half
    for out, (dp, dg) in zip(outs, plan.blocks):
        first = pl.multiple_of((part ^ dp) * rows, rows)
        lane = pl.multiple_of((grid ^ dg) * half // LANES * LANES, LANES)
        turn = (grid ^ dg) * half % LANES
        for i in range(0, plan.levels, 2):
            two = [slab[pl.ds(first, rows), pl.ds(lane, LANES)].astype(F32) for slab in slabs[i : i + 2]]
            one = pltpu.roll(two[0], turn, 1)
            if len(two) > 1:
                one = jnp.where(low, one, pltpu.roll(two[1], half - turn, 1))
            out[i // 2] = one.astype(BF)


def result_kernel(plan, *refs):
    _, part, grid = plan.place()
    refs = list(refs)
    scratch, out = refs.pop(), refs.pop()
    c = plan.chunk
    shape = (plan.rows, LANES)
    lane = lax.broadcasted_iota(jnp.int32, shape, 1)
    row = lax.broadcasted_iota(jnp.int32, shape, 0)
    picks = [jnp.where(lane == row + i * plan.rows, 1.0, 0.0).astype(BF) for i in range(2)]
    for k in range(plan.kept):
        for ref, (dp, dg) in zip(refs, plan.blocks):
            at = ((part ^ dp) * plan.groups + (grid ^ dg)) * c
            for i in range((plan.levels + 1) // 2):
                scratch[i, k, pl.ds(pl.multiple_of(at, c), c), :] = ref[i, k * c : (k + 1) * c, :]
    for level in range(plan.levels):
        for k in range(plan.kept):
            out[level, k] = nt(picks[level % 2], scratch[level // 2, k]).astype(BF)


VM = pl.BlockSpec(memory_space=pltpu.VMEM)
ANY = pl.BlockSpec(memory_space=pltpu.HBM)
UNREAD = pl.BlockSpec(memory_space=pl.ANY)


def call(body, args, specs, outs, scratch, flops, moved, vmem=VMEM_BYTES):
    return pl.pallas_call(
        body,
        in_specs=specs,
        out_specs=[VM] * len(outs),
        out_shape=[jax.ShapeDtypeStruct(shape, dtype) for shape, dtype in outs],
        scratch_shapes=scratch,
        compiler_params=pltpu.CompilerParams(vmem_limit_bytes=vmem),
        cost_estimate=pl.CostEstimate(flops=flops, bytes_accessed=moved, transcendentals=0),
    )(*args)


def gate(x, *others):
    return pl.pallas_call(
        gate_kernel,
        in_specs=[UNREAD] * (1 + len(others)),
        out_specs=UNREAD,
        out_shape=jax.ShapeDtypeStruct(x.shape, x.dtype),
        input_output_aliases={0: 0},
        compiler_params=pltpu.CompilerParams(vmem_limit_bytes=2**20),
        cost_estimate=pl.CostEstimate(flops=0, bytes_accessed=0, transcendentals=0),
    )(x, *others)


def stack(plan, jobs, *others):
    args = [x for parts, _ in jobs for x, _ in parts]
    return call(
        functools.partial(stack_kernel, plan, [[first for _, first in parts] for parts, _ in jobs]),
        args + list(others), [VM] * len(args) + [UNREAD] * len(others),
        [(shape, BF) for _, shape in jobs], [], 1, 2**19,
    )


def solve(plan, rhs, fwd_inv, bwd_inv, upd_t, bwd_t, dest_owner, dest_row):
    levels, owners = plan.levels, plan.owners
    owner_at, part, grid = plan.place()

    def over_leaf(x, step):
        return lax.ppermute(x, "leaf", [(i, i ^ step) for i in range(plan.leaves)])

    def over_grid(x, step):
        return lax.ppermute(x, "grid", [(i, i ^ step) for i in range(plan.groups)])

    def swap(x, dp, dg):
        if (dp, dg) == (0, 0):
            return x
        g = plan.groups
        moves = [(i, ((i // g) ^ dp) * g + ((i % g) ^ dg)) for i in range(plan.leaves * g)]
        return lax.ppermute(x, ("leaf", "grid"), moves)

    top, every = levels - 1, slice(None)
    halves = plan.update_rows // plan.width
    tall = plan.group_rows // plan.rows

    def parts_of(name, level):
        if name == "upd":
            return [(2, (level, every, every, pl.ds(h * plan.width, plan.width))) for h in range(halves)]
        if name == "upper":
            return [(3, (level, every, pl.ds(h * plan.rows, plan.rows))) for h in range(tall)]
        return [(dict(fwd=0, inv=1)[name], (level,))]

    names = [[("fwd", level), ("upd", level)] for level in range(top)]
    names.append([("fwd", top), ("inv", top)])
    names += [[("upper", level), ("inv", level)] for level in reversed(range(top))]
    where, layouts = {}, []
    for number, chunk in enumerate(names):
        layouts.append([])
        for name, level in chunk:
            where[name, level] = (number, len(layouts[-1]))
            layouts[-1] += parts_of(name, level)
    pairs = [tuple(range(i, min(i + 2, levels))) for i in range(0, levels, 2)]
    slab = (plan.rows, plan.width)
    matrices_given = (fwd_inv, bwd_inv, upd_t, bwd_t)

    ways, extra = len(plan.chips), len(pairs) + 1
    *given, second = call(
        functools.partial(first_kernel, plan, layouts[0], layouts[1], pairs),
        [*matrices_given, rhs, dest_owner.reshape(dest_row.shape), dest_row],
        [ANY] * 5 + [VM] * 2,
        [((len(layouts[0]) * plan.kept + extra,) + slab, BF)] * ways
        + [((len(layouts[1]) * plan.kept,) + slab, BF)],
        [
            pltpu.VMEM(rhs.shape, BF),
            pltpu.VMEM((plan.kept, plan.columns, LANES), BF),
            pltpu.VMEM((ways, extra) + slab, BF),
            pltpu.SemaphoreType.DMA((1 + ways * (len(layouts[0]) + 1) + len(layouts[1]),)),
        ],
        1, 2**20, PACK_VMEM_BYTES,
    )
    sizes = [len(x) * plan.kept for x in layouts]
    later = levels + 1
    grouped = [layouts[2], sum(layouts[3:later], []), sum(layouts[later:], [])]
    owned = call(
        functools.partial(pack_kernel, plan, grouped),
        [*matrices_given, given[0]], [ANY] * 4 + [UNREAD],
        [((len(x) * plan.kept,) + slab, BF) for x in grouped],
        [pltpu.SemaphoreType.DMA((sum(len(x) for x in grouped),))],
        1, 2**20,
    )
    given[-1] = gate(given[-1], owned[0])
    got = {chip: swap(x, *chip) for chip, x in zip(plan.chips, given)}
    chunks = {0: [got[dp, dg] if dg % 2 == 0 else over_grid(got[dp, dg - 1], 1) for dp, dg in plan.blocks]}

    def to_part(x):
        return [x] + [over_leaf(x, dp) for dp in range(1, plan.parts)]

    def to_chip(x):
        return [x] + [over_grid(x, dg) for dg in range(2, plan.groups, 2)]

    chip_there = got[plan.chips[-2]]
    second = to_part(gate(second, chip_there))
    second = second + sum([[over_grid(x, dg) for x in second] for dg in range(2, plan.groups, 2)], [])
    from_part, two = {}, {1: [(x, 0) for x in second]}

    def slices(first, last, x):
        parts, at = to_part(x), 0
        for number in range(first, last):
            from_part[number] = [(part, at) for part in parts]
            at += sizes[number]
        return parts[-1]

    marks = [slices(2, 3, gate(owned[0], chip_there))]
    before_first = second[1:] + marks

    def advance(stage, mark):
        if stage == 0:
            marks.append(slices(3, later, gate(owned[1], mark)))
        if stage == 1:
            slices(later, len(layouts), gate(owned[2], mark, marks[-1]))
        jobs, done = [], []
        if stage + 1 in two:
            shape = (plan.groups // 2, plan.parts, sizes[stage + 1]) + slab
            jobs.append((two[stage + 1], shape))
            done.append(stage + 1)
        if stage + 2 in from_part:
            jobs.append((from_part[stage + 2], (plan.parts, sizes[stage + 2]) + slab))
            done.append(stage + 2)
        for x, number in zip(stack(plan, jobs, mark) if jobs else [], done):
            if number == stage + 1:
                chunks[number] = [x, over_grid(x, 1)]
            else:
                two[number] = [(x, 0) for x in to_chip(x)]

    def matrices(level, wanted):
        (number,) = {where[name, level][0] for name in wanted}
        return chunks[number], {name: where[name, level][1] for name in wanted}

    full = (plan.parts, plan.kept, plan.groups, plan.rows, plan.width)
    slab_bytes = plan.slab[0] * plan.slab[1] * 2
    one_pass = 2 * plan.slab[0] * plan.slab[1] * plan.sources * plan.groups * max(1, owners // 4)

    forward_out, sent, starts, arrived, more = [], [], {}, [], None
    for level in range(levels):
        last, fresh = level == top, level == 0
        blocks, part_of = matrices(level, ["fwd", "inv" if last else "upd"])
        count = len(blocks)
        args, specs = [], []
        if not last and not fresh:
            args.append(keys)
            specs.append(VM)
        if not fresh:
            args += [starts[level]] + arrived
            specs += [VM] * (1 + owners)
        if more is not None and not last:
            args.append(more)
            specs.append(VM)
        args += blocks
        specs += [ANY if fresh else VM] * count
        if fresh:
            args += before_first
            specs += [UNREAD] * len(before_first)
        outs = [(plan.slab, F32)]
        if last:
            outs.append((plan.slab, BF))
        else:
            outs.append(((plan.slab[0], plan.update_rows), BF))
            outs += [(plan.slab, F32)] + [(plan.slab, BF)] * (owners - 1)
        if fresh:
            outs.append(((2, levels - 1, plan.groups, plan.sources), jnp.int32))
            outs += [(plan.slab, F32)] * top
        scratch = []
        if fresh:
            scratch = [
                pltpu.VMEM((plan.parts, plan.groups, plan.coded, plan.width), BF),
                pltpu.VMEM((plan.parts, plan.groups, len(pairs), plan.rows, LANES), BF),
                pltpu.VMEM(full, BF),
                pltpu.VMEM((halves,) + full, BF),
                pltpu.SemaphoreType.DMA((len(plan.blocks) * (2 + halves + len(pairs)),)),
            ]
        got = call(
            functools.partial(
                forward_kernel, plan, level, part_of, more is not None and not last
            ),
            args, specs, outs, scratch, one_pass, 24 * slab_bytes,
        )
        forward_out.append(got[0])
        if last:
            solved = got[1]
            break
        sent.append(got[1])
        if fresh:
            keys = got[-1 - top]
            starts.update(zip(range(1, levels), got[-top:]))
        arrived = [got[2]] + [over_leaf(got[2 + d], d * plan.parts) for d in range(1, owners)]
        advance(level, got[1])
        more = None
        if level + 1 < top:
            (more,) = call(
                functools.partial(ahead_kernel, plan, level + 1),
                sent + [keys], [VM] * (len(sent) + 1), [((owners,) + plan.slab, F32)], [],
                one_pass * len(sent), 16 * slab_bytes,
            )

    solutions = {top: solved}
    everywhere = {}
    for level in reversed(range(top)):
        above = solutions[level + 1]
        everywhere[level + 1] = [above] + [over_leaf(above, d * plan.parts) for d in range(1, owners)]
        froms = list(range(level + 2, levels))
        known = []
        if froms:
            slabs = sum([everywhere[f] for f in froms], [])
            known = call(
                functools.partial(known_kernel, plan, level, froms),
                [keys] + slabs, [VM] * (1 + len(slabs)),
                [((plan.groups, plan.chunk, plan.sources), BF)], [],
                one_pass * len(froms), 16 * slab_bytes,
            )
        advance(levels + top - level - 2, above)
        blocks, part_of = matrices(level, ["upper", "inv"])
        args = [keys] + everywhere[level + 1] + list(known) + [forward_out[level]]
        (solutions[level],) = call(
            functools.partial(backward_kernel, plan, level, part_of, bool(froms)),
            args + blocks, [VM] * (len(args) + len(blocks)), [(plan.slab, BF)], [],
            one_pass, 24 * slab_bytes,
        )

    piece = ((levels + 1) // 2, plan.kept * plan.chunk, LANES)
    own = call(
        functools.partial(pieces_kernel, plan),
        [solutions[level] for level in range(levels)], [VM] * levels,
        [(piece, BF)] * len(plan.blocks), [], 1, 8 * slab_bytes,
    )
    theirs = [swap(x, dp, dg) for x, (dp, dg) in zip(own, plan.blocks)]
    (result,) = call(
        functools.partial(result_kernel, plan),
        theirs, [VM] * len(theirs), [(rhs.shape, BF)],
        [pltpu.VMEM(((levels + 1) // 2, plan.kept, plan.columns, LANES), BF)], 1, 8 * slab_bytes,
    )
    return result


def solution(mesh):
    def local(rhs, fwd_inv, bwd_inv, upd_t, bwd_t, dest_owner, dest_row):
        plan = Plan(mesh, rhs, upd_t, bwd_t)
        return solve(plan, rhs, fwd_inv, bwd_inv, upd_t, bwd_t, dest_owner, dest_row)

    rows = P(None, "leaf", "grid", None)
    placed = (rows, rows, rows, rows, rows, P(None, "leaf", "grid", None, None), rows)
    return jax.shard_map(local, mesh=mesh, in_specs=placed, out_specs=rows, check_vma=False)
```

time: 229 us -> 148 us (0.65)
  local copies, waits for them, and re-layouts: 29 us -> 0.99 us
  Pallas kernels: 44.9 us -> 23.3 us
  blocking collectives: 16 us -> 0 us
  waiting for transfers between devices: 71.2 us -> 58 us
    pallas_call x18 -> x27, Pallas kernels: 44.9 us -> 23.3 us  [call(): pl.pallas_call(body, in_specs=specs, out_specs=[VM] * len(outs), out_shap...]
    all_gather x2 -> x0, blocking collectives: 16 us -> none  [the longest x1 11.7 us: solve(): code = lax.all_gather(code, 'grid', axis=0)]
    ppermute x33 -> x28, waiting for transfers between devices: 55.1 us -> 42.2 us  [over_leaf(): return lax.ppermute(x, 'leaf', [(i, i ^ step) for i in range(plan.leaves)])]
    unnamed x55 -> x14, local copies, waits for them, and re-layouts: 10.4 us -> 0.99 us
    ppermute x33 -> x21, waiting for transfers between devices: 11.1 us -> 2.5 us  [over_grid(): return lax.ppermute(x, 'grid', [(i, i ^ step) for i in range(plan.groups)])]
    ppermute x7 -> x10, waiting for transfers between devices: 5 us -> 13.3 us  [swap(): return lax.ppermute(x, ('leaf', 'grid'), moves)]
    div x3 -> x0, local copies, waits for them, and re-layouts: 5.55 us -> none  [solve(): leaf_to, row_to = (code // per_owner, code % per_owner)]
    rem x3 -> x0, local copies, waits for them, and re-layouts: 5.55 us -> none  [solve(): leaf_to, row_to = (code // per_owner, code % per_owner)]
  transfers between devices with their start and end apart: 73 -> 59, of which waited for: 27 -> 25; matrix products, arithmetic and copies ran while one was open for 8% -> 0% of each run, Pallas kernels for 16% -> 9%
where the time goes in v1:
time: 148 us
  starting transfers between devices  65.1 us (44%)
  waiting for transfers between devices  58 us (39%)
  Pallas kernels  23.3 us (16%)
    ppermute x28, starting transfers between devices, over_leaf(): return lax.ppermute(x, 'leaf', [(i, i ^ step) for i in range(plan.leaves)])  44.3 us
    ppermute x28, waiting for transfers between devices, over_leaf(): return lax.ppermute(x, 'leaf', [(i, i ^ step) for i in range(plan.leaves)])  42.2 us
    pallas_call x27, Pallas kernels, call(): pl.pallas_call(body, in_specs=specs, out_specs=[VM] * len(outs), out_shap...  23.3 us
    ppermute x10, waiting for transfers between devices, swap(): return lax.ppermute(x, ('leaf', 'grid'), moves)  13.3 us
    ppermute x10, starting transfers between devices, swap(): return lax.ppermute(x, ('leaf', 'grid'), moves)  11 us
    ppermute x21, starting transfers between devices, over_grid(): return lax.ppermute(x, 'grid', [(i, i ^ step) for i in range(plan.groups)])  9.83 us
  transfers between devices with their start and end apart: 59, of which 25 were waited for; matrix products, arithmetic and copies ran while one was open for 0% of the time, Pallas kernels for 9%

profile of v1, /device:TPU:0, one launch (start us, length us, event | category | flops | bytes accessed | tf_op | source)
XLA Modules:
  0.0 147.8 jit_solution(2208245320286214009)
XLA Ops:
  0.0 4.2 %shard_map.73 = (bf16[10,64,256]{2,1,0:T(8,128)(2,1)}, bf16[10,64,256]{2,1,0:T(8,128)(2,1)}, bf16[10,64,256]{2,1,0:T(8,128)(2,1)}, bf16[10,64,256]{2,1,0:T(8,128)(2,1)}, bf16[6,64,256]{2,1,0:T(8,128)(2,1)}) custom-call(bf16[5,2,64,256]{3,2,1,0:T(8,128)(2,1)} %refs_0_.3, bf16[5,2,64,256]{3,2,1,0:T(8,128)(2,1)} %refs_1_.3, bf16[4,2,64,512]{3,2,1,0:T(8,128)(2,1)} %refs_2_.3, ...), custom_call_target="tpu_custom_call" | custom-call | flops 1 | bytes 1048576 | tf_op jit(solution)/shard_map/pallas_call | solution.py:472
  4.2 3.0 %collective-permute-start.1 = (bf16[10,64,256]{2,1,0:T(8,128)(2,1)}, bf16[10,64,256]{2,1,0:T(8,128)(2,1)S(1)}, u32[]{:S(2)}, u32[]{:S(2)}) collective-permute-start(bf16[10,64,256]{2,1,0:T(8,128)(2,1)} %get-tuple-element.66), channel_id=1, source_target_pairs={{0,2},{1,3},{2,0},{3,1},{4,6},{5,7},{6,4},{7,5},{8,10},{9,11},{10,... | collective-permute-start | bytes 983048 | tf_op jit(solution)/shard_map/ppermute | solution.py:519
  11.2 4.8 %collective-permute-done.1.refs_1_.refs_2_ = bf16[10,64,256]{2,1,0:T(8,128)(2,1)S(1)} collective-permute-done((bf16[10,64,256]{2,1,0:T(8,128)(2,1)}, bf16[10,64,256]{2,1,0:T(8,128)(2,1)S(1)}, u32[]{:S(2)}, u32[]{:S(2)}) %collective-permute-start.1) | collective-permute-done | bytes 327712 | tf_op jit(solution)/shard_map/ppermute | solution.py:519
  16.0 2.1 %collective-permute-start.7 = (bf16[6,64,256]{2,1,0:T(8,128)(2,1)S(1)}, bf16[6,64,256]{2,1,0:T(8,128)(2,1)S(1)}, u32[]{:S(2)}, u32[]{:S(2)}) collective-permute-start(bf16[6,64,256]{2,1,0:T(8,128)(2,1)S(1)} %shard_map.76.refs_0_), channel_id=1, source_target_pairs={{0,4},{4,0},{8,12},{12,8},{16,20},{20,16},{24,28},{28,24},{1,5},{5... | collective-permute-start | bytes 589832 | tf_op jit(solution)/shard_map/ppermute | solution.py:509
  19.6 5.4 %collective-permute-done.3.refs_4_ = bf16[10,64,256]{2,1,0:T(8,128)(2,1)S(1)} collective-permute-done((bf16[10,64,256]{2,1,0:T(8,128)(2,1)}, bf16[10,64,256]{2,1,0:T(8,128)(2,1)S(1)}, u32[]{:S(2)}, u32[]{:S(2)}) %collective-permute-start.3) | collective-permute-done | bytes 327712 | tf_op jit(solution)/shard_map/ppermute | solution.py:519
  25.5 3.3 %collective-permute-done.7.refs_8_.refs_1_ = bf16[6,64,256]{2,1,0:T(8,128)(2,1)S(1)} collective-permute-done((bf16[6,64,256]{2,1,0:T(8,128)(2,1)S(1)}, bf16[6,64,256]{2,1,0:T(8,128)(2,1)S(1)}, u32[]{:S(2)}, u32[]{:S(2)}) %collective-permute-start.7) | collective-permute-done | bytes 196640 | tf_op jit(solution)/shard_map/ppermute | solution.py:509
  30.9 4.5 %collective-permute-done.10.refs_11_.refs_5_ = bf16[6,64,256]{2,1,0:T(8,128)(2,1)S(1)} collective-permute-done((bf16[6,64,256]{2,1,0:T(8,128)(2,1)S(1)}, bf16[6,64,256]{2,1,0:T(8,128)(2,1)S(1)}, u32[]{:S(2)}, u32[]{:S(2)}) %collective-permute-start.10) | collective-permute-done | bytes 196640 | tf_op jit(solution)/shard_map/ppermute | solution.py:509
  36.6 3.3 %shard_map.78 = (f32[128,256]{1,0:T(8,128)S(1)}, bf16[128,512]{1,0:T(8,128)(2,1)S(1)}, f32[128,256]{1,0:T(8,128)S(1)}, bf16[128,256]{1,0:T(8,128)(2,1)S(1)}, bf1...) custom-call(bf16[10,64,256]{2,1,0:T(8,128)(2,1)S(1)} %copy-done.4, ...), custom_call_target="tpu_custom_call" | custom-call | flops 134217728 | bytes 1572864 | tf_op jit(solution)/shard_map/pallas_call | solution.py:472
  41.1 1.7 %collective-permute-start.11 = (bf16[128,256]{1,0:T(8,128)(2,1)S(1)}, bf16[128,256]{1,0:T(8,128)(2,1)S(1)}, u32[]{:S(2)}, u32[]{:S(2)}) collective-permute-start(bf16[128,256]{1,0:T(8,128)(2,1)S(1)} %get-tuple-element.77), channel_id=1, source_target_pairs={{0,8},{4,12},{8,0},{12,4},{16,24},{20,28},{24,16},{28,20},{1,9},{5... | collective-permute-start | bytes 196616 | tf_op jit(solution)/shard_map/ppermute | solution.py:509
  42.8 2.6 %collective-permute-start.12 = (bf16[128,256]{1,0:T(8,128)(2,1)S(1)}, bf16[128,256]{1,0:T(8,128)(2,1)S(1)}, u32[]{:S(2)}, u32[]{:S(2)}) collective-permute-start(bf16[128,256]{1,0:T(8,128)(2,1)S(1)} %get-tuple-element.78), channel_id=1, source_target_pairs={{0,16},{4,20},{8,24},{12,28},{16,0},{20,4},{24,8},{28,12},{1,17},{... | collective-permute-start | bytes 196616 | tf_op jit(solution)/shard_map/ppermute | solution.py:509
  45.4 4.4 %collective-permute-start.13 = (bf16[128,256]{1,0:T(8,128)(2,1)S(1)}, bf16[128,256]{1,0:T(8,128)(2,1)S(1)}, u32[]{:S(2)}, u32[]{:S(2)}) collective-permute-start(bf16[128,256]{1,0:T(8,128)(2,1)S(1)} %get-tuple-element.79), channel_id=1, source_target_pairs={{0,24},{4,28},{8,16},{12,20},{16,8},{20,12},{24,0},{28,4},{1,25},{... | collective-permute-start | bytes 196616 | tf_op jit(solution)/shard_map/ppermute | solution.py:509
  50.3 1.6 %collective-permute-done.13.refs_5_ = bf16[128,256]{1,0:T(8,128)(2,1)S(1)} collective-permute-done((bf16[128,256]{1,0:T(8,128)(2,1)S(1)}, bf16[128,256]{1,0:T(8,128)(2,1)S(1)}, u32[]{:S(2)}, u32[]{:S(2)}) %collective-permute-start.13) | collective-permute-done | bytes 65568 | tf_op jit(solution)/shard_map/ppermute | solution.py:509
  56.8 2.6 %collective-permute-start.16 = (bf16[128,256]{1,0:T(8,128)(2,1)S(1)}, bf16[128,256]{1,0:T(8,128)(2,1)S(1)}, u32[]{:S(2)}, u32[]{:S(2)}) collective-permute-start(bf16[128,256]{1,0:T(8,128)(2,1)S(1)} %get-tuple-element.84), channel_id=1, source_target_pairs={{0,16},{4,20},{8,24},{12,28},{16,0},{20,4},{24,8},{28,12},{1,17},{... | collective-permute-start | bytes 196616 | tf_op jit(solution)/shard_map/ppermute | solution.py:509
  60.5 3.8 %collective-permute-done.16.refs_4_ = bf16[128,256]{1,0:T(8,128)(2,1)S(1)} collective-permute-done((bf16[128,256]{1,0:T(8,128)(2,1)S(1)}, bf16[128,256]{1,0:T(8,128)(2,1)S(1)}, u32[]{:S(2)}, u32[]{:S(2)}) %collective-permute-start.16) | collective-permute-done | bytes 65568 | tf_op jit(solution)/shard_map/ppermute | solution.py:509
  69.1 2.0 %collective-permute-start.22 = (bf16[128,256]{1,0:T(8,128)(2,1)S(1)}, bf16[128,256]{1,0:T(8,128)(2,1)S(1)}, u32[]{:S(2)}, u32[]{:S(2)}) collective-permute-start(bf16[128,256]{1,0:T(8,128)(2,1)S(1)} %get-tuple-element.92), channel_id=1, source_target_pairs={{0,16},{4,20},{8,24},{12,28},{16,0},{20,4},{24,8},{28,12},{1,17},{... | collective-permute-start | bytes 196616 | tf_op jit(solution)/shard_map/ppermute | solution.py:509
  74.4 3.0 %collective-permute-done.22.refs_4_ = bf16[128,256]{1,0:T(8,128)(2,1)S(1)} collective-permute-done((bf16[128,256]{1,0:T(8,128)(2,1)S(1)}, bf16[128,256]{1,0:T(8,128)(2,1)S(1)}, u32[]{:S(2)}, u32[]{:S(2)}) %collective-permute-start.22) | collective-permute-done | bytes 65568 | tf_op jit(solution)/shard_map/ppermute | solution.py:509
  80.8 1.7 %collective-permute-start.27 = (bf16[128,256]{1,0:T(8,128)(2,1)S(1)}, bf16[128,256]{1,0:T(8,128)(2,1)S(1)}, u32[]{:S(2)}, u32[]{:S(2)}) collective-permute-start(bf16[128,256]{1,0:T(8,128)(2,1)S(1)} %get-tuple-element.99), channel_id=1, source_target_pairs={{0,16},{4,20},{8,24},{12,28},{16,0},{20,4},{24,8},{28,12},{1,17},{... | collective-permute-start | bytes 196616 | tf_op jit(solution)/shard_map/ppermute | solution.py:509
  82.5 1.7 %collective-permute-done.26.refs_2_ = bf16[128,256]{1,0:T(8,128)(2,1)S(1)} collective-permute-done((bf16[128,256]{1,0:T(8,128)(2,1)S(1)}, bf16[128,256]{1,0:T(8,128)(2,1)S(1)}, u32[]{:S(2)}, u32[]{:S(2)}) %collective-permute-start.26) | collective-permute-done | bytes 65568 | tf_op jit(solution)/shard_map/ppermute | solution.py:509
  84.2 2.0 %collective-permute-start.28 = (bf16[128,256]{1,0:T(8,128)(2,1)S(1)}, bf16[128,256]{1,0:T(8,128)(2,1)S(1)}, u32[]{:S(2)}, u32[]{:S(2)}) collective-permute-start(bf16[128,256]{1,0:T(8,128)(2,1)S(1)} %get-tuple-element.100), channel_id=1, source_target_pairs={{0,24},{4,28},{8,16},{12,20},{16,8},{20,12},{24,0},{28,4},{1,25},{... | collective-permute-start | bytes 196616 | tf_op jit(solution)/shard_map/ppermute | solution.py:509
  87.3 3.0 %collective-permute-done.28.refs_4_ = bf16[128,256]{1,0:T(8,128)(2,1)S(1)} collective-permute-done((bf16[128,256]{1,0:T(8,128)(2,1)S(1)}, bf16[128,256]{1,0:T(8,128)(2,1)S(1)}, u32[]{:S(2)}, u32[]{:S(2)}) %collective-permute-start.28) | collective-permute-done | bytes 65568 | tf_op jit(solution)/shard_map/ppermute | solution.py:509
  92.9 2.2 %collective-permute-start.32 = (bf16[128,256]{1,0:T(8,128)(2,1)S(1)}, bf16[128,256]{1,0:T(8,128)(2,1)S(1)}, u32[]{:S(2)}, u32[]{:S(2)}) collective-permute-start(bf16[128,256]{1,0:T(8,128)(2,1)S(1)} %get-tuple-element.104.refs_4_.refs_1_.refs_5_.refs_9_), channel_id=1, source_target_pairs={{0,16},{4,20},{8,24},{12,28},{16,0},{20,4},{24,8},{28,12},{1,17},{... | collective-permute-start | bytes 196616 | tf_op jit(solution)/shard_map/ppermute | solution.py:509
  95.1 1.6 %collective-permute-start.33 = (bf16[128,256]{1,0:T(8,128)(2,1)S(1)}, bf16[128,256]{1,0:T(8,128)(2,1)S(1)}, u32[]{:S(2)}, u32[]{:S(2)}) collective-permute-start(bf16[128,256]{1,0:T(8,128)(2,1)S(1)} %get-tuple-element.104.refs_4_.refs_1_.refs_5_.refs_9_), channel_id=1, source_target_pairs={{0,24},{4,28},{8,16},{12,20},{16,8},{20,12},{24,0},{28,4},{1,25},{... | collective-permute-start | bytes 196616 | tf_op jit(solution)/shard_map/ppermute | solution.py:509
  97.3 4.1 %collective-permute-done.32.refs_3_.refs_7_.refs_11_ = bf16[128,256]{1,0:T(8,128)(2,1)S(1)} collective-permute-done((bf16[128,256]{1,0:T(8,128)(2,1)S(1)}, bf16[128,256]{1,0:T(8,128)(2,1)S(1)}, u32[]{:S(2)}, u32[]{:S(2)}) %collective-permute-start.32) | collective-permute-done | bytes 65568 | tf_op jit(solution)/shard_map/ppermute | solution.py:509
  104.8 2.0 %collective-permute-start.38 = (bf16[128,256]{1,0:T(8,128)(2,1)S(1)}, bf16[128,256]{1,0:T(8,128)(2,1)S(1)}, u32[]{:S(2)}, u32[]{:S(2)}) collective-permute-start(bf16[128,256]{1,0:T(8,128)(2,1)S(1)} %shard_map.93.refs_4_.refs_1_.refs_5_.refs_3_), channel_id=1, source_target_pairs={{0,16},{4,20},{8,24},{12,28},{16,0},{20,4},{24,8},{28,12},{1,17},{... | collective-permute-start | bytes 196616 | tf_op jit(solution)/shard_map/ppermute | solution.py:509
  106.8 1.6 %collective-permute-start.39 = (bf16[128,256]{1,0:T(8,128)(2,1)S(1)}, bf16[128,256]{1,0:T(8,128)(2,1)S(1)}, u32[]{:S(2)}, u32[]{:S(2)}) collective-permute-start(bf16[128,256]{1,0:T(8,128)(2,1)S(1)} %shard_map.93.refs_4_.refs_1_.refs_5_.refs_3_), channel_id=1, source_target_pairs={{0,24},{4,28},{8,16},{12,20},{16,8},{20,12},{24,0},{28,4},{1,25},{... | collective-permute-start | bytes 196616 | tf_op jit(solution)/shard_map/ppermute | solution.py:509
  108.9 4.4 %collective-permute-done.38.refs_3_.refs_7_ = bf16[128,256]{1,0:T(8,128)(2,1)S(1)} collective-permute-done((bf16[128,256]{1,0:T(8,128)(2,1)S(1)}, bf16[128,256]{1,0:T(8,128)(2,1)S(1)}, u32[]{:S(2)}, u32[]{:S(2)}) %collective-permute-start.38) | collective-permute-done | bytes 65568 | tf_op jit(solution)/shard_map/ppermute | solution.py:509
  116.8 1.7 %collective-permute-start.43 = (bf16[128,256]{1,0:T(8,128)(2,1)S(1)}, bf16[128,256]{1,0:T(8,128)(2,1)S(1)}, u32[]{:S(2)}, u32[]{:S(2)}) collective-permute-start(bf16[128,256]{1,0:T(8,128)(2,1)S(1)} %shard_map.96.refs_4_.refs_1_.refs_2_), channel_id=1, source_target_pairs={{0,16},{4,20},{8,24},{12,28},{16,0},{20,4},{24,8},{28,12},{1,17},{... | collective-permute-start | bytes 196616 | tf_op jit(solution)/shard_map/ppermute | solution.py:509
  118.5 1.6 %collective-permute-start.44 = (bf16[128,256]{1,0:T(8,128)(2,1)S(1)}, bf16[128,256]{1,0:T(8,128)(2,1)S(1)}, u32[]{:S(2)}, u32[]{:S(2)}) collective-permute-start(bf16[128,256]{1,0:T(8,128)(2,1)S(1)} %shard_map.96.refs_4_.refs_1_.refs_2_), channel_id=1, source_target_pairs={{0,24},{4,28},{8,16},{12,20},{16,8},{20,12},{24,0},{28,4},{1,25},{... | collective-permute-start | bytes 196616 | tf_op jit(solution)/shard_map/ppermute | solution.py:509
  120.9 4.2 %collective-permute-done.43.refs_3_ = bf16[128,256]{1,0:T(8,128)(2,1)S(1)} collective-permute-done((bf16[128,256]{1,0:T(8,128)(2,1)S(1)}, bf16[128,256]{1,0:T(8,128)(2,1)S(1)}, u32[]{:S(2)}, u32[]{:S(2)}) %collective-permute-start.43) | collective-permute-done | bytes 65568 | tf_op jit(solution)/shard_map/ppermute | solution.py:509
  129.2 1.7 %collective-permute-start.49 = (bf16[128,256]{1,0:T(8,128)(2,1)S(1)}, bf16[128,256]{1,0:T(8,128)(2,1)S(1)}, u32[]{:S(2)}, u32[]{:S(2)}) collective-permute-start(bf16[128,256]{1,0:T(8,128)(2,1)S(1)} %shard_map.99.refs_2_.refs_1_), channel_id=1, source_target_pairs={{0,24},{4,28},{8,16},{12,20},{16,8},{20,12},{24,0},{28,4},{1,25},{... | collective-permute-start | bytes 196616 | tf_op jit(solution)/shard_map/ppermute | solution.py:509
  131.8 4.3 %collective-permute-done.48.refs_3_ = bf16[128,256]{1,0:T(8,128)(2,1)S(1)} collective-permute-done((bf16[128,256]{1,0:T(8,128)(2,1)S(1)}, bf16[128,256]{1,0:T(8,128)(2,1)S(1)}, u32[]{:S(2)}, u32[]{:S(2)}) %collective-permute-start.48) | collective-permute-done | bytes 65568 | tf_op jit(solution)/shard_map/ppermute | solution.py:509
  143.8 2.0 %collective-permute-done.57.refs_6_ = bf16[3,64,128]{2,1,0:T(8,128)(2,1)S(1)} collective-permute-done((bf16[3,64,128]{2,1,0:T(8,128)(2,1)S(1)}, bf16[3,64,128]{2,1,0:T(8,128)(2,1)S(1)}, u32[]{:S(2)}, u32[]{:S(2)}) %collective-permute-start.57) | collective-permute-done | bytes 49184 | tf_op jit(solution)/shard_map/ppermute | solution.py:519
  (132 shorter events, 55.4 us)
Async XLA Ops:
  4.2 11.8 %collective-permute-start.1 = (bf16[10,64,256]{2,1,0:T(8,128)(2,1)}, bf16[10,64,256]{2,1,0:T(8,128)(2,1)S(1)}, u32[]{:S(2)}, u32[]{:S(2)}) collective-permute-start(bf16[10,64,256]{2,1,0:T(8,128)(2,1)} %get-tuple-element.66), channel_id=1, source_target_pairs={{0,2},{1,3},{2,0},{3,1},{4,6},{5,7},{6,4},{7,5},{8,10},{9,11},{10,... | collective-permute-start | bytes 983048 | tf_op jit(solution)/shard_map/ppermute | solution.py:519
  7.2 12.3 %collective-permute-start = (bf16[10,64,256]{2,1,0:T(8,128)(2,1)}, bf16[10,64,256]{2,1,0:T(8,128)(2,1)S(1)}, u32[]{:S(2)}, u32[]{:S(2)}) collective-permute-start(bf16[10,64,256]{2,1,0:T(8,128)(2,1)} %get-tuple-element.65.refs_4_.refs_0_), channel_id=1, source_target_pairs={{0,1},{1,0},{2,3},{3,2},{4,5},{5,4},{6,7},{7,6},{8,9},{9,8},{10,11... | collective-permute-start | bytes 983048 | tf_op jit(solution)/shard_map/ppermute | solution.py:512
  7.2 17.7 %collective-permute-start.3 = (bf16[10,64,256]{2,1,0:T(8,128)(2,1)}, bf16[10,64,256]{2,1,0:T(8,128)(2,1)S(1)}, u32[]{:S(2)}, u32[]{:S(2)}) collective-permute-start(bf16[10,64,256]{2,1,0:T(8,128)(2,1)} %get-tuple-element.67), channel_id=1, source_target_pairs={{0,4},{1,5},{2,6},{3,7},{4,0},{5,1},{6,2},{7,3},{8,12},{9,13},{10,... | collective-permute-start | bytes 983048 | tf_op jit(solution)/shard_map/ppermute | solution.py:519
  11.0 14.0 %collective-permute-start.5 = (bf16[10,64,256]{2,1,0:T(8,128)(2,1)S(1)}, bf16[10,64,256]{2,1,0:T(8,128)(2,1)S(1)}, u32[]{:S(2)}, u32[]{:S(2)}) collective-permute-start(bf16[10,64,256]{2,1,0:T(8,128)(2,1)S(1)} %shard_map.75), channel_id=1, source_target_pairs={{0,6},{1,7},{2,4},{3,5},{4,2},{5,3},{6,0},{7,1},{8,14},{9,15},{10,... | collective-permute-start | bytes 983048 | tf_op jit(solution)/shard_map/ppermute | solution.py:519
  16.0 12.8 %collective-permute-start.7 = (bf16[6,64,256]{2,1,0:T(8,128)(2,1)S(1)}, bf16[6,64,256]{2,1,0:T(8,128)(2,1)S(1)}, u32[]{:S(2)}, u32[]{:S(2)}) collective-permute-start(bf16[6,64,256]{2,1,0:T(8,128)(2,1)S(1)} %shard_map.76.refs_0_), channel_id=1, source_target_pairs={{0,4},{4,0},{8,12},{12,8},{16,20},{20,16},{24,28},{28,24},{1,5},{5... | collective-permute-start | bytes 589832 | tf_op jit(solution)/shard_map/ppermute | solution.py:509
  18.1 12.3 %collective-permute-start.8 = (bf16[6,64,256]{2,1,0:T(8,128)(2,1)S(1)}, bf16[6,64,256]{2,1,0:T(8,128)(2,1)S(1)}, u32[]{:S(2)}, u32[]{:S(2)}) collective-permute-start(bf16[6,64,256]{2,1,0:T(8,128)(2,1)S(1)} %shard_map.76.refs_0_), channel_id=1, source_target_pairs={{0,2},{1,3},{2,0},{3,1},{4,6},{5,7},{6,4},{7,5},{8,10},{9,11},{10,... | collective-permute-start | bytes 589832 | tf_op jit(solution)/shard_map/ppermute | solution.py:512
  19.6 15.8 %collective-permute-start.2 = (bf16[10,64,256]{2,1,0:T(8,128)(2,1)S(1)}, bf16[10,64,256]{2,1,0:T(8,128)(2,1)S(1)}, u32[]{:S(2)}, u32[]{:S(2)}) collective-permute-start(bf16[10,64,256]{2,1,0:T(8,128)(2,1)S(1)} %collective-permute-done.1.refs_1_.refs_2_), channel_id=1, source_target_pairs={{0,1},{1,0},{2,3},{3,2},{4,5},{5,4},{6,7},{7,6},{8,9},{9,8},{10,11... | collective-permute-start | bytes 983048 | tf_op jit(solution)/shard_map/ppermute | solution.py:512
  25.0 10.4 %collective-permute-start.4 = (bf16[10,64,256]{2,1,0:T(8,128)(2,1)S(1)}, bf16[10,64,256]{2,1,0:T(8,128)(2,1)S(1)}, u32[]{:S(2)}, u32[]{:S(2)}) collective-permute-start(bf16[10,64,256]{2,1,0:T(8,128)(2,1)S(1)} %collective-permute-done.3.refs_4_), channel_id=1, source_target_pairs={{0,1},{1,0},{2,3},{3,2},{4,5},{5,4},{6,7},{7,6},{8,9},{9,8},{10,11... | collective-permute-start | bytes 983048 | tf_op jit(solution)/shard_map/ppermute | solution.py:512
  25.0 10.4 %collective-permute-start.6 = (bf16[10,64,256]{2,1,0:T(8,128)(2,1)S(1)}, bf16[10,64,256]{2,1,0:T(8,128)(2,1)S(1)}, u32[]{:S(2)}, u32[]{:S(2)}) collective-permute-start(bf16[10,64,256]{2,1,0:T(8,128)(2,1)S(1)} %collective-permute-done.5.refs_6_), channel_id=1, source_target_pairs={{0,1},{1,0},{2,3},{3,2},{4,5},{5,4},{6,7},{7,6},{8,9},{9,8},{10,11... | collective-permute-start | bytes 983048 | tf_op jit(solution)/shard_map/ppermute | solution.py:512
  40.0 12.0 %collective-permute-start.14 = (bf16[2,2,6,64,256]{4,3,2,1,0:T(8,128)(2,1)S(1)}, bf16[2,2,6,64,256]{4,3,2,1,0:T(8,128)(2,1)S(1)}, u32[]{:S(2)}, u32[]{:S(2)}) collective-permute-start(bf16[2,2,6,64,256]{4,3,2,1,0:T(8,128)(2,1)S(1)} %get-tuple-element.81.refs_7_), channel_id=1, source_target_pairs={{0,1},{1,0},{2,3},{3,2},{4,5},{5,4},{6,7},{7,6},{8,9},{9,8},{10,11... | collective-permute-start | bytes 2359304 | tf_op jit(solution)/shard_map/ppermute | solution.py:512
  40.1 14.3 %collective-permute-start.19 = (bf16[16,64,256]{2,1,0:T(8,128)(2,1)S(1)}, bf16[16,64,256]{2,1,0:T(8,128)(2,1)S(1)}, u32[]{:S(2)}, u32[]{:S(2)}) collective-permute-start(bf16[16,64,256]{2,1,0:T(8,128)(2,1)S(1)} %shard_map.83.refs_2_), channel_id=1, source_target_pairs={{0,4},{4,0},{8,12},{12,8},{16,20},{20,16},{24,28},{28,24},{1,5},{5... | collective-permute-start | bytes 1572872 | tf_op jit(solution)/shard_map/ppermute | solution.py:509
  40.7 12.3 %collective-permute-start.18 = (bf16[2,6,64,256]{3,2,1,0:T(8,128)(2,1)S(1)}, bf16[2,6,64,256]{3,2,1,0:T(8,128)(2,1)S(1)}, u32[]{:S(2)}, u32[]{:S(2)}) collective-permute-start(bf16[2,6,64,256]{3,2,1,0:T(8,128)(2,1)S(1)} %get-tuple-element.87.refs_0_), channel_id=1, source_target_pairs={{0,2},{1,3},{2,0},{3,1},{4,6},{5,7},{6,4},{7,5},{8,10},{9,11},{10,... | collective-permute-start | bytes 1179656 | tf_op jit(solution)/shard_map/ppermute | solution.py:512
  42.8 7.6 %collective-permute-start.12 = (bf16[128,256]{1,0:T(8,128)(2,1)S(1)}, bf16[128,256]{1,0:T(8,128)(2,1)S(1)}, u32[]{:S(2)}, u32[]{:S(2)}) collective-permute-start(bf16[128,256]{1,0:T(8,128)(2,1)S(1)} %get-tuple-element.78), channel_id=1, source_target_pairs={{0,16},{4,20},{8,24},{12,28},{16,0},{20,4},{24,8},{28,12},{1,17},{... | collective-permute-start | bytes 196616 | tf_op jit(solution)/shard_map/ppermute | solution.py:509
  54.5 11.0 %collective-permute-start.20 = (bf16[2,2,6,64,256]{4,3,2,1,0:T(8,128)(2,1)S(1)}, bf16[2,2,6,64,256]{4,3,2,1,0:T(8,128)(2,1)S(1)}, u32[]{:S(2)}, u32[]{:S(2)}) collective-permute-start(bf16[2,2,6,64,256]{4,3,2,1,0:T(8,128)(2,1)S(1)} %get-tuple-element.89.refs_7_), channel_id=1, source_target_pairs={{0,1},{1,0},{2,3},{3,2},{4,5},{5,4},{6,7},{7,6},{8,9},{9,8},{10,11... | collective-permute-start | bytes 2359304 | tf_op jit(solution)/shard_map/ppermute | solution.py:512
  54.6 11.9 %collective-permute-start.24 = (bf16[2,6,64,256]{3,2,1,0:T(8,128)(2,1)S(1)}, bf16[2,6,64,256]{3,2,1,0:T(8,128)(2,1)S(1)}, u32[]{:S(2)}, u32[]{:S(2)}) collective-permute-start(bf16[2,6,64,256]{3,2,1,0:T(8,128)(2,1)S(1)} %get-tuple-element.95.refs_0_), channel_id=1, source_target_pairs={{0,2},{1,3},{2,0},{3,1},{4,6},{5,7},{6,4},{7,5},{8,10},{9,11},{10,... | collective-permute-start | bytes 1179656 | tf_op jit(solution)/shard_map/ppermute | solution.py:512
  66.6 10.9 %collective-permute-start.25 = (bf16[2,2,6,64,256]{4,3,2,1,0:T(8,128)(2,1)S(1)}, bf16[2,2,6,64,256]{4,3,2,1,0:T(8,128)(2,1)S(1)}, u32[]{:S(2)}, u32[]{:S(2)}) collective-permute-start(bf16[2,2,6,64,256]{4,3,2,1,0:T(8,128)(2,1)S(1)} %get-tuple-element.96.refs_7_), channel_id=1, source_target_pairs={{0,1},{1,0},{2,3},{3,2},{4,5},{5,4},{6,7},{7,6},{8,9},{9,8},{10,11... | collective-permute-start | bytes 2359304 | tf_op jit(solution)/shard_map/ppermute | solution.py:512
  66.7 11.7 %collective-permute-start.29 = (bf16[2,4,64,256]{3,2,1,0:T(8,128)(2,1)S(1)}, bf16[2,4,64,256]{3,2,1,0:T(8,128)(2,1)S(1)}, u32[]{:S(2)}, u32[]{:S(2)}) collective-permute-start(bf16[2,4,64,256]{3,2,1,0:T(8,128)(2,1)S(1)} %get-tuple-element.101.refs_0_), channel_id=1, source_target_pairs={{0,2},{1,3},{2,0},{3,1},{4,6},{5,7},{6,4},{7,5},{8,10},{9,11},{10,... | collective-permute-start | bytes 786440 | tf_op jit(solution)/shard_map/ppermute | solution.py:512
  69.1 8.4 %collective-permute-start.22 = (bf16[128,256]{1,0:T(8,128)(2,1)S(1)}, bf16[128,256]{1,0:T(8,128)(2,1)S(1)}, u32[]{:S(2)}, u32[]{:S(2)}) collective-permute-start(bf16[128,256]{1,0:T(8,128)(2,1)S(1)} %get-tuple-element.92), channel_id=1, source_target_pairs={{0,16},{4,20},{8,24},{12,28},{16,0},{20,4},{24,8},{28,12},{1,17},{... | collective-permute-start | bytes 196616 | tf_op jit(solution)/shard_map/ppermute | solution.py:509
  72.6 18.6 %collective-permute-start.35 = (bf16[18,64,256]{2,1,0:T(8,128)(2,1)S(1)}, bf16[18,64,256]{2,1,0:T(8,128)(2,1)S(1)}, u32[]{:S(2)}, u32[]{:S(2)}) collective-permute-start(bf16[18,64,256]{2,1,0:T(8,128)(2,1)S(1)} %shard_map.91.refs_2_), channel_id=1, source_target_pairs={{0,4},{4,0},{8,12},{12,8},{16,20},{20,16},{24,28},{28,24},{1,5},{5... | collective-permute-start | bytes 1769480 | tf_op jit(solution)/shard_map/ppermute | solution.py:509
  78.5 11.8 %collective-permute-start.30 = (bf16[2,2,4,64,256]{4,3,2,1,0:T(8,128)(2,1)S(1)}, bf16[2,2,4,64,256]{4,3,2,1,0:T(8,128)(2,1)S(1)}, u32[]{:S(2)}, u32[]{:S(2)}) collective-permute-start(bf16[2,2,4,64,256]{4,3,2,1,0:T(8,128)(2,1)S(1)} %get-tuple-element.103.refs_5_), channel_id=1, source_target_pairs={{0,1},{1,0},{2,3},{3,2},{4,5},{5,4},{6,7},{7,6},{8,9},{9,8},{10,11... | collective-permute-start | bytes 1572872 | tf_op jit(solution)/shard_map/ppermute | solution.py:512
  78.6 12.6 %collective-permute-start.34 = (bf16[2,6,64,256]{3,2,1,0:T(8,128)(2,1)S(1)}, bf16[2,6,64,256]{3,2,1,0:T(8,128)(2,1)S(1)}, u32[]{:S(2)}, u32[]{:S(2)}) collective-permute-start(bf16[2,6,64,256]{3,2,1,0:T(8,128)(2,1)S(1)} %get-tuple-element.106.refs_0_), channel_id=1, source_target_pairs={{0,2},{1,3},{2,0},{3,1},{4,6},{5,7},{6,4},{7,5},{8,10},{9,11},{10,... | collective-permute-start | bytes 1179656 | tf_op jit(solution)/shard_map/ppermute | solution.py:512
  91.3 10.1 %collective-permute-start.36 = (bf16[2,2,6,64,256]{4,3,2,1,0:T(8,128)(2,1)S(1)}, bf16[2,2,6,64,256]{4,3,2,1,0:T(8,128)(2,1)S(1)}, u32[]{:S(2)}, u32[]{:S(2)}) collective-permute-start(bf16[2,2,6,64,256]{4,3,2,1,0:T(8,128)(2,1)S(1)} %get-tuple-element.108.refs_6_), channel_id=1, source_target_pairs={{0,1},{1,0},{2,3},{3,2},{4,5},{5,4},{6,7},{7,6},{8,9},{9,8},{10,11... | collective-permute-start | bytes 2359304 | tf_op jit(solution)/shard_map/ppermute | solution.py:512
  91.4 11.5 %collective-permute-start.40 = (bf16[2,6,64,256]{3,2,1,0:T(8,128)(2,1)S(1)}, bf16[2,6,64,256]{3,2,1,0:T(8,128)(2,1)S(1)}, u32[]{:S(2)}, u32[]{:S(2)}) collective-permute-start(bf16[2,6,64,256]{3,2,1,0:T(8,128)(2,1)S(1)} %get-tuple-element.110.refs_0_), channel_id=1, source_target_pairs={{0,2},{1,3},{2,0},{3,1},{4,6},{5,7},{6,4},{7,5},{8,10},{9,11},{10,... | collective-permute-start | bytes 1179656 | tf_op jit(solution)/shard_map/ppermute | solution.py:512
  92.9 8.5 %collective-permute-start.32 = (bf16[128,256]{1,0:T(8,128)(2,1)S(1)}, bf16[128,256]{1,0:T(8,128)(2,1)S(1)}, u32[]{:S(2)}, u32[]{:S(2)}) collective-permute-start(bf16[128,256]{1,0:T(8,128)(2,1)S(1)} %get-tuple-element.104.refs_4_.refs_1_.refs_5_.refs_9_), channel_id=1, source_target_pairs={{0,16},{4,20},{8,24},{12,28},{16,0},{20,4},{24,8},{28,12},{1,17},{... | collective-permute-start | bytes 196616 | tf_op jit(solution)/shard_map/ppermute | solution.py:509
  103.0 10.3 %collective-permute-start.41 = (bf16[2,2,6,64,256]{4,3,2,1,0:T(8,128)(2,1)S(1)}, bf16[2,2,6,64,256]{4,3,2,1,0:T(8,128)(2,1)S(1)}, u32[]{:S(2)}, u32[]{:S(2)}) collective-permute-start(bf16[2,2,6,64,256]{4,3,2,1,0:T(8,128)(2,1)S(1)} %get-tuple-element.111.refs_7_), channel_id=1, source_target_pairs={{0,1},{1,0},{2,3},{3,2},{4,5},{5,4},{6,7},{7,6},{8,9},{9,8},{10,11... | collective-permute-start | bytes 2359304 | tf_op jit(solution)/shard_map/ppermute | solution.py:512
  103.1 11.5 %collective-permute-start.45 = (bf16[2,6,64,256]{3,2,1,0:T(8,128)(2,1)S(1)}, bf16[2,6,64,256]{3,2,1,0:T(8,128)(2,1)S(1)}, u32[]{:S(2)}, u32[]{:S(2)}) collective-permute-start(bf16[2,6,64,256]{3,2,1,0:T(8,128)(2,1)S(1)} %get-tuple-element.113.refs_0_), channel_id=1, source_target_pairs={{0,2},{1,3},{2,0},{3,1},{4,6},{5,7},{6,4},{7,5},{8,10},{9,11},{10,... | collective-permute-start | bytes 1179656 | tf_op jit(solution)/shard_map/ppermute | solution.py:512
  104.8 8.4 %collective-permute-start.38 = (bf16[128,256]{1,0:T(8,128)(2,1)S(1)}, bf16[128,256]{1,0:T(8,128)(2,1)S(1)}, u32[]{:S(2)}, u32[]{:S(2)}) collective-permute-start(bf16[128,256]{1,0:T(8,128)(2,1)S(1)} %shard_map.93.refs_4_.refs_1_.refs_5_.refs_3_), channel_id=1, source_target_pairs={{0,16},{4,20},{8,24},{12,28},{16,0},{20,4},{24,8},{28,12},{1,17},{... | collective-permute-start | bytes 196616 | tf_op jit(solution)/shard_map/ppermute | solution.py:509
  114.7 10.3 %collective-permute-start.46 = (bf16[2,2,6,64,256]{4,3,2,1,0:T(8,128)(2,1)S(1)}, bf16[2,2,6,64,256]{4,3,2,1,0:T(8,128)(2,1)S(1)}, u32[]{:S(2)}, u32[]{:S(2)}) collective-permute-start(bf16[2,2,6,64,256]{4,3,2,1,0:T(8,128)(2,1)S(1)} %get-tuple-element.114.refs_7_), channel_id=1, source_target_pairs={{0,1},{1,0},{2,3},{3,2},{4,5},{5,4},{6,7},{7,6},{8,9},{9,8},{10,11... | collective-permute-start | bytes 2359304 | tf_op jit(solution)/shard_map/ppermute | solution.py:512
  114.8 11.5 %collective-permute-start.50 = (bf16[2,6,64,256]{3,2,1,0:T(8,128)(2,1)S(1)}, bf16[2,6,64,256]{3,2,1,0:T(8,128)(2,1)S(1)}, u32[]{:S(2)}, u32[]{:S(2)}) collective-permute-start(bf16[2,6,64,256]{3,2,1,0:T(8,128)(2,1)S(1)} %get-tuple-element.116.refs_0_), channel_id=1, source_target_pairs={{0,2},{1,3},{2,0},{3,1},{4,6},{5,7},{6,4},{7,5},{8,10},{9,11},{10,... | collective-permute-start | bytes 1179656 | tf_op jit(solution)/shard_map/ppermute | solution.py:512
  116.8 8.3 %collective-permute-start.43 = (bf16[128,256]{1,0:T(8,128)(2,1)S(1)}, bf16[128,256]{1,0:T(8,128)(2,1)S(1)}, u32[]{:S(2)}, u32[]{:S(2)}) collective-permute-start(bf16[128,256]{1,0:T(8,128)(2,1)S(1)} %shard_map.96.refs_4_.refs_1_.refs_2_), channel_id=1, source_target_pairs={{0,16},{4,20},{8,24},{12,28},{16,0},{20,4},{24,8},{28,12},{1,17},{... | collective-permute-start | bytes 196616 | tf_op jit(solution)/shard_map/ppermute | solution.py:509
  126.4 9.7 %collective-permute-start.51 = (bf16[2,2,6,64,256]{4,3,2,1,0:T(8,128)(2,1)S(1)}, bf16[2,2,6,64,256]{4,3,2,1,0:T(8,128)(2,1)S(1)}, u32[]{:S(2)}, u32[]{:S(2)}) collective-permute-start(bf16[2,2,6,64,256]{4,3,2,1,0:T(8,128)(2,1)S(1)} %shard_map.101.refs_7_), channel_id=1, source_target_pairs={{0,1},{1,0},{2,3},{3,2},{4,5},{5,4},{6,7},{7,6},{8,9},{9,8},{10,11... | collective-permute-start | bytes 2359304 | tf_op jit(solution)/shard_map/ppermute | solution.py:512
  127.7 8.4 %collective-permute-start.48 = (bf16[128,256]{1,0:T(8,128)(2,1)S(1)}, bf16[128,256]{1,0:T(8,128)(2,1)S(1)}, u32[]{:S(2)}, u32[]{:S(2)}) collective-permute-start(bf16[128,256]{1,0:T(8,128)(2,1)S(1)} %shard_map.99.refs_2_.refs_1_), channel_id=1, source_target_pairs={{0,16},{4,20},{8,24},{12,28},{16,0},{20,4},{24,8},{28,12},{1,17},{... | collective-permute-start | bytes 196616 | tf_op jit(solution)/shard_map/ppermute | solution.py:509
  (34 other events, 190.8 us)

commit v2 on v1

--- a/solution.py
+++ b/solution.py
@@ -36,6 +36,7 @@
         self.group_rows = bwd_t.shape[2]
         self.slab = (self.supers * self.chunk, self.width)
         self.chips = [(dp, dg) for dg in range(0, self.groups, 2) for dp in range(self.parts)]
+        self.shared = self.levels % 2 == 1
         self.coded = -(-3 * (self.levels - 1) // 16) * 16
         self.sources = self.supers * self.group_rows
         self.blocks = [(dp, dg) for dp in range(self.parts) for dg in range(self.groups)]
@@ -45,70 +46,51 @@
         return leaf // self.parts, leaf % self.parts, grid
 
 
-def fetch(plan, blocks, pieces, sems):
-    _, part, grid = plan.place()
-    copies, k = [], plan.kept
-    for slab, make in pieces:
-        group = []
-        for ref, (dp, dg) in zip(blocks, plan.blocks):
-            sem = sems.at[len(copies) * len(plan.blocks) + len(group)]
-            source = ref.at[pl.ds(slab * k, k)]
-            group.append(pltpu.make_async_copy(source, make(part ^ dp, grid ^ dg), sem))
-            group[-1].start()
-        copies.append(group)
-    return copies
-
-
 def wait(group):
     for copy in group:
         copy.wait()
 
 
-def matrix(plan, ref, s):
-    whole = ref[s // plan.kept, s % plan.kept]
-    return whole.reshape(-1, whole.shape[-1])
+def block_of(plan, stacks, p, g, row):
+    same = lax.axis_index("grid") % 2 == g % 2
+    return jnp.where(same, stacks[0][g // 2, p, row], stacks[1][g // 2, p, row])
 
 
 def joined(plan, stacks, slab, s, count=1):
-    own, other = stacks
-    first = lax.axis_index("grid") % 2 == 0
-    rows = []
-    for x in range(plan.groups // 2):
-        at = [(x, s // plan.kept, (slab + i) * plan.kept + s % plan.kept) for i in range(count)]
-        rows += [jnp.where(first, own[i], other[i]) for i in at]
-        rows += [jnp.where(first, other[i], own[i]) for i in at]
+    p, k = s // plan.kept, s % plan.kept
+    rows = [
+        block_of(plan, stacks, p, g, (slab + i) * plan.kept + k)
+        for g in range(plan.groups)
+        for i in range(count)
+    ]
     return jnp.concatenate(rows, axis=0)
 
 
-def start_slab(plan, pieces, at, upper):
+def start_slab(plan, stacks, first, level):
+    low_core = lax.axis_index("grid") % 2 == 0
+
+    def piece(p, g):
+        both = block_of(plan, stacks, p, g, first + level // 2).astype(F32)
+        return jnp.where(low_core, both[:, :LANES], both[:, LANES:])
+
     out = []
     for pair in range(plan.groups // 2):
-        out.append(
-            jnp.concatenate(
-                [
-                    cross(*[pieces[p, 2 * pair + i, at].astype(F32) for i in range(2)])[upper]
-                    for p in range(plan.parts)
-                ],
-                axis=0,
-            )
-        )
+        halves = [cross(piece(p, 2 * pair), piece(p, 2 * pair + 1))[level % 2] for p in range(plan.parts)]
+        out.append(jnp.concatenate(halves, axis=0))
     return jnp.concatenate(out, axis=1)
 
 
-def fetch_pieces(plan, blocks, first, count, target, sems, at):
-    _, part, grid = plan.place()
-    lanes = pl.ds(pl.multiple_of(grid % 2 * LANES, LANES), LANES)
-    copies = []
-    for ref, (dp, dg) in zip(blocks, plan.blocks):
-        for i in range(count):
-            copy = pltpu.make_async_copy(
-                ref.at[first + i, :, lanes],
-                target.at[part ^ dp, grid ^ dg, i],
-                sems.at[at + len(copies)],
-            )
-            copy.start()
-            copies.append(copy)
-    return copies
+def coded_lines(plan, stacks, p, g, end):
+    if not plan.shared:
+        return block_of(plan, stacks, p, g, end)[: plan.coded].astype(F32)
+    both = block_of(plan, stacks, p, g, end - 1).astype(F32)
+    lines = jnp.where(lax.axis_index("grid") % 2 == 0, both[:, :LANES], both[:, LANES:])
+    low = lax.broadcasted_iota(jnp.int32, (plan.coded, LANES), 1) < LANES // 2
+    out = []
+    for i in range(0, 2 * plan.width // LANES, 2):
+        one, two = [lines[(i + j) * plan.coded : (i + j + 1) * plan.coded] for j in range(2)]
+        out.append(jnp.where(low, pltpu.roll(one, LANES // 2, 1), two))
+    return jnp.concatenate(out, axis=1)
 
 
 def copy_matrices(plan, sources, layout, target, sems, at):
@@ -133,7 +115,7 @@
     sources = [refs.pop(0) for _ in range(4)]
     rhs_ref, owner_ref, row_ref = [refs.pop(0) for _ in range(3)]
     firsts, second_ref = [refs.pop(0) for _ in plan.chips], refs.pop(0)
-    raw_ref, turned_ref, sent_ref, sems = refs
+    raw_ref, turned_ref, sems = refs
     owner_at, part, grid = plan.place()
     k, r, c = plan.kept, plan.rows, plan.chunk
     fill = pltpu.make_async_copy(rhs_ref, raw_ref, sems.at[0])
@@ -155,8 +137,15 @@
     now, then = lax.broadcasted_iota(jnp.int32, shape, 0), lax.broadcasted_iota(jnp.int32, shape, 1)
     move = jnp.where(now == then % plan.group_rows * k + then // plan.group_rows, 1.0, 0.0).astype(BF)
     lines = nn(jnp.concatenate(lines, axis=0).astype(BF), move).astype(BF)
-    for i in range(len(plan.chips)):
-        sent_ref[i, len(pairs)] = lines
+    if plan.shared:
+        lines = lines[: plan.coded].astype(F32)
+        parts = []
+        for i in range(0, plan.width, LANES):
+            parts += [pltpu.roll(lines[:, i : i + LANES], LANES // 2, 1), lines[:, i : i + LANES]]
+        lines = jnp.concatenate(parts, axis=0)
+    else:
+        for target in firsts:
+            target[first + len(pairs)] = lines
     shape = (plan.columns, plan.columns)
     same = lax.broadcasted_iota(jnp.int32, shape, 0) == lax.broadcasted_iota(jnp.int32, shape, 1)
     same = jnp.where(same, 1.0, 0.0).astype(BF)
@@ -166,17 +155,16 @@
             two = [raw_ref[level, s] for level in pair]
             two += [jnp.zeros((r, plan.columns), BF)] * (2 - len(two))
             turned_ref[s] = nt(same, jnp.concatenate(two, axis=0)).astype(BF)
-        for i, (dp, dg) in enumerate(plan.chips):
+        for target, (dp, dg) in zip(firsts, plan.chips):
             for s in range(k):
                 for core in range(2):
                     column = ((part ^ dp) * plan.groups + (grid ^ dg) // 2 * 2 + core) * c
                     piece = turned_ref[s, pl.ds(pl.multiple_of(column, c), c), :]
-                    sent_ref[i, j, s * c : (s + 1) * c, core * LANES : (core + 1) * LANES] = piece
-    extra = len(pairs) + 1
-    for i, target in enumerate(firsts):
-        copy = pltpu.make_async_copy(sent_ref.at[i], target.at[pl.ds(first, extra)], sems.at[1 + len(copies)])
-        copy.start()
-        copies.append(copy)
+                    if plan.shared and j == len(pairs) - 1:
+                        low = lax.broadcasted_iota(jnp.int32, piece.shape, 1) < LANES // 2
+                        here = lines[s * c : (s + 1) * c]
+                        piece = jnp.where(low, piece.astype(F32), here).astype(BF)
+                    target[first + j, s * c : (s + 1) * c, core * LANES : (core + 1) * LANES] = piece
     wait(copies)
 
 
@@ -287,7 +275,7 @@
                 out[part ^ i] = ref[first : first + out.shape[1]]
 
 
-def forward_kernel(plan, level, part_of, added, *refs):
+def forward_kernel(plan, level, part_of, added, unread, *refs):
     refs = list(refs)
     last, fresh = level == plan.levels - 1, level == 0
     c, halves = plan.chunk, plan.update_rows // plan.width
@@ -295,9 +283,9 @@
     if not fresh:
         start_ref, *arrived = [refs.pop(0) for _ in range(1 + plan.owners)]
     more_ref = refs.pop(0) if added else None
-    blocks = [refs.pop(0) for _ in (plan.blocks if fresh else range(2))]
+    blocks = [refs.pop(0) for _ in range(2)]
     if fresh:
-        del refs[: len(plan.chips)]
+        del refs[:unread]
     out_ref = refs.pop(0)
     if last:
         solved_ref = refs.pop(0)
@@ -307,39 +295,16 @@
     if fresh:
         key_ref = refs.pop(0)
         next_refs = [refs.pop(0) for _ in range(plan.levels - 1)]
-        coded_ref, piece_ref, inv_ref, upd_ref, sems = refs
-        _, part, grid = plan.place()
-        pairs, size = piece_ref.shape[2], len(plan.blocks)
-        first = blocks[0].shape[0] - 1 - pairs
-        arriving = fetch_pieces(plan, blocks, first, pairs, piece_ref, sems, size * (2 + halves))
-        pieces = [(part_of["fwd"], lambda p, g: inv_ref.at[p, :, g])]
-        for half in range(halves):
-            pieces.append((part_of["upd"] + half, lambda p, g, half=half: upd_ref.at[half, p, :, g]))
-        copies = fetch(plan, blocks, pieces, sems)
-        coded = []
-        for i, (ref, (dp, dg)) in enumerate(zip(blocks, plan.blocks)):
-            coded.append(
-                pltpu.make_async_copy(
-                    ref.at[ref.shape[0] - 1, pl.ds(0, plan.coded)],
-                    coded_ref.at[part ^ dp, grid ^ dg],
-                    sems.at[(1 + halves) * size + i],
-                )
-            )
-            coded[-1].start()
-        wait(arriving)
-        block = start_slab(plan, piece_ref, 0, 0)
-        wait(copies[0])
-        lower = lambda s: matrix(plan, inv_ref, s)
-        update = lambda s, half: matrix(plan, upd_ref.at[half], s)
+        pairs = (plan.levels + 1) // 2
+        first = blocks[0].shape[2] - (not plan.shared) - pairs
+        block = start_slab(plan, blocks, first, 0)
     else:
         block = start_ref[...] - arrived[0][...]
         for ref in arrived[1:]:
             block = block - ref[...].astype(F32)
-        lower = lambda s: joined(plan, blocks, part_of["fwd"], s)
-        update = lambda s, half: joined(plan, blocks, part_of["upd"] + half, s)
     block = block.astype(BF)
     solved = jnp.concatenate(
-        [nt(block[s * c : (s + 1) * c], lower(s)) for s in range(plan.supers)], axis=0
+        [nt(block[s * c : (s + 1) * c], joined(plan, blocks, part_of["fwd"], s)) for s in range(plan.supers)], axis=0
     )
     out_ref[...] = solved
     lowered = solved.astype(BF)
@@ -349,24 +314,22 @@
             solved_ref[at, :] = nt(lowered[at], joined(plan, blocks, part_of["inv"], s)).astype(BF)
         return
     if fresh:
-        wait(coded)
+        coded = [
+            [coded_lines(plan, blocks, p, g, first + pairs) for p in range(plan.parts)]
+            for g in range(plan.groups)
+        ]
         for to in range(plan.levels - 1):
             for g in range(plan.groups):
                 distance, row, super_to = [
-                    jnp.concatenate(
-                        [coded_ref[p, g, 3 * to + i : 3 * to + i + 1, :] for p in range(plan.parts)], axis=1
-                    ).astype(F32)
-                    for i in range(3)
+                    jnp.concatenate([x[3 * to + i : 3 * to + i + 1] for x in coded[g]], axis=1) for i in range(3)
                 ]
                 key_ref[0, to, g : g + 1, :] = (distance * plan.rows + row).astype(jnp.int32)
                 key_ref[1, to, g : g + 1, :] = super_to.astype(jnp.int32)
-        for group in copies[1:]:
-            wait(group)
     for s in range(plan.supers):
         at = slice(s * c, (s + 1) * c)
         for half in range(halves):
             lanes = slice(half * plan.width, (half + 1) * plan.width)
-            sent_ref[at, lanes] = nn(lowered[at], update(s, half)).astype(BF)
+            sent_ref[at, lanes] = nn(lowered[at], joined(plan, blocks, part_of["upd"] + half, s)).astype(BF)
 
     def emit(to, distance, pair, value):
         lanes = slice(pair * LANES, (pair + 1) * LANES)
@@ -377,7 +340,7 @@
     scatter(plan, sent_ref[...], key_ref, level, [level + 1], emit)
     if fresh:
         for i, ref in enumerate(next_refs):
-            ref[...] = start_slab(plan, piece_ref, (i + 1) // 2, (i + 1) % 2)
+            ref[...] = start_slab(plan, blocks, first, i + 1)
 
 
 def ahead_kernel(plan, level, *refs):
@@ -511,6 +474,10 @@
     def over_grid(x, step):
         return lax.ppermute(x, "grid", [(i, i ^ step) for i in range(plan.groups)])
 
+    def from_owners(x):
+        got = {d: over_leaf(x[d], d * plan.parts) for d in reversed(range(1, owners))}
+        return [x[0]] + [got[d] for d in range(1, owners)]
+
     def swap(x, dp, dg):
         if (dp, dg) == (0, 0):
             return x
@@ -542,7 +509,7 @@
     slab = (plan.rows, plan.width)
     matrices_given = (fwd_inv, bwd_inv, upd_t, bwd_t)
 
-    ways, extra = len(plan.chips), len(pairs) + 1
+    ways, extra = len(plan.chips), len(pairs) + (not plan.shared)
     *given, second = call(
         functools.partial(first_kernel, plan, layouts[0], layouts[1], pairs),
         [*matrices_given, rhs, dest_owner.reshape(dest_row.shape), dest_row],
@@ -552,8 +519,7 @@
         [
             pltpu.VMEM(rhs.shape, BF),
             pltpu.VMEM((plan.kept, plan.columns, LANES), BF),
-            pltpu.VMEM((ways, extra) + slab, BF),
-            pltpu.SemaphoreType.DMA((1 + ways * (len(layouts[0]) + 1) + len(layouts[1]),)),
+            pltpu.SemaphoreType.DMA((1 + ways * len(layouts[0]) + len(layouts[1]),)),
         ],
         1, 2**20, PACK_VMEM_BYTES,
     )
@@ -567,20 +533,27 @@
         [pltpu.SemaphoreType.DMA((sum(len(x) for x in grouped),))],
         1, 2**20,
     )
-    given[-1] = gate(given[-1], owned[0])
     got = {chip: swap(x, *chip) for chip, x in zip(plan.chips, given)}
-    chunks = {0: [got[dp, dg] if dg % 2 == 0 else over_grid(got[dp, dg - 1], 1) for dp, dg in plan.blocks]}
-
     def to_part(x):
         return [x] + [over_leaf(x, dp) for dp in range(1, plan.parts)]
 
     def to_chip(x):
         return [x] + [over_grid(x, dg) for dg in range(2, plan.groups, 2)]
 
-    chip_there = got[plan.chips[-2]]
-    second = to_part(gate(second, chip_there))
+    second = to_part(second)
     second = second + sum([[over_grid(x, dg) for x in second] for dg in range(2, plan.groups, 2)], [])
-    from_part, two = {}, {1: [(x, 0) for x in second]}
+    third = to_part(owned[0])
+    shape = (plan.groups // 2, plan.parts)
+    begun = stack(
+        plan,
+        [
+            ([(got[chip], 0) for chip in plan.chips], shape + given[0].shape),
+            ([(x, 0) for x in second], shape + second[0].shape),
+            ([(x, 0) for x in third], (plan.parts,) + third[0].shape),
+        ],
+    )
+    chunks = {number: [begun[number], over_grid(begun[number], 1)] for number in range(2)}
+    from_part, two = {}, {2: [(x, 0) for x in to_chip(begun[2])]}
 
     def slices(first, last, x):
         parts, at = to_part(x), 0
@@ -589,12 +562,10 @@
             at += sizes[number]
         return parts[-1]
 
-    marks = [slices(2, 3, gate(owned[0], chip_there))]
-    before_first = second[1:] + marks
+    marks = [slices(3, later, gate(owned[1], begun[2]))]
+    before_first = []
 
     def advance(stage, mark):
-        if stage == 0:
-            marks.append(slices(3, later, gate(owned[1], mark)))
         if stage == 1:
             slices(later, len(layouts), gate(owned[2], mark, marks[-1]))
         jobs, done = [], []
@@ -635,7 +606,7 @@
             args.append(more)
             specs.append(VM)
         args += blocks
-        specs += [ANY if fresh else VM] * count
+        specs += [VM] * count
         if fresh:
             args += before_first
             specs += [UNREAD] * len(before_first)
@@ -648,20 +619,12 @@
         if fresh:
             outs.append(((2, levels - 1, plan.groups, plan.sources), jnp.int32))
             outs += [(plan.slab, F32)] * top
-        scratch = []
-        if fresh:
-            scratch = [
-                pltpu.VMEM((plan.parts, plan.groups, plan.coded, plan.width), BF),
-                pltpu.VMEM((plan.parts, plan.groups, len(pairs), plan.rows, LANES), BF),
-                pltpu.VMEM(full, BF),
-                pltpu.VMEM((halves,) + full, BF),
-                pltpu.SemaphoreType.DMA((len(plan.blocks) * (2 + halves + len(pairs)),)),
-            ]
         got = call(
             functools.partial(
-                forward_kernel, plan, level, part_of, more is not None and not last
+                forward_kernel, plan, level, part_of, more is not None and not last,
+                len(before_first),
             ),
-            args, specs, outs, scratch, one_pass, 24 * slab_bytes,
+            args, specs, outs, [], one_pass, 24 * slab_bytes,
         )
         forward_out.append(got[0])
         if last:
@@ -671,7 +634,7 @@
         if fresh:
             keys = got[-1 - top]
             starts.update(zip(range(1, levels), got[-top:]))
-        arrived = [got[2]] + [over_leaf(got[2 + d], d * plan.parts) for d in range(1, owners)]
+        arrived = from_owners(got[2 : 2 + owners])
         advance(level, got[1])
         more = None
         if level + 1 < top:
@@ -685,7 +648,7 @@
     everywhere = {}
     for level in reversed(range(top)):
         above = solutions[level + 1]
-        everywhere[level + 1] = [above] + [over_leaf(above, d * plan.parts) for d in range(1, owners)]
+        everywhere[level + 1] = from_owners([above] * owners)
         froms = list(range(level + 2, levels))
         known = []
         if froms:
@@ -711,7 +674,9 @@
         [solutions[level] for level in range(levels)], [VM] * levels,
         [(piece, BF)] * len(plan.blocks), [], 1, 8 * slab_bytes,
     )
-    theirs = [swap(x, dp, dg) for x, (dp, dg) in zip(own, plan.blocks)]
+    far_first = sorted(range(len(plan.blocks)), key=lambda i: -sum(b.bit_count() for b in plan.blocks[i]))
+    theirs = {i: swap(own[i], *plan.blocks[i]) for i in far_first}
+    theirs = [theirs[i] for i in range(len(own))]
     (result,) = call(
         functools.partial(result_kernel, plan),
         theirs, [VM] * len(theirs), [(rhs.shape, BF)],

time: 148 us -> 139 us (0.939)
  waiting for transfers between devices: 58 us -> 54 us
  Pallas kernels: 23.3 us -> 20.4 us
  starting transfers between devices: 65.1 us -> 62.7 us
    ppermute x10, waiting for transfers between devices: 13.3 us -> 3.11 us  [swap(): return lax.ppermute(x, ('leaf', 'grid'), moves)]
    ppermute x28, waiting for transfers between devices: 42.2 us -> 47.8 us  [over_leaf(): return lax.ppermute(x, 'leaf', [(i, i ^ step) for i in range(plan.leaves)])]
    ppermute x28, starting transfers between devices: 44.3 us -> 40.2 us  [over_leaf(): return lax.ppermute(x, 'leaf', [(i, i ^ step) for i in range(plan.leaves)])]
    pallas_call x27, Pallas kernels: 23.3 us -> 20.4 us  [call(): pl.pallas_call(body, in_specs=specs, out_specs=[VM] * len(outs), out_shap...]
    ppermute x21 -> x18, starting transfers between devices: 9.83 us -> 12.7 us  [over_grid(): return lax.ppermute(x, 'grid', [(i, i ^ step) for i in range(plan.groups)])]
    ppermute x21 -> x18, waiting for transfers between devices: 2.5 us -> 3.09 us  [over_grid(): return lax.ppermute(x, 'grid', [(i, i ^ step) for i in range(plan.groups)])]
  transfers between devices with their start and end apart: 59 -> 56, of which waited for: 25 -> 25; matrix products, arithmetic and copies ran while one was open for 0% -> 0% of each run, Pallas kernels for 9% -> 10%
where the time goes in v2:
time: 139 us; the launch traced here: 138 us
  starting transfers between devices  62.7 us (45%)
  waiting for transfers between devices  54 us (39%)
  Pallas kernels  20.4 us (15%)
    ppermute x28, waiting for transfers between devices, over_leaf(): return lax.ppermute(x, 'leaf', [(i, i ^ step) for i in range(plan.leaves)])  47.8 us
    ppermute x28, starting transfers between devices, over_leaf(): return lax.ppermute(x, 'leaf', [(i, i ^ step) for i in range(plan.leaves)])  40.2 us
    pallas_call x27, Pallas kernels, call(): pl.pallas_call(body, in_specs=specs, out_specs=[VM] * len(outs), out_shap...  20.4 us
    ppermute x18, starting transfers between devices, over_grid(): return lax.ppermute(x, 'grid', [(i, i ^ step) for i in range(plan.groups)])  12.7 us
    ppermute x10, starting transfers between devices, swap(): return lax.ppermute(x, ('leaf', 'grid'), moves)  9.81 us
    ppermute x10, waiting for transfers between devices, swap(): return lax.ppermute(x, ('leaf', 'grid'), moves)  3.11 us
    ppermute x18, waiting for transfers between devices, over_grid(): return lax.ppermute(x, 'grid', [(i, i ^ step) for i in range(plan.groups)])  3.09 us
  transfers between devices with their start and end apart: 56, of which 25 were waited for; matrix products, arithmetic and copies ran while one was open for 0% of the time, Pallas kernels for 10%

profile of v2, /device:TPU:0, one launch (start us, length us, event | category | flops | bytes accessed | tf_op | source)
XLA Modules:
  0.0 138.4 jit_solution(14397450655348636737)
XLA Ops:
  0.0 3.5 %shard_map.73 = (bf16[9,64,256]{2,1,0:T(8,128)(2,1)}, bf16[9,64,256]{2,1,0:T(8,128)(2,1)}, bf16[9,64,256]{2,1,0:T(8,128)(2,1)}, bf16[9,64,256]{2,1,0:T(8,128)(2,1)}, bf16[6,64,256]{2,1,0:T(8,128)(2,1)}) custom-call(bf16[5,2,64,256]{3,2,1,0:T(8,128)(2,1)} %refs_0_.3, bf16[5,2,64,256]{3,2,1,0:T(8,128)(2,1)} %refs_1_.3, bf16[4,2,64,512]{3,2,1,0:T(8,128)(2,1)} %refs_2_.3, ...), custom_call_target="tpu_custom_call" | custom-call | flops 1 | bytes 1048576 | tf_op jit(solution)/shard_map/pallas_call | solution.py:435
  3.5 3.0 %collective-permute-start.3 = (bf16[6,64,256]{2,1,0:T(8,128)(2,1)}, bf16[6,64,256]{2,1,0:T(8,128)(2,1)S(1)}, u32[]{:S(2)}, u32[]{:S(2)}) collective-permute-start(bf16[6,64,256]{2,1,0:T(8,128)(2,1)} %get-tuple-element.70.refs_4_), channel_id=1, source_target_pairs={{0,4},{4,0},{8,12},{12,8},{16,20},{20,16},{24,28},{28,24},{1,5},{5... | collective-permute-start | bytes 589832 | tf_op jit(solution)/shard_map/ppermute | solution.py:472
  6.5 1.5 %collective-permute-start.4 = (bf16[6,64,256]{2,1,0:T(8,128)(2,1)}, bf16[6,64,256]{2,1,0:T(8,128)(2,1)S(1)}, u32[]{:S(2)}, u32[]{:S(2)}) collective-permute-start(bf16[6,64,256]{2,1,0:T(8,128)(2,1)} %get-tuple-element.70.refs_4_), channel_id=1, source_target_pairs={{0,2},{1,3},{2,0},{3,1},{4,6},{5,7},{6,4},{7,5},{8,10},{9,11},{10,... | collective-permute-start | bytes 589832 | tf_op jit(solution)/shard_map/ppermute | solution.py:475
  8.6 2.9 %collective-permute-start.2 = (bf16[9,64,256]{2,1,0:T(8,128)(2,1)}, bf16[9,64,256]{2,1,0:T(8,128)(2,1)S(1)}, u32[]{:S(2)}, u32[]{:S(2)}) collective-permute-start(bf16[9,64,256]{2,1,0:T(8,128)(2,1)} %get-tuple-element.69), channel_id=1, source_target_pairs={{0,6},{1,7},{2,4},{3,5},{4,2},{5,3},{6,0},{7,1},{8,14},{9,15},{10,... | collective-permute-start | bytes 884744 | tf_op jit(solution)/shard_map/ppermute | solution.py:486
  16.1 12.4 %collective-permute-done.6.refs_9_ = bf16[6,64,256]{2,1,0:T(8,128)(2,1)S(1)} collective-permute-done((bf16[6,64,256]{2,1,0:T(8,128)(2,1)S(1)}, bf16[6,64,256]{2,1,0:T(8,128)(2,1)S(1)}, u32[]{:S(2)}, u32[]{:S(2)}) %collective-permute-start.6) | collective-permute-done | bytes 196640 | tf_op jit(solution)/shard_map/ppermute | solution.py:472
  31.1 1.6 %collective-permute-start.15 = (bf16[2,6,64,256]{3,2,1,0:T(8,128)(2,1)S(1)}, bf16[2,6,64,256]{3,2,1,0:T(8,128)(2,1)S(1)}, u32[]{:S(2)}, u32[]{:S(2)}) collective-permute-start(bf16[2,6,64,256]{3,2,1,0:T(8,128)(2,1)S(1)} %get-tuple-element.89.refs_1_.refs_0_), channel_id=1, source_target_pairs={{0,2},{1,3},{2,0},{3,1},{4,6},{5,7},{6,4},{7,5},{8,10},{9,11},{10,... | collective-permute-start | bytes 1179656 | tf_op jit(solution)/shard_map/ppermute | solution.py:475
  34.1 1.6 %collective-permute-start.8 = (bf16[128,256]{1,0:T(8,128)(2,1)S(1)}, bf16[128,256]{1,0:T(8,128)(2,1)S(1)}, u32[]{:S(2)}, u32[]{:S(2)}) collective-permute-start(bf16[128,256]{1,0:T(8,128)(2,1)S(1)} %get-tuple-element.79), channel_id=1, source_target_pairs={{0,8},{4,12},{8,0},{12,4},{16,24},{20,28},{24,16},{28,20},{1,9},{5... | collective-permute-start | bytes 196616 | tf_op jit(solution)/shard_map/ppermute | solution.py:472
  35.8 2.6 %collective-permute-start.9 = (bf16[128,256]{1,0:T(8,128)(2,1)S(1)}, bf16[128,256]{1,0:T(8,128)(2,1)S(1)}, u32[]{:S(2)}, u32[]{:S(2)}) collective-permute-start(bf16[128,256]{1,0:T(8,128)(2,1)S(1)} %get-tuple-element.80), channel_id=1, source_target_pairs={{0,16},{4,20},{8,24},{12,28},{16,0},{20,4},{24,8},{28,12},{1,17},{... | collective-permute-start | bytes 196616 | tf_op jit(solution)/shard_map/ppermute | solution.py:472
  39.2 4.1 %collective-permute-done.9.refs_4_ = bf16[128,256]{1,0:T(8,128)(2,1)S(1)} collective-permute-done((bf16[128,256]{1,0:T(8,128)(2,1)S(1)}, bf16[128,256]{1,0:T(8,128)(2,1)S(1)}, u32[]{:S(2)}, u32[]{:S(2)}) %collective-permute-start.9) | collective-permute-done | bytes 65568 | tf_op jit(solution)/shard_map/ppermute | solution.py:472
  45.7 1.6 %collective-permute-start.21 = (bf16[2,6,64,256]{3,2,1,0:T(8,128)(2,1)S(1)}, bf16[2,6,64,256]{3,2,1,0:T(8,128)(2,1)S(1)}, u32[]{:S(2)}, u32[]{:S(2)}) collective-permute-start(bf16[2,6,64,256]{3,2,1,0:T(8,128)(2,1)S(1)} %get-tuple-element.97.refs_0_), channel_id=1, source_target_pairs={{0,2},{1,3},{2,0},{3,1},{4,6},{5,7},{6,4},{7,5},{8,10},{9,11},{10,... | collective-permute-start | bytes 1179656 | tf_op jit(solution)/shard_map/ppermute | solution.py:475
  48.1 2.5 %collective-permute-start.13 = (bf16[128,256]{1,0:T(8,128)(2,1)S(1)}, bf16[128,256]{1,0:T(8,128)(2,1)S(1)}, u32[]{:S(2)}, u32[]{:S(2)}) collective-permute-start(bf16[128,256]{1,0:T(8,128)(2,1)S(1)} %get-tuple-element.86), channel_id=1, source_target_pairs={{0,16},{4,20},{8,24},{12,28},{16,0},{20,4},{24,8},{28,12},{1,17},{... | collective-permute-start | bytes 196616 | tf_op jit(solution)/shard_map/ppermute | solution.py:472
  52.6 3.2 %collective-permute-done.13.refs_4_ = bf16[128,256]{1,0:T(8,128)(2,1)S(1)} collective-permute-done((bf16[128,256]{1,0:T(8,128)(2,1)S(1)}, bf16[128,256]{1,0:T(8,128)(2,1)S(1)}, u32[]{:S(2)}, u32[]{:S(2)}) %collective-permute-start.13) | collective-permute-done | bytes 65568 | tf_op jit(solution)/shard_map/ppermute | solution.py:472
  59.8 2.5 %collective-permute-start.19 = (bf16[128,256]{1,0:T(8,128)(2,1)S(1)}, bf16[128,256]{1,0:T(8,128)(2,1)S(1)}, u32[]{:S(2)}, u32[]{:S(2)}) collective-permute-start(bf16[128,256]{1,0:T(8,128)(2,1)S(1)} %get-tuple-element.94), channel_id=1, source_target_pairs={{0,16},{4,20},{8,24},{12,28},{16,0},{20,4},{24,8},{28,12},{1,17},{... | collective-permute-start | bytes 196616 | tf_op jit(solution)/shard_map/ppermute | solution.py:472
  65.2 2.3 %collective-permute-done.19.refs_4_ = bf16[128,256]{1,0:T(8,128)(2,1)S(1)} collective-permute-done((bf16[128,256]{1,0:T(8,128)(2,1)S(1)}, bf16[128,256]{1,0:T(8,128)(2,1)S(1)}, u32[]{:S(2)}, u32[]{:S(2)}) %collective-permute-start.19) | collective-permute-done | bytes 65568 | tf_op jit(solution)/shard_map/ppermute | solution.py:472
  73.2 1.7 %collective-permute-done.23.refs_2_ = bf16[128,256]{1,0:T(8,128)(2,1)S(1)} collective-permute-done((bf16[128,256]{1,0:T(8,128)(2,1)S(1)}, bf16[128,256]{1,0:T(8,128)(2,1)S(1)}, u32[]{:S(2)}, u32[]{:S(2)}) %collective-permute-start.23) | collective-permute-done | bytes 65568 | tf_op jit(solution)/shard_map/ppermute | solution.py:472
  74.8 2.0 %collective-permute-start.25 = (bf16[128,256]{1,0:T(8,128)(2,1)S(1)}, bf16[128,256]{1,0:T(8,128)(2,1)S(1)}, u32[]{:S(2)}, u32[]{:S(2)}) collective-permute-start(bf16[128,256]{1,0:T(8,128)(2,1)S(1)} %get-tuple-element.102), channel_id=1, source_target_pairs={{0,24},{4,28},{8,16},{12,20},{16,8},{20,12},{24,0},{28,4},{1,25},{... | collective-permute-start | bytes 196616 | tf_op jit(solution)/shard_map/ppermute | solution.py:472
  76.9 1.5 %collective-permute-done.24.refs_3_ = bf16[128,256]{1,0:T(8,128)(2,1)S(1)} collective-permute-done((bf16[128,256]{1,0:T(8,128)(2,1)S(1)}, bf16[128,256]{1,0:T(8,128)(2,1)S(1)}, u32[]{:S(2)}, u32[]{:S(2)}) %collective-permute-start.24) | collective-permute-done | bytes 65568 | tf_op jit(solution)/shard_map/ppermute | solution.py:472
  78.4 2.5 %collective-permute-done.25.refs_4_ = bf16[128,256]{1,0:T(8,128)(2,1)S(1)} collective-permute-done((bf16[128,256]{1,0:T(8,128)(2,1)S(1)}, bf16[128,256]{1,0:T(8,128)(2,1)S(1)}, u32[]{:S(2)}, u32[]{:S(2)}) %collective-permute-start.25) | collective-permute-done | bytes 65568 | tf_op jit(solution)/shard_map/ppermute | solution.py:472
  83.5 2.4 %collective-permute-start.29 = (bf16[128,256]{1,0:T(8,128)(2,1)S(1)}, bf16[128,256]{1,0:T(8,128)(2,1)S(1)}, u32[]{:S(2)}, u32[]{:S(2)}) collective-permute-start(bf16[128,256]{1,0:T(8,128)(2,1)S(1)} %get-tuple-element.106.refs_4_.refs_1_.refs_5_.refs_9_), channel_id=1, source_target_pairs={{0,16},{4,20},{8,24},{12,28},{16,0},{20,4},{24,8},{28,12},{1,17},{... | collective-permute-start | bytes 196616 | tf_op jit(solution)/shard_map/ppermute | solution.py:472
  85.9 1.7 %collective-permute-start.30 = (bf16[128,256]{1,0:T(8,128)(2,1)S(1)}, bf16[128,256]{1,0:T(8,128)(2,1)S(1)}, u32[]{:S(2)}, u32[]{:S(2)}) collective-permute-start(bf16[128,256]{1,0:T(8,128)(2,1)S(1)} %get-tuple-element.106.refs_4_.refs_1_.refs_5_.refs_9_), channel_id=1, source_target_pairs={{0,24},{4,28},{8,16},{12,20},{16,8},{20,12},{24,0},{28,4},{1,25},{... | collective-permute-start | bytes 196616 | tf_op jit(solution)/shard_map/ppermute | solution.py:472
  88.3 3.1 %collective-permute-done.29.refs_3_.refs_7_.refs_11_ = bf16[128,256]{1,0:T(8,128)(2,1)S(1)} collective-permute-done((bf16[128,256]{1,0:T(8,128)(2,1)S(1)}, bf16[128,256]{1,0:T(8,128)(2,1)S(1)}, u32[]{:S(2)}, u32[]{:S(2)}) %collective-permute-start.29) | collective-permute-done | bytes 65568 | tf_op jit(solution)/shard_map/ppermute | solution.py:472
  95.5 2.1 %collective-permute-start.35 = (bf16[128,256]{1,0:T(8,128)(2,1)S(1)}, bf16[128,256]{1,0:T(8,128)(2,1)S(1)}, u32[]{:S(2)}, u32[]{:S(2)}) collective-permute-start(bf16[128,256]{1,0:T(8,128)(2,1)S(1)} %shard_map.90.refs_4_.refs_1_.refs_5_.refs_3_), channel_id=1, source_target_pairs={{0,16},{4,20},{8,24},{12,28},{16,0},{20,4},{24,8},{28,12},{1,17},{... | collective-permute-start | bytes 196616 | tf_op jit(solution)/shard_map/ppermute | solution.py:472
  97.6 1.7 %collective-permute-start.36 = (bf16[128,256]{1,0:T(8,128)(2,1)S(1)}, bf16[128,256]{1,0:T(8,128)(2,1)S(1)}, u32[]{:S(2)}, u32[]{:S(2)}) collective-permute-start(bf16[128,256]{1,0:T(8,128)(2,1)S(1)} %shard_map.90.refs_4_.refs_1_.refs_5_.refs_3_), channel_id=1, source_target_pairs={{0,24},{4,28},{8,16},{12,20},{16,8},{20,12},{24,0},{28,4},{1,25},{... | collective-permute-start | bytes 196616 | tf_op jit(solution)/shard_map/ppermute | solution.py:472
  99.9 4.2 %collective-permute-done.35.refs_3_.refs_7_ = bf16[128,256]{1,0:T(8,128)(2,1)S(1)} collective-permute-done((bf16[128,256]{1,0:T(8,128)(2,1)S(1)}, bf16[128,256]{1,0:T(8,128)(2,1)S(1)}, u32[]{:S(2)}, u32[]{:S(2)}) %collective-permute-start.35) | collective-permute-done | bytes 65568 | tf_op jit(solution)/shard_map/ppermute | solution.py:472
  107.5 1.8 %collective-permute-start.40 = (bf16[128,256]{1,0:T(8,128)(2,1)S(1)}, bf16[128,256]{1,0:T(8,128)(2,1)S(1)}, u32[]{:S(2)}, u32[]{:S(2)}) collective-permute-start(bf16[128,256]{1,0:T(8,128)(2,1)S(1)} %shard_map.93.refs_4_.refs_1_.refs_2_), channel_id=1, source_target_pairs={{0,16},{4,20},{8,24},{12,28},{16,0},{20,4},{24,8},{28,12},{1,17},{... | collective-permute-start | bytes 196616 | tf_op jit(solution)/shard_map/ppermute | solution.py:472
  109.3 1.7 %collective-permute-start.41 = (bf16[128,256]{1,0:T(8,128)(2,1)S(1)}, bf16[128,256]{1,0:T(8,128)(2,1)S(1)}, u32[]{:S(2)}, u32[]{:S(2)}) collective-permute-start(bf16[128,256]{1,0:T(8,128)(2,1)S(1)} %shard_map.93.refs_4_.refs_1_.refs_2_), channel_id=1, source_target_pairs={{0,24},{4,28},{8,16},{12,20},{16,8},{20,12},{24,0},{28,4},{1,25},{... | collective-permute-start | bytes 196616 | tf_op jit(solution)/shard_map/ppermute | solution.py:472
  111.9 3.9 %collective-permute-done.40.refs_3_ = bf16[128,256]{1,0:T(8,128)(2,1)S(1)} collective-permute-done((bf16[128,256]{1,0:T(8,128)(2,1)S(1)}, bf16[128,256]{1,0:T(8,128)(2,1)S(1)}, u32[]{:S(2)}, u32[]{:S(2)}) %collective-permute-start.40) | collective-permute-done | bytes 65568 | tf_op jit(solution)/shard_map/ppermute | solution.py:472
  118.2 1.6 %collective-permute-start.45 = (bf16[128,256]{1,0:T(8,128)(2,1)S(1)}, bf16[128,256]{1,0:T(8,128)(2,1)S(1)}, u32[]{:S(2)}, u32[]{:S(2)}) collective-permute-start(bf16[128,256]{1,0:T(8,128)(2,1)S(1)} %shard_map.96.refs_2_.refs_1_), channel_id=1, source_target_pairs={{0,16},{4,20},{8,24},{12,28},{16,0},{20,4},{24,8},{28,12},{1,17},{... | collective-permute-start | bytes 196616 | tf_op jit(solution)/shard_map/ppermute | solution.py:472
  119.9 1.7 %collective-permute-start.46 = (bf16[128,256]{1,0:T(8,128)(2,1)S(1)}, bf16[128,256]{1,0:T(8,128)(2,1)S(1)}, u32[]{:S(2)}, u32[]{:S(2)}) collective-permute-start(bf16[128,256]{1,0:T(8,128)(2,1)S(1)} %shard_map.96.refs_2_.refs_1_), channel_id=1, source_target_pairs={{0,24},{4,28},{8,16},{12,20},{16,8},{20,12},{24,0},{28,4},{1,25},{... | collective-permute-start | bytes 196616 | tf_op jit(solution)/shard_map/ppermute | solution.py:472
  122.5 4.2 %collective-permute-done.45.refs_3_ = bf16[128,256]{1,0:T(8,128)(2,1)S(1)} collective-permute-done((bf16[128,256]{1,0:T(8,128)(2,1)S(1)}, bf16[128,256]{1,0:T(8,128)(2,1)S(1)}, u32[]{:S(2)}, u32[]{:S(2)}) %collective-permute-start.45) | collective-permute-done | bytes 65568 | tf_op jit(solution)/shard_map/ppermute | solution.py:472
  132.5 1.8 %collective-permute-start.55 = (bf16[3,64,128]{2,1,0:T(8,128)(2,1)S(1)}, bf16[3,64,128]{2,1,0:T(8,128)(2,1)S(1)}, u32[]{:S(2)}, u32[]{:S(2)}) collective-permute-start(bf16[3,64,128]{2,1,0:T(8,128)(2,1)S(1)} %get-tuple-element.126), channel_id=1, source_target_pairs={{0,7},{1,6},{2,5},{3,4},{4,3},{5,2},{6,1},{7,0},{8,15},{9,14},{10,... | collective-permute-start | bytes 147464 | tf_op jit(solution)/shard_map/ppermute | solution.py:486
  134.4 2.3 %collective-permute-done.54.refs_6_ = bf16[3,64,128]{2,1,0:T(8,128)(2,1)S(1)} collective-permute-done((bf16[3,64,128]{2,1,0:T(8,128)(2,1)S(1)}, bf16[3,64,128]{2,1,0:T(8,128)(2,1)S(1)}, u32[]{:S(2)}, u32[]{:S(2)}) %collective-permute-start.54) | collective-permute-done | bytes 49184 | tf_op jit(solution)/shard_map/ppermute | solution.py:486
  (121 shorter events, 51.0 us)
Async XLA Ops:
  3.5 10.2 %collective-permute-start.3 = (bf16[6,64,256]{2,1,0:T(8,128)(2,1)}, bf16[6,64,256]{2,1,0:T(8,128)(2,1)S(1)}, u32[]{:S(2)}, u32[]{:S(2)}) collective-permute-start(bf16[6,64,256]{2,1,0:T(8,128)(2,1)} %get-tuple-element.70.refs_4_), channel_id=1, source_target_pairs={{0,4},{4,0},{8,12},{12,8},{16,20},{20,16},{24,28},{28,24},{1,5},{5... | collective-permute-start | bytes 589832 | tf_op jit(solution)/shard_map/ppermute | solution.py:472
  6.5 8.0 %collective-permute-start.4 = (bf16[6,64,256]{2,1,0:T(8,128)(2,1)}, bf16[6,64,256]{2,1,0:T(8,128)(2,1)S(1)}, u32[]{:S(2)}, u32[]{:S(2)}) collective-permute-start(bf16[6,64,256]{2,1,0:T(8,128)(2,1)} %get-tuple-element.70.refs_4_), channel_id=1, source_target_pairs={{0,2},{1,3},{2,0},{3,1},{4,6},{5,7},{6,4},{7,5},{8,10},{9,11},{10,... | collective-permute-start | bytes 589832 | tf_op jit(solution)/shard_map/ppermute | solution.py:475
  8.0 20.5 %collective-permute-start = (bf16[9,64,256]{2,1,0:T(8,128)(2,1)}, bf16[9,64,256]{2,1,0:T(8,128)(2,1)S(1)}, u32[]{:S(2)}, u32[]{:S(2)}) collective-permute-start(bf16[9,64,256]{2,1,0:T(8,128)(2,1)} %get-tuple-element.67), channel_id=1, source_target_pairs={{0,4},{1,5},{2,6},{3,7},{4,0},{5,1},{6,2},{7,3},{8,12},{9,13},{10,... | collective-permute-start | bytes 884744 | tf_op jit(solution)/shard_map/ppermute | solution.py:486
  8.5 20.0 %collective-permute-start.1 = (bf16[9,64,256]{2,1,0:T(8,128)(2,1)}, bf16[9,64,256]{2,1,0:T(8,128)(2,1)S(1)}, u32[]{:S(2)}, u32[]{:S(2)}) collective-permute-start(bf16[9,64,256]{2,1,0:T(8,128)(2,1)} %get-tuple-element.68), channel_id=1, source_target_pairs={{0,2},{1,3},{2,0},{3,1},{4,6},{5,7},{6,4},{7,5},{8,10},{9,11},{10,... | collective-permute-start | bytes 884744 | tf_op jit(solution)/shard_map/ppermute | solution.py:486
  8.6 19.9 %collective-permute-start.2 = (bf16[9,64,256]{2,1,0:T(8,128)(2,1)}, bf16[9,64,256]{2,1,0:T(8,128)(2,1)S(1)}, u32[]{:S(2)}, u32[]{:S(2)}) collective-permute-start(bf16[9,64,256]{2,1,0:T(8,128)(2,1)} %get-tuple-element.69), channel_id=1, source_target_pairs={{0,6},{1,7},{2,4},{3,5},{4,2},{5,3},{6,0},{7,1},{8,14},{9,15},{10,... | collective-permute-start | bytes 884744 | tf_op jit(solution)/shard_map/ppermute | solution.py:486
  13.7 14.8 %collective-permute-start.6 = (bf16[6,64,256]{2,1,0:T(8,128)(2,1)S(1)}, bf16[6,64,256]{2,1,0:T(8,128)(2,1)S(1)}, u32[]{:S(2)}, u32[]{:S(2)}) collective-permute-start(bf16[6,64,256]{2,1,0:T(8,128)(2,1)S(1)} %get-tuple-element.71.refs_8_), channel_id=1, source_target_pairs={{0,4},{4,0},{8,12},{12,8},{16,20},{20,16},{24,28},{28,24},{1,5},{5... | collective-permute-start | bytes 589832 | tf_op jit(solution)/shard_map/ppermute | solution.py:472
  14.6 15.4 %collective-permute-start.5 = (bf16[6,64,256]{2,1,0:T(8,128)(2,1)S(1)}, bf16[6,64,256]{2,1,0:T(8,128)(2,1)S(1)}, u32[]{:S(2)}, u32[]{:S(2)}) collective-permute-start(bf16[6,64,256]{2,1,0:T(8,128)(2,1)S(1)} %collective-permute-done.3.refs_5_), channel_id=1, source_target_pairs={{0,2},{1,3},{2,0},{3,1},{4,6},{5,7},{6,4},{7,5},{8,10},{9,11},{10,... | collective-permute-start | bytes 589832 | tf_op jit(solution)/shard_map/ppermute | solution.py:475
  30.3 8.1 %collective-permute-start.11 = (bf16[2,2,6,64,256]{4,3,2,1,0:T(8,128)(2,1)S(1)}, bf16[2,2,6,64,256]{4,3,2,1,0:T(8,128)(2,1)S(1)}, u32[]{:S(2)}, u32[]{:S(2)}) collective-permute-start(bf16[2,2,6,64,256]{4,3,2,1,0:T(8,128)(2,1)S(1)} %get-tuple-element.83.refs_7_), channel_id=1, source_target_pairs={{0,1},{1,0},{2,3},{3,2},{4,5},{5,4},{6,7},{7,6},{8,9},{9,8},{10,11... | collective-permute-start | bytes 2359304 | tf_op jit(solution)/shard_map/ppermute | solution.py:475
  30.7 14.7 %collective-permute-start.16 = (bf16[16,64,256]{2,1,0:T(8,128)(2,1)S(1)}, bf16[16,64,256]{2,1,0:T(8,128)(2,1)S(1)}, u32[]{:S(2)}, u32[]{:S(2)}) collective-permute-start(bf16[16,64,256]{2,1,0:T(8,128)(2,1)S(1)} %shard_map.80.refs_2_), channel_id=1, source_target_pairs={{0,4},{4,0},{8,12},{12,8},{16,20},{20,16},{24,28},{28,24},{1,5},{5... | collective-permute-start | bytes 1572872 | tf_op jit(solution)/shard_map/ppermute | solution.py:472
  31.1 14.4 %collective-permute-start.15 = (bf16[2,6,64,256]{3,2,1,0:T(8,128)(2,1)S(1)}, bf16[2,6,64,256]{3,2,1,0:T(8,128)(2,1)S(1)}, u32[]{:S(2)}, u32[]{:S(2)}) collective-permute-start(bf16[2,6,64,256]{3,2,1,0:T(8,128)(2,1)S(1)} %get-tuple-element.89.refs_1_.refs_0_), channel_id=1, source_target_pairs={{0,2},{1,3},{2,0},{3,1},{4,6},{5,7},{6,4},{7,5},{8,10},{9,11},{10,... | collective-permute-start | bytes 1179656 | tf_op jit(solution)/shard_map/ppermute | solution.py:475
  35.8 7.5 %collective-permute-start.9 = (bf16[128,256]{1,0:T(8,128)(2,1)S(1)}, bf16[128,256]{1,0:T(8,128)(2,1)S(1)}, u32[]{:S(2)}, u32[]{:S(2)}) collective-permute-start(bf16[128,256]{1,0:T(8,128)(2,1)S(1)} %get-tuple-element.80), channel_id=1, source_target_pairs={{0,16},{4,20},{8,24},{12,28},{16,0},{20,4},{24,8},{28,12},{1,17},{... | collective-permute-start | bytes 196616 | tf_op jit(solution)/shard_map/ppermute | solution.py:472
  45.6 11.1 %collective-permute-start.17 = (bf16[2,2,6,64,256]{4,3,2,1,0:T(8,128)(2,1)S(1)}, bf16[2,2,6,64,256]{4,3,2,1,0:T(8,128)(2,1)S(1)}, u32[]{:S(2)}, u32[]{:S(2)}) collective-permute-start(bf16[2,2,6,64,256]{4,3,2,1,0:T(8,128)(2,1)S(1)} %get-tuple-element.91.refs_7_), channel_id=1, source_target_pairs={{0,1},{1,0},{2,3},{3,2},{4,5},{5,4},{6,7},{7,6},{8,9},{9,8},{10,11... | collective-permute-start | bytes 2359304 | tf_op jit(solution)/shard_map/ppermute | solution.py:475
  45.7 12.0 %collective-permute-start.21 = (bf16[2,6,64,256]{3,2,1,0:T(8,128)(2,1)S(1)}, bf16[2,6,64,256]{3,2,1,0:T(8,128)(2,1)S(1)}, u32[]{:S(2)}, u32[]{:S(2)}) collective-permute-start(bf16[2,6,64,256]{3,2,1,0:T(8,128)(2,1)S(1)} %get-tuple-element.97.refs_0_), channel_id=1, source_target_pairs={{0,2},{1,3},{2,0},{3,1},{4,6},{5,7},{6,4},{7,5},{8,10},{9,11},{10,... | collective-permute-start | bytes 1179656 | tf_op jit(solution)/shard_map/ppermute | solution.py:475
  48.1 7.7 %collective-permute-start.13 = (bf16[128,256]{1,0:T(8,128)(2,1)S(1)}, bf16[128,256]{1,0:T(8,128)(2,1)S(1)}, u32[]{:S(2)}, u32[]{:S(2)}) collective-permute-start(bf16[128,256]{1,0:T(8,128)(2,1)S(1)} %get-tuple-element.86), channel_id=1, source_target_pairs={{0,16},{4,20},{8,24},{12,28},{16,0},{20,4},{24,8},{28,12},{1,17},{... | collective-permute-start | bytes 196616 | tf_op jit(solution)/shard_map/ppermute | solution.py:472
  57.8 10.6 %collective-permute-start.22 = (bf16[2,2,6,64,256]{4,3,2,1,0:T(8,128)(2,1)S(1)}, bf16[2,2,6,64,256]{4,3,2,1,0:T(8,128)(2,1)S(1)}, u32[]{:S(2)}, u32[]{:S(2)}) collective-permute-start(bf16[2,2,6,64,256]{4,3,2,1,0:T(8,128)(2,1)S(1)} %get-tuple-element.98.refs_7_), channel_id=1, source_target_pairs={{0,1},{1,0},{2,3},{3,2},{4,5},{5,4},{6,7},{7,6},{8,9},{9,8},{10,11... | collective-permute-start | bytes 2359304 | tf_op jit(solution)/shard_map/ppermute | solution.py:475
  57.9 11.5 %collective-permute-start.26 = (bf16[2,4,64,256]{3,2,1,0:T(8,128)(2,1)S(1)}, bf16[2,4,64,256]{3,2,1,0:T(8,128)(2,1)S(1)}, u32[]{:S(2)}, u32[]{:S(2)}) collective-permute-start(bf16[2,4,64,256]{3,2,1,0:T(8,128)(2,1)S(1)} %get-tuple-element.103.refs_0_), channel_id=1, source_target_pairs={{0,2},{1,3},{2,0},{3,1},{4,6},{5,7},{6,4},{7,5},{8,10},{9,11},{10,... | collective-permute-start | bytes 786440 | tf_op jit(solution)/shard_map/ppermute | solution.py:475
  59.8 7.7 %collective-permute-start.19 = (bf16[128,256]{1,0:T(8,128)(2,1)S(1)}, bf16[128,256]{1,0:T(8,128)(2,1)S(1)}, u32[]{:S(2)}, u32[]{:S(2)}) collective-permute-start(bf16[128,256]{1,0:T(8,128)(2,1)S(1)} %get-tuple-element.94), channel_id=1, source_target_pairs={{0,16},{4,20},{8,24},{12,28},{16,0},{20,4},{24,8},{28,12},{1,17},{... | collective-permute-start | bytes 196616 | tf_op jit(solution)/shard_map/ppermute | solution.py:472
  63.3 18.5 %collective-permute-start.32 = (bf16[18,64,256]{2,1,0:T(8,128)(2,1)S(1)}, bf16[18,64,256]{2,1,0:T(8,128)(2,1)S(1)}, u32[]{:S(2)}, u32[]{:S(2)}) collective-permute-start(bf16[18,64,256]{2,1,0:T(8,128)(2,1)S(1)} %shard_map.88.refs_2_), channel_id=1, source_target_pairs={{0,4},{4,0},{8,12},{12,8},{16,20},{20,16},{24,28},{28,24},{1,5},{5... | collective-permute-start | bytes 1769480 | tf_op jit(solution)/shard_map/ppermute | solution.py:472
  69.5 11.4 %collective-permute-start.27 = (bf16[2,2,4,64,256]{4,3,2,1,0:T(8,128)(2,1)S(1)}, bf16[2,2,4,64,256]{4,3,2,1,0:T(8,128)(2,1)S(1)}, u32[]{:S(2)}, u32[]{:S(2)}) collective-permute-start(bf16[2,2,4,64,256]{4,3,2,1,0:T(8,128)(2,1)S(1)} %get-tuple-element.105.refs_5_), channel_id=1, source_target_pairs={{0,1},{1,0},{2,3},{3,2},{4,5},{5,4},{6,7},{7,6},{8,9},{9,8},{10,11... | collective-permute-start | bytes 1572872 | tf_op jit(solution)/shard_map/ppermute | solution.py:475
  69.6 12.3 %collective-permute-start.31 = (bf16[2,6,64,256]{3,2,1,0:T(8,128)(2,1)S(1)}, bf16[2,6,64,256]{3,2,1,0:T(8,128)(2,1)S(1)}, u32[]{:S(2)}, u32[]{:S(2)}) collective-permute-start(bf16[2,6,64,256]{3,2,1,0:T(8,128)(2,1)S(1)} %get-tuple-element.108.refs_0_), channel_id=1, source_target_pairs={{0,2},{1,3},{2,0},{3,1},{4,6},{5,7},{6,4},{7,5},{8,10},{9,11},{10,... | collective-permute-start | bytes 1179656 | tf_op jit(solution)/shard_map/ppermute | solution.py:475
  82.0 10.1 %collective-permute-start.33 = (bf16[2,2,6,64,256]{4,3,2,1,0:T(8,128)(2,1)S(1)}, bf16[2,2,6,64,256]{4,3,2,1,0:T(8,128)(2,1)S(1)}, u32[]{:S(2)}, u32[]{:S(2)}) collective-permute-start(bf16[2,2,6,64,256]{4,3,2,1,0:T(8,128)(2,1)S(1)} %get-tuple-element.110.refs_6_), channel_id=1, source_target_pairs={{0,1},{1,0},{2,3},{3,2},{4,5},{5,4},{6,7},{7,6},{8,9},{9,8},{10,11... | collective-permute-start | bytes 2359304 | tf_op jit(solution)/shard_map/ppermute | solution.py:475
  82.1 11.5 %collective-permute-start.37 = (bf16[2,6,64,256]{3,2,1,0:T(8,128)(2,1)S(1)}, bf16[2,6,64,256]{3,2,1,0:T(8,128)(2,1)S(1)}, u32[]{:S(2)}, u32[]{:S(2)}) collective-permute-start(bf16[2,6,64,256]{3,2,1,0:T(8,128)(2,1)S(1)} %get-tuple-element.112.refs_0_), channel_id=1, source_target_pairs={{0,2},{1,3},{2,0},{3,1},{4,6},{5,7},{6,4},{7,5},{8,10},{9,11},{10,... | collective-permute-start | bytes 1179656 | tf_op jit(solution)/shard_map/ppermute | solution.py:475
  83.5 7.8 %collective-permute-start.29 = (bf16[128,256]{1,0:T(8,128)(2,1)S(1)}, bf16[128,256]{1,0:T(8,128)(2,1)S(1)}, u32[]{:S(2)}, u32[]{:S(2)}) collective-permute-start(bf16[128,256]{1,0:T(8,128)(2,1)S(1)} %get-tuple-element.106.refs_4_.refs_1_.refs_5_.refs_9_), channel_id=1, source_target_pairs={{0,16},{4,20},{8,24},{12,28},{16,0},{20,4},{24,8},{28,12},{1,17},{... | collective-permute-start | bytes 196616 | tf_op jit(solution)/shard_map/ppermute | solution.py:472
  93.7 10.3 %collective-permute-start.38 = (bf16[2,2,6,64,256]{4,3,2,1,0:T(8,128)(2,1)S(1)}, bf16[2,2,6,64,256]{4,3,2,1,0:T(8,128)(2,1)S(1)}, u32[]{:S(2)}, u32[]{:S(2)}) collective-permute-start(bf16[2,2,6,64,256]{4,3,2,1,0:T(8,128)(2,1)S(1)} %get-tuple-element.113.refs_7_), channel_id=1, source_target_pairs={{0,1},{1,0},{2,3},{3,2},{4,5},{5,4},{6,7},{7,6},{8,9},{9,8},{10,11... | collective-permute-start | bytes 2359304 | tf_op jit(solution)/shard_map/ppermute | solution.py:475
  93.8 11.5 %collective-permute-start.42 = (bf16[2,6,64,256]{3,2,1,0:T(8,128)(2,1)S(1)}, bf16[2,6,64,256]{3,2,1,0:T(8,128)(2,1)S(1)}, u32[]{:S(2)}, u32[]{:S(2)}) collective-permute-start(bf16[2,6,64,256]{3,2,1,0:T(8,128)(2,1)S(1)} %get-tuple-element.115.refs_0_), channel_id=1, source_target_pairs={{0,2},{1,3},{2,0},{3,1},{4,6},{5,7},{6,4},{7,5},{8,10},{9,11},{10,... | collective-permute-start | bytes 1179656 | tf_op jit(solution)/shard_map/ppermute | solution.py:475
  95.5 8.5 %collective-permute-start.35 = (bf16[128,256]{1,0:T(8,128)(2,1)S(1)}, bf16[128,256]{1,0:T(8,128)(2,1)S(1)}, u32[]{:S(2)}, u32[]{:S(2)}) collective-permute-start(bf16[128,256]{1,0:T(8,128)(2,1)S(1)} %shard_map.90.refs_4_.refs_1_.refs_5_.refs_3_), channel_id=1, source_target_pairs={{0,16},{4,20},{8,24},{12,28},{16,0},{20,4},{24,8},{28,12},{1,17},{... | collective-permute-start | bytes 196616 | tf_op jit(solution)/shard_map/ppermute | solution.py:472
  105.4 10.4 %collective-permute-start.43 = (bf16[2,2,6,64,256]{4,3,2,1,0:T(8,128)(2,1)S(1)}, bf16[2,2,6,64,256]{4,3,2,1,0:T(8,128)(2,1)S(1)}, u32[]{:S(2)}, u32[]{:S(2)}) collective-permute-start(bf16[2,2,6,64,256]{4,3,2,1,0:T(8,128)(2,1)S(1)} %get-tuple-element.116.refs_7_), channel_id=1, source_target_pairs={{0,1},{1,0},{2,3},{3,2},{4,5},{5,4},{6,7},{7,6},{8,9},{9,8},{10,11... | collective-permute-start | bytes 2359304 | tf_op jit(solution)/shard_map/ppermute | solution.py:475
  105.5 11.5 %collective-permute-start.47 = (bf16[2,6,64,256]{3,2,1,0:T(8,128)(2,1)S(1)}, bf16[2,6,64,256]{3,2,1,0:T(8,128)(2,1)S(1)}, u32[]{:S(2)}, u32[]{:S(2)}) collective-permute-start(bf16[2,6,64,256]{3,2,1,0:T(8,128)(2,1)S(1)} %get-tuple-element.118.refs_0_), channel_id=1, source_target_pairs={{0,2},{1,3},{2,0},{3,1},{4,6},{5,7},{6,4},{7,5},{8,10},{9,11},{10,... | collective-permute-start | bytes 1179656 | tf_op jit(solution)/shard_map/ppermute | solution.py:475
  107.5 8.3 %collective-permute-start.40 = (bf16[128,256]{1,0:T(8,128)(2,1)S(1)}, bf16[128,256]{1,0:T(8,128)(2,1)S(1)}, u32[]{:S(2)}, u32[]{:S(2)}) collective-permute-start(bf16[128,256]{1,0:T(8,128)(2,1)S(1)} %shard_map.93.refs_4_.refs_1_.refs_2_), channel_id=1, source_target_pairs={{0,16},{4,20},{8,24},{12,28},{16,0},{20,4},{24,8},{28,12},{1,17},{... | collective-permute-start | bytes 196616 | tf_op jit(solution)/shard_map/ppermute | solution.py:472
  117.1 9.6 %collective-permute-start.48 = (bf16[2,2,6,64,256]{4,3,2,1,0:T(8,128)(2,1)S(1)}, bf16[2,2,6,64,256]{4,3,2,1,0:T(8,128)(2,1)S(1)}, u32[]{:S(2)}, u32[]{:S(2)}) collective-permute-start(bf16[2,2,6,64,256]{4,3,2,1,0:T(8,128)(2,1)S(1)} %shard_map.98.refs_7_), channel_id=1, source_target_pairs={{0,1},{1,0},{2,3},{3,2},{4,5},{5,4},{6,7},{7,6},{8,9},{9,8},{10,11... | collective-permute-start | bytes 2359304 | tf_op jit(solution)/shard_map/ppermute | solution.py:475
  118.2 8.5 %collective-permute-start.45 = (bf16[128,256]{1,0:T(8,128)(2,1)S(1)}, bf16[128,256]{1,0:T(8,128)(2,1)S(1)}, u32[]{:S(2)}, u32[]{:S(2)}) collective-permute-start(bf16[128,256]{1,0:T(8,128)(2,1)S(1)} %shard_map.96.refs_2_.refs_1_), channel_id=1, source_target_pairs={{0,16},{4,20},{8,24},{12,28},{16,0},{20,4},{24,8},{28,12},{1,17},{... | collective-permute-start | bytes 196616 | tf_op jit(solution)/shard_map/ppermute | solution.py:472
  119.9 6.8 %collective-permute-start.46 = (bf16[128,256]{1,0:T(8,128)(2,1)S(1)}, bf16[128,256]{1,0:T(8,128)(2,1)S(1)}, u32[]{:S(2)}, u32[]{:S(2)}) collective-permute-start(bf16[128,256]{1,0:T(8,128)(2,1)S(1)} %shard_map.96.refs_2_.refs_1_), channel_id=1, source_target_pairs={{0,24},{4,28},{8,16},{12,20},{16,8},{20,12},{24,0},{28,4},{1,25},{... | collective-permute-start | bytes 196616 | tf_op jit(solution)/shard_map/ppermute | solution.py:472
  (30 other events, 189.5 us)

commit v3 on v2

--- a/solution.py
+++ b/solution.py
@@ -443,7 +443,7 @@
     )(*args)
 
 
-def gate(x, *others):
+def gate(x, *others, flops=0):
     return pl.pallas_call(
         gate_kernel,
         in_specs=[UNREAD] * (1 + len(others)),
@@ -451,7 +451,7 @@
         out_shape=jax.ShapeDtypeStruct(x.shape, x.dtype),
         input_output_aliases={0: 0},
         compiler_params=pltpu.CompilerParams(vmem_limit_bytes=2**20),
-        cost_estimate=pl.CostEstimate(flops=0, bytes_accessed=0, transcendentals=0),
+        cost_estimate=pl.CostEstimate(flops=flops, bytes_accessed=0, transcendentals=0),
     )(x, *others)
 
 
@@ -637,11 +637,13 @@
         arrived = from_owners(got[2 : 2 + owners])
         advance(level, got[1])
         more = None
+        if level + 1 == top:
+            starts[top] = gate(starts[top], got[1], flops=100 * one_pass)
         if level + 1 < top:
             (more,) = call(
                 functools.partial(ahead_kernel, plan, level + 1),
                 sent + [keys], [VM] * (len(sent) + 1), [((owners,) + plan.slab, F32)], [],
-                one_pass * len(sent), 16 * slab_bytes,
+                100 * one_pass * len(sent), 16 * slab_bytes,
             )
 
     solutions = {top: solved}
@@ -651,13 +653,15 @@
         everywhere[level + 1] = from_owners([above] * owners)
         froms = list(range(level + 2, levels))
         known = []
+        if not froms:
+            forward_out[level] = gate(forward_out[level], above, flops=100 * one_pass)
         if froms:
             slabs = sum([everywhere[f] for f in froms], [])
             known = call(
                 functools.partial(known_kernel, plan, level, froms),
                 [keys] + slabs, [VM] * (1 + len(slabs)),
                 [((plan.groups, plan.chunk, plan.sources), BF)], [],
-                one_pass * len(froms), 16 * slab_bytes,
+                100 * one_pass * len(froms), 16 * slab_bytes,
             )
         advance(levels + top - level - 2, above)
         blocks, part_of = matrices(level, ["upper", "inv"])

time: 139 us -> 133 us (0.957)
  waiting for transfers between devices: 54 us -> 46.1 us
  starting transfers between devices: 62.7 us -> 64.5 us
    ppermute x28, waiting for transfers between devices: 47.8 us -> 23.5 us  [over_leaf(): return lax.ppermute(x, 'leaf', [(i, i ^ step) for i in range(plan.leaves)])]
    ppermute x18, waiting for transfers between devices: 3.09 us -> 18.7 us  [over_grid(): return lax.ppermute(x, 'grid', [(i, i ^ step) for i in range(plan.groups)])]
    ppermute x18, starting transfers between devices: 12.7 us -> 14.5 us  [over_grid(): return lax.ppermute(x, 'grid', [(i, i ^ step) for i in range(plan.groups)])]
  transfers between devices with their start and end apart: 56 -> 56, of which waited for: 25 -> 22; matrix products, arithmetic and copies ran while one was open for 0% -> 0% of each run, Pallas kernels for 10% -> 11%
where the time goes in v3:
time: 133 us; the launch traced here: 132 us
  starting transfers between devices  64.5 us (48%)
  waiting for transfers between devices  46.1 us (35%)
  Pallas kernels  20.4 us (15%)
    ppermute x28, starting transfers between devices, over_leaf(): return lax.ppermute(x, 'leaf', [(i, i ^ step) for i in range(plan.leaves)])  40.2 us
    ppermute x28, waiting for transfers between devices, over_leaf(): return lax.ppermute(x, 'leaf', [(i, i ^ step) for i in range(plan.leaves)])  23.5 us
    pallas_call x27, Pallas kernels, call(): pl.pallas_call(body, in_specs=specs, out_specs=[VM] * len(outs), out_shap...  20.4 us
    ppermute x18, waiting for transfers between devices, over_grid(): return lax.ppermute(x, 'grid', [(i, i ^ step) for i in range(plan.groups)])  18.7 us
    ppermute x18, starting transfers between devices, over_grid(): return lax.ppermute(x, 'grid', [(i, i ^ step) for i in range(plan.groups)])  14.5 us
    ppermute x10, starting transfers between devices, swap(): return lax.ppermute(x, ('leaf', 'grid'), moves)  9.81 us
    ppermute x10, waiting for transfers between devices, swap(): return lax.ppermute(x, ('leaf', 'grid'), moves)  3.92 us
  transfers between devices with their start and end apart: 56, of which 22 were waited for; matrix products, arithmetic and copies ran while one was open for 0% of the time, Pallas kernels for 11%

profile of v3, /device:TPU:0, one launch (start us, length us, event | category | flops | bytes accessed | tf_op | source)
XLA Modules:
  0.0 132.4 jit_solution(17947689779846901172)
XLA Ops:
  0.0 3.5 %shard_map.73 = (bf16[9,64,256]{2,1,0:T(8,128)(2,1)}, bf16[9,64,256]{2,1,0:T(8,128)(2,1)}, bf16[9,64,256]{2,1,0:T(8,128)(2,1)}, bf16[9,64,256]{2,1,0:T(8,128)(2,1)}, bf16[6,64,256]{2,1,0:T(8,128)(2,1)}) custom-call(bf16[5,2,64,256]{3,2,1,0:T(8,128)(2,1)} %refs_0_.3, bf16[5,2,64,256]{3,2,1,0:T(8,128)(2,1)} %refs_1_.3, bf16[4,2,64,512]{3,2,1,0:T(8,128)(2,1)} %refs_2_.3, ...), custom_call_target="tpu_custom_call" | custom-call | flops 1 | bytes 1048576 | tf_op jit(solution)/shard_map/pallas_call | solution.py:435
  3.5 3.0 %collective-permute-start.3 = (bf16[6,64,256]{2,1,0:T(8,128)(2,1)}, bf16[6,64,256]{2,1,0:T(8,128)(2,1)S(1)}, u32[]{:S(2)}, u32[]{:S(2)}) collective-permute-start(bf16[6,64,256]{2,1,0:T(8,128)(2,1)} %get-tuple-element.70.refs_4_), channel_id=1, source_target_pairs={{0,4},{4,0},{8,12},{12,8},{16,20},{20,16},{24,28},{28,24},{1,5},{5... | collective-permute-start | bytes 589832 | tf_op jit(solution)/shard_map/ppermute | solution.py:472
  8.6 2.9 %collective-permute-start.2 = (bf16[9,64,256]{2,1,0:T(8,128)(2,1)}, bf16[9,64,256]{2,1,0:T(8,128)(2,1)S(1)}, u32[]{:S(2)}, u32[]{:S(2)}) collective-permute-start(bf16[9,64,256]{2,1,0:T(8,128)(2,1)} %get-tuple-element.69), channel_id=1, source_target_pairs={{0,6},{1,7},{2,4},{3,5},{4,2},{5,3},{6,0},{7,1},{8,14},{9,15},{10,... | collective-permute-start | bytes 884744 | tf_op jit(solution)/shard_map/ppermute | solution.py:486
  16.1 12.4 %collective-permute-done.6.refs_9_ = bf16[6,64,256]{2,1,0:T(8,128)(2,1)S(1)} collective-permute-done((bf16[6,64,256]{2,1,0:T(8,128)(2,1)S(1)}, bf16[6,64,256]{2,1,0:T(8,128)(2,1)S(1)}, u32[]{:S(2)}, u32[]{:S(2)}) %collective-permute-start.6) | collective-permute-done | bytes 196640 | tf_op jit(solution)/shard_map/ppermute | solution.py:472
  30.7 1.5 %collective-permute-start.15 = (bf16[2,6,64,256]{3,2,1,0:T(8,128)(2,1)S(1)}, bf16[2,6,64,256]{3,2,1,0:T(8,128)(2,1)S(1)}, u32[]{:S(2)}, u32[]{:S(2)}) collective-permute-start(bf16[2,6,64,256]{3,2,1,0:T(8,128)(2,1)S(1)} %get-tuple-element.89.refs_1_.refs_0_), channel_id=1, source_target_pairs={{0,2},{1,3},{2,0},{3,1},{4,6},{5,7},{6,4},{7,5},{8,10},{9,11},{10,... | collective-permute-start | bytes 1179656 | tf_op jit(solution)/shard_map/ppermute | solution.py:475
  34.1 1.6 %collective-permute-start.8 = (bf16[128,256]{1,0:T(8,128)(2,1)S(1)}, bf16[128,256]{1,0:T(8,128)(2,1)S(1)}, u32[]{:S(2)}, u32[]{:S(2)}) collective-permute-start(bf16[128,256]{1,0:T(8,128)(2,1)S(1)} %get-tuple-element.79), channel_id=1, source_target_pairs={{0,8},{4,12},{8,0},{12,4},{16,24},{20,28},{24,16},{28,20},{1,9},{5... | collective-permute-start | bytes 196616 | tf_op jit(solution)/shard_map/ppermute | solution.py:472
  35.8 2.6 %collective-permute-start.9 = (bf16[128,256]{1,0:T(8,128)(2,1)S(1)}, bf16[128,256]{1,0:T(8,128)(2,1)S(1)}, u32[]{:S(2)}, u32[]{:S(2)}) collective-permute-start(bf16[128,256]{1,0:T(8,128)(2,1)S(1)} %get-tuple-element.80), channel_id=1, source_target_pairs={{0,16},{4,20},{8,24},{12,28},{16,0},{20,4},{24,8},{28,12},{1,17},{... | collective-permute-start | bytes 196616 | tf_op jit(solution)/shard_map/ppermute | solution.py:472
  39.2 4.1 %collective-permute-done.9.refs_4_ = bf16[128,256]{1,0:T(8,128)(2,1)S(1)} collective-permute-done((bf16[128,256]{1,0:T(8,128)(2,1)S(1)}, bf16[128,256]{1,0:T(8,128)(2,1)S(1)}, u32[]{:S(2)}, u32[]{:S(2)}) %collective-permute-start.9) | collective-permute-done | bytes 65568 | tf_op jit(solution)/shard_map/ppermute | solution.py:472
  46.4 1.7 %collective-permute-start.13 = (bf16[128,256]{1,0:T(8,128)(2,1)S(1)}, bf16[128,256]{1,0:T(8,128)(2,1)S(1)}, u32[]{:S(2)}, u32[]{:S(2)}) collective-permute-start(bf16[128,256]{1,0:T(8,128)(2,1)S(1)} %get-tuple-element.86), channel_id=1, source_target_pairs={{0,16},{4,20},{8,24},{12,28},{16,0},{20,4},{24,8},{28,12},{1,17},{... | collective-permute-start | bytes 196616 | tf_op jit(solution)/shard_map/ppermute | solution.py:472
  48.1 1.8 %collective-permute-start.14 = (bf16[128,256]{1,0:T(8,128)(2,1)S(1)}, bf16[128,256]{1,0:T(8,128)(2,1)S(1)}, u32[]{:S(2)}, u32[]{:S(2)}) collective-permute-start(bf16[128,256]{1,0:T(8,128)(2,1)S(1)} %get-tuple-element.87), channel_id=1, source_target_pairs={{0,24},{4,28},{8,16},{12,20},{16,8},{20,12},{24,0},{28,4},{1,25},{... | collective-permute-start | bytes 196616 | tf_op jit(solution)/shard_map/ppermute | solution.py:472
  50.1 1.6 %collective-permute-start.21 = (bf16[2,6,64,256]{3,2,1,0:T(8,128)(2,1)S(1)}, bf16[2,6,64,256]{3,2,1,0:T(8,128)(2,1)S(1)}, u32[]{:S(2)}, u32[]{:S(2)}) collective-permute-start(bf16[2,6,64,256]{3,2,1,0:T(8,128)(2,1)S(1)} %get-tuple-element.97.refs_0_), channel_id=1, source_target_pairs={{0,2},{1,3},{2,0},{3,1},{4,6},{5,7},{6,4},{7,5},{8,10},{9,11},{10,... | collective-permute-start | bytes 1179656 | tf_op jit(solution)/shard_map/ppermute | solution.py:475
  55.2 2.5 %collective-permute-start.19 = (bf16[128,256]{1,0:T(8,128)(2,1)S(1)}, bf16[128,256]{1,0:T(8,128)(2,1)S(1)}, u32[]{:S(2)}, u32[]{:S(2)}) collective-permute-start(bf16[128,256]{1,0:T(8,128)(2,1)S(1)} %get-tuple-element.94), channel_id=1, source_target_pairs={{0,16},{4,20},{8,24},{12,28},{16,0},{20,4},{24,8},{28,12},{1,17},{... | collective-permute-start | bytes 196616 | tf_op jit(solution)/shard_map/ppermute | solution.py:472
  57.7 1.9 %collective-permute-start.20 = (bf16[128,256]{1,0:T(8,128)(2,1)S(1)}, bf16[128,256]{1,0:T(8,128)(2,1)S(1)}, u32[]{:S(2)}, u32[]{:S(2)}) collective-permute-start(bf16[128,256]{1,0:T(8,128)(2,1)S(1)} %get-tuple-element.95), channel_id=1, source_target_pairs={{0,24},{4,28},{8,16},{12,20},{16,8},{20,12},{24,0},{28,4},{1,25},{... | collective-permute-start | bytes 196616 | tf_op jit(solution)/shard_map/ppermute | solution.py:472
  59.6 2.1 %collective-permute-done.21.refs_1_ = bf16[2,6,64,256]{3,2,1,0:T(8,128)(2,1)S(1)} collective-permute-done((bf16[2,6,64,256]{3,2,1,0:T(8,128)(2,1)S(1)}, bf16[2,6,64,256]{3,2,1,0:T(8,128)(2,1)S(1)}, u32[]{:S(2)}, u32[]{:S(2)}) %collective-permute-start.21) | collective-permute-done | bytes 393248 | tf_op jit(solution)/shard_map/ppermute | solution.py:475
  61.8 1.6 %collective-permute-start.26 = (bf16[2,4,64,256]{3,2,1,0:T(8,128)(2,1)S(1)}, bf16[2,4,64,256]{3,2,1,0:T(8,128)(2,1)S(1)}, u32[]{:S(2)}, u32[]{:S(2)}) collective-permute-start(bf16[2,4,64,256]{3,2,1,0:T(8,128)(2,1)S(1)} %get-tuple-element.104.refs_0_), channel_id=1, source_target_pairs={{0,2},{1,3},{2,0},{3,1},{4,6},{5,7},{6,4},{7,5},{8,10},{9,11},{10,... | collective-permute-start | bytes 786440 | tf_op jit(solution)/shard_map/ppermute | solution.py:475
  66.3 2.5 %collective-permute-start.24 = (bf16[128,256]{1,0:T(8,128)(2,1)S(1)}, bf16[128,256]{1,0:T(8,128)(2,1)S(1)}, u32[]{:S(2)}, u32[]{:S(2)}) collective-permute-start(bf16[128,256]{1,0:T(8,128)(2,1)S(1)} %get-tuple-element.102), channel_id=1, source_target_pairs={{0,16},{4,20},{8,24},{12,28},{16,0},{20,4},{24,8},{28,12},{1,17},{... | collective-permute-start | bytes 196616 | tf_op jit(solution)/shard_map/ppermute | solution.py:472
  68.8 1.8 %collective-permute-start.25 = (bf16[128,256]{1,0:T(8,128)(2,1)S(1)}, bf16[128,256]{1,0:T(8,128)(2,1)S(1)}, u32[]{:S(2)}, u32[]{:S(2)}) collective-permute-start(bf16[128,256]{1,0:T(8,128)(2,1)S(1)} %get-tuple-element.103), channel_id=1, source_target_pairs={{0,24},{4,28},{8,16},{12,20},{16,8},{20,12},{24,0},{28,4},{1,25},{... | collective-permute-start | bytes 196616 | tf_op jit(solution)/shard_map/ppermute | solution.py:472
  72.3 1.8 %collective-permute-done.24.refs_3_ = bf16[128,256]{1,0:T(8,128)(2,1)S(1)} collective-permute-done((bf16[128,256]{1,0:T(8,128)(2,1)S(1)}, bf16[128,256]{1,0:T(8,128)(2,1)S(1)}, u32[]{:S(2)}, u32[]{:S(2)}) %collective-permute-start.24) | collective-permute-done | bytes 65568 | tf_op jit(solution)/shard_map/ppermute | solution.py:472
  78.3 2.0 %collective-permute-start.30 = (bf16[128,256]{1,0:T(8,128)(2,1)S(1)}, bf16[128,256]{1,0:T(8,128)(2,1)S(1)}, u32[]{:S(2)}, u32[]{:S(2)}) collective-permute-start(bf16[128,256]{1,0:T(8,128)(2,1)S(1)} %get-tuple-element.106.refs_1_.refs_4_.refs_5_.refs_9_), channel_id=1, source_target_pairs={{0,24},{4,28},{8,16},{12,20},{16,8},{20,12},{24,0},{28,4},{1,25},{... | collective-permute-start | bytes 196616 | tf_op jit(solution)/shard_map/ppermute | solution.py:472
  86.3 2.0 %collective-permute-start.35 = (bf16[128,256]{1,0:T(8,128)(2,1)S(1)}, bf16[128,256]{1,0:T(8,128)(2,1)S(1)}, u32[]{:S(2)}, u32[]{:S(2)}) collective-permute-start(bf16[128,256]{1,0:T(8,128)(2,1)S(1)} %shard_map.92.refs_4_.refs_1_.refs_5_.refs_3_), channel_id=1, source_target_pairs={{0,16},{4,20},{8,24},{12,28},{16,0},{20,4},{24,8},{28,12},{1,17},{... | collective-permute-start | bytes 196616 | tf_op jit(solution)/shard_map/ppermute | solution.py:472
  88.3 1.8 %collective-permute-start.36 = (bf16[128,256]{1,0:T(8,128)(2,1)S(1)}, bf16[128,256]{1,0:T(8,128)(2,1)S(1)}, u32[]{:S(2)}, u32[]{:S(2)}) collective-permute-start(bf16[128,256]{1,0:T(8,128)(2,1)S(1)} %shard_map.92.refs_4_.refs_1_.refs_5_.refs_3_), channel_id=1, source_target_pairs={{0,24},{4,28},{8,16},{12,20},{16,8},{20,12},{24,0},{28,4},{1,25},{... | collective-permute-start | bytes 196616 | tf_op jit(solution)/shard_map/ppermute | solution.py:472
  90.1 3.9 %collective-permute-done.37.refs_1_ = bf16[2,6,64,256]{3,2,1,0:T(8,128)(2,1)S(1)} collective-permute-done((bf16[2,6,64,256]{3,2,1,0:T(8,128)(2,1)S(1)}, bf16[2,6,64,256]{3,2,1,0:T(8,128)(2,1)S(1)}, u32[]{:S(2)}, u32[]{:S(2)}) %collective-permute-start.37) | collective-permute-done | bytes 393248 | tf_op jit(solution)/shard_map/ppermute | solution.py:475
  98.0 2.0 %collective-permute-start.40 = (bf16[128,256]{1,0:T(8,128)(2,1)S(1)}, bf16[128,256]{1,0:T(8,128)(2,1)S(1)}, u32[]{:S(2)}, u32[]{:S(2)}) collective-permute-start(bf16[128,256]{1,0:T(8,128)(2,1)S(1)} %shard_map.95.refs_4_.refs_1_.refs_2_), channel_id=1, source_target_pairs={{0,16},{4,20},{8,24},{12,28},{16,0},{20,4},{24,8},{28,12},{1,17},{... | collective-permute-start | bytes 196616 | tf_op jit(solution)/shard_map/ppermute | solution.py:472
  100.0 1.8 %collective-permute-start.41 = (bf16[128,256]{1,0:T(8,128)(2,1)S(1)}, bf16[128,256]{1,0:T(8,128)(2,1)S(1)}, u32[]{:S(2)}, u32[]{:S(2)}) collective-permute-start(bf16[128,256]{1,0:T(8,128)(2,1)S(1)} %shard_map.95.refs_4_.refs_1_.refs_2_), channel_id=1, source_target_pairs={{0,24},{4,28},{8,16},{12,20},{16,8},{20,12},{24,0},{28,4},{1,25},{... | collective-permute-start | bytes 196616 | tf_op jit(solution)/shard_map/ppermute | solution.py:472
  101.8 3.9 %collective-permute-done.42.refs_1_ = bf16[2,6,64,256]{3,2,1,0:T(8,128)(2,1)S(1)} collective-permute-done((bf16[2,6,64,256]{3,2,1,0:T(8,128)(2,1)S(1)}, bf16[2,6,64,256]{3,2,1,0:T(8,128)(2,1)S(1)}, u32[]{:S(2)}, u32[]{:S(2)}) %collective-permute-start.42) | collective-permute-done | bytes 393248 | tf_op jit(solution)/shard_map/ppermute | solution.py:475
  109.7 2.1 %collective-permute-start.45 = (bf16[128,256]{1,0:T(8,128)(2,1)S(1)}, bf16[128,256]{1,0:T(8,128)(2,1)S(1)}, u32[]{:S(2)}, u32[]{:S(2)}) collective-permute-start(bf16[128,256]{1,0:T(8,128)(2,1)S(1)} %shard_map.98.refs_2_.refs_1_), channel_id=1, source_target_pairs={{0,16},{4,20},{8,24},{12,28},{16,0},{20,4},{24,8},{28,12},{1,17},{... | collective-permute-start | bytes 196616 | tf_op jit(solution)/shard_map/ppermute | solution.py:472
  111.8 1.8 %collective-permute-start.46 = (bf16[128,256]{1,0:T(8,128)(2,1)S(1)}, bf16[128,256]{1,0:T(8,128)(2,1)S(1)}, u32[]{:S(2)}, u32[]{:S(2)}) collective-permute-start(bf16[128,256]{1,0:T(8,128)(2,1)S(1)} %shard_map.98.refs_2_.refs_1_), channel_id=1, source_target_pairs={{0,24},{4,28},{8,16},{12,20},{16,8},{20,12},{24,0},{28,4},{1,25},{... | collective-permute-start | bytes 196616 | tf_op jit(solution)/shard_map/ppermute | solution.py:472
  113.7 3.8 %collective-permute-done.47.refs_1_ = bf16[2,6,64,256]{3,2,1,0:T(8,128)(2,1)S(1)} collective-permute-done((bf16[2,6,64,256]{3,2,1,0:T(8,128)(2,1)S(1)}, bf16[2,6,64,256]{3,2,1,0:T(8,128)(2,1)S(1)}, u32[]{:S(2)}, u32[]{:S(2)}) %collective-permute-start.47) | collective-permute-done | bytes 393248 | tf_op jit(solution)/shard_map/ppermute | solution.py:475
  123.0 1.5 %collective-permute-start.52 = (bf16[3,64,128]{2,1,0:T(8,128)(2,1)S(1)}, bf16[3,64,128]{2,1,0:T(8,128)(2,1)S(1)}, u32[]{:S(2)}, u32[]{:S(2)}) collective-permute-start(bf16[3,64,128]{2,1,0:T(8,128)(2,1)S(1)} %get-tuple-element.123), channel_id=1, source_target_pairs={{0,4},{1,5},{2,6},{3,7},{4,0},{5,1},{6,2},{7,3},{8,12},{9,13},{10,... | collective-permute-start | bytes 147464 | tf_op jit(solution)/shard_map/ppermute | solution.py:486
  124.8 1.8 %collective-permute-start.54 = (bf16[3,64,128]{2,1,0:T(8,128)(2,1)S(1)}, bf16[3,64,128]{2,1,0:T(8,128)(2,1)S(1)}, u32[]{:S(2)}, u32[]{:S(2)}) collective-permute-start(bf16[3,64,128]{2,1,0:T(8,128)(2,1)S(1)} %get-tuple-element.125), channel_id=1, source_target_pairs={{0,6},{1,7},{2,4},{3,5},{4,2},{5,3},{6,0},{7,1},{8,14},{9,15},{10,... | collective-permute-start | bytes 147464 | tf_op jit(solution)/shard_map/ppermute | solution.py:486
  128.2 1.6 %collective-permute-done.54.refs_6_ = bf16[3,64,128]{2,1,0:T(8,128)(2,1)S(1)} collective-permute-done((bf16[3,64,128]{2,1,0:T(8,128)(2,1)S(1)}, bf16[3,64,128]{2,1,0:T(8,128)(2,1)S(1)}, u32[]{:S(2)}, u32[]{:S(2)}) %collective-permute-start.54) | collective-permute-done | bytes 49184 | tf_op jit(solution)/shard_map/ppermute | solution.py:486
  129.8 1.5 %collective-permute-done.55.refs_7_ = bf16[3,64,128]{2,1,0:T(8,128)(2,1)S(1)} collective-permute-done((bf16[3,64,128]{2,1,0:T(8,128)(2,1)S(1)}, bf16[3,64,128]{2,1,0:T(8,128)(2,1)S(1)}, u32[]{:S(2)}, u32[]{:S(2)}) %collective-permute-start.55) | collective-permute-done | bytes 49184 | tf_op jit(solution)/shard_map/ppermute | solution.py:486
  (123 shorter events, 49.4 us)
Async XLA Ops:
  3.5 10.2 %collective-permute-start.3 = (bf16[6,64,256]{2,1,0:T(8,128)(2,1)}, bf16[6,64,256]{2,1,0:T(8,128)(2,1)S(1)}, u32[]{:S(2)}, u32[]{:S(2)}) collective-permute-start(bf16[6,64,256]{2,1,0:T(8,128)(2,1)} %get-tuple-element.70.refs_4_), channel_id=1, source_target_pairs={{0,4},{4,0},{8,12},{12,8},{16,20},{20,16},{24,28},{28,24},{1,5},{5... | collective-permute-start | bytes 589832 | tf_op jit(solution)/shard_map/ppermute | solution.py:472
  6.5 8.0 %collective-permute-start.4 = (bf16[6,64,256]{2,1,0:T(8,128)(2,1)}, bf16[6,64,256]{2,1,0:T(8,128)(2,1)S(1)}, u32[]{:S(2)}, u32[]{:S(2)}) collective-permute-start(bf16[6,64,256]{2,1,0:T(8,128)(2,1)} %get-tuple-element.70.refs_4_), channel_id=1, source_target_pairs={{0,2},{1,3},{2,0},{3,1},{4,6},{5,7},{6,4},{7,5},{8,10},{9,11},{10,... | collective-permute-start | bytes 589832 | tf_op jit(solution)/shard_map/ppermute | solution.py:475
  8.0 20.5 %collective-permute-start = (bf16[9,64,256]{2,1,0:T(8,128)(2,1)}, bf16[9,64,256]{2,1,0:T(8,128)(2,1)S(1)}, u32[]{:S(2)}, u32[]{:S(2)}) collective-permute-start(bf16[9,64,256]{2,1,0:T(8,128)(2,1)} %get-tuple-element.67), channel_id=1, source_target_pairs={{0,4},{1,5},{2,6},{3,7},{4,0},{5,1},{6,2},{7,3},{8,12},{9,13},{10,... | collective-permute-start | bytes 884744 | tf_op jit(solution)/shard_map/ppermute | solution.py:486
  8.5 20.0 %collective-permute-start.1 = (bf16[9,64,256]{2,1,0:T(8,128)(2,1)}, bf16[9,64,256]{2,1,0:T(8,128)(2,1)S(1)}, u32[]{:S(2)}, u32[]{:S(2)}) collective-permute-start(bf16[9,64,256]{2,1,0:T(8,128)(2,1)} %get-tuple-element.68), channel_id=1, source_target_pairs={{0,2},{1,3},{2,0},{3,1},{4,6},{5,7},{6,4},{7,5},{8,10},{9,11},{10,... | collective-permute-start | bytes 884744 | tf_op jit(solution)/shard_map/ppermute | solution.py:486
  8.6 19.9 %collective-permute-start.2 = (bf16[9,64,256]{2,1,0:T(8,128)(2,1)}, bf16[9,64,256]{2,1,0:T(8,128)(2,1)S(1)}, u32[]{:S(2)}, u32[]{:S(2)}) collective-permute-start(bf16[9,64,256]{2,1,0:T(8,128)(2,1)} %get-tuple-element.69), channel_id=1, source_target_pairs={{0,6},{1,7},{2,4},{3,5},{4,2},{5,3},{6,0},{7,1},{8,14},{9,15},{10,... | collective-permute-start | bytes 884744 | tf_op jit(solution)/shard_map/ppermute | solution.py:486
  13.7 14.8 %collective-permute-start.6 = (bf16[6,64,256]{2,1,0:T(8,128)(2,1)S(1)}, bf16[6,64,256]{2,1,0:T(8,128)(2,1)S(1)}, u32[]{:S(2)}, u32[]{:S(2)}) collective-permute-start(bf16[6,64,256]{2,1,0:T(8,128)(2,1)S(1)} %get-tuple-element.71.refs_8_), channel_id=1, source_target_pairs={{0,4},{4,0},{8,12},{12,8},{16,20},{20,16},{24,28},{28,24},{1,5},{5... | collective-permute-start | bytes 589832 | tf_op jit(solution)/shard_map/ppermute | solution.py:472
  14.6 15.4 %collective-permute-start.5 = (bf16[6,64,256]{2,1,0:T(8,128)(2,1)S(1)}, bf16[6,64,256]{2,1,0:T(8,128)(2,1)S(1)}, u32[]{:S(2)}, u32[]{:S(2)}) collective-permute-start(bf16[6,64,256]{2,1,0:T(8,128)(2,1)S(1)} %collective-permute-done.3.refs_5_), channel_id=1, source_target_pairs={{0,2},{1,3},{2,0},{3,1},{4,6},{5,7},{6,4},{7,5},{8,10},{9,11},{10,... | collective-permute-start | bytes 589832 | tf_op jit(solution)/shard_map/ppermute | solution.py:475
  30.3 8.1 %collective-permute-start.11 = (bf16[2,2,6,64,256]{4,3,2,1,0:T(8,128)(2,1)S(1)}, bf16[2,2,6,64,256]{4,3,2,1,0:T(8,128)(2,1)S(1)}, u32[]{:S(2)}, u32[]{:S(2)}) collective-permute-start(bf16[2,2,6,64,256]{4,3,2,1,0:T(8,128)(2,1)S(1)} %get-tuple-element.83.refs_7_), channel_id=1, source_target_pairs={{0,1},{1,0},{2,3},{3,2},{4,5},{5,4},{6,7},{7,6},{8,9},{9,8},{10,11... | collective-permute-start | bytes 2359304 | tf_op jit(solution)/shard_map/ppermute | solution.py:475
  30.7 19.2 %collective-permute-start.15 = (bf16[2,6,64,256]{3,2,1,0:T(8,128)(2,1)S(1)}, bf16[2,6,64,256]{3,2,1,0:T(8,128)(2,1)S(1)}, u32[]{:S(2)}, u32[]{:S(2)}) collective-permute-start(bf16[2,6,64,256]{3,2,1,0:T(8,128)(2,1)S(1)} %get-tuple-element.89.refs_1_.refs_0_), channel_id=1, source_target_pairs={{0,2},{1,3},{2,0},{3,1},{4,6},{5,7},{6,4},{7,5},{8,10},{9,11},{10,... | collective-permute-start | bytes 1179656 | tf_op jit(solution)/shard_map/ppermute | solution.py:475
  32.2 17.7 %collective-permute-start.16 = (bf16[16,64,256]{2,1,0:T(8,128)(2,1)S(1)}, bf16[16,64,256]{2,1,0:T(8,128)(2,1)S(1)}, u32[]{:S(2)}, u32[]{:S(2)}) collective-permute-start(bf16[16,64,256]{2,1,0:T(8,128)(2,1)S(1)} %shard_map.80.refs_2_), channel_id=1, source_target_pairs={{0,4},{4,0},{8,12},{12,8},{16,20},{20,16},{24,28},{28,24},{1,5},{5... | collective-permute-start | bytes 1572872 | tf_op jit(solution)/shard_map/ppermute | solution.py:472
  35.8 7.5 %collective-permute-start.9 = (bf16[128,256]{1,0:T(8,128)(2,1)S(1)}, bf16[128,256]{1,0:T(8,128)(2,1)S(1)}, u32[]{:S(2)}, u32[]{:S(2)}) collective-permute-start(bf16[128,256]{1,0:T(8,128)(2,1)S(1)} %get-tuple-element.80), channel_id=1, source_target_pairs={{0,16},{4,20},{8,24},{12,28},{16,0},{20,4},{24,8},{28,12},{1,17},{... | collective-permute-start | bytes 196616 | tf_op jit(solution)/shard_map/ppermute | solution.py:472
  45.5 7.1 %collective-permute-start.12 = (bf16[128,256]{1,0:T(8,128)(2,1)S(1)}, bf16[128,256]{1,0:T(8,128)(2,1)S(1)}, u32[]{:S(2)}, u32[]{:S(2)}) collective-permute-start(bf16[128,256]{1,0:T(8,128)(2,1)S(1)} %get-tuple-element.85), channel_id=1, source_target_pairs={{0,8},{4,12},{8,0},{12,4},{16,24},{20,28},{24,16},{28,20},{1,9},{5... | collective-permute-start | bytes 196616 | tf_op jit(solution)/shard_map/ppermute | solution.py:472
  50.1 11.5 %collective-permute-start.21 = (bf16[2,6,64,256]{3,2,1,0:T(8,128)(2,1)S(1)}, bf16[2,6,64,256]{3,2,1,0:T(8,128)(2,1)S(1)}, u32[]{:S(2)}, u32[]{:S(2)}) collective-permute-start(bf16[2,6,64,256]{3,2,1,0:T(8,128)(2,1)S(1)} %get-tuple-element.97.refs_0_), channel_id=1, source_target_pairs={{0,2},{1,3},{2,0},{3,1},{4,6},{5,7},{6,4},{7,5},{8,10},{9,11},{10,... | collective-permute-start | bytes 1179656 | tf_op jit(solution)/shard_map/ppermute | solution.py:475
  55.1 9.5 %collective-permute-start.18 = (bf16[128,256]{1,0:T(8,128)(2,1)S(1)}, bf16[128,256]{1,0:T(8,128)(2,1)S(1)}, u32[]{:S(2)}, u32[]{:S(2)}) collective-permute-start(bf16[128,256]{1,0:T(8,128)(2,1)S(1)} %get-tuple-element.93), channel_id=1, source_target_pairs={{0,8},{4,12},{8,0},{12,4},{16,24},{20,28},{24,16},{28,20},{1,9},{5... | collective-permute-start | bytes 196616 | tf_op jit(solution)/shard_map/ppermute | solution.py:472
  55.2 9.5 %collective-permute-start.19 = (bf16[128,256]{1,0:T(8,128)(2,1)S(1)}, bf16[128,256]{1,0:T(8,128)(2,1)S(1)}, u32[]{:S(2)}, u32[]{:S(2)}) collective-permute-start(bf16[128,256]{1,0:T(8,128)(2,1)S(1)} %get-tuple-element.94), channel_id=1, source_target_pairs={{0,16},{4,20},{8,24},{12,28},{16,0},{20,4},{24,8},{28,12},{1,17},{... | collective-permute-start | bytes 196616 | tf_op jit(solution)/shard_map/ppermute | solution.py:472
  61.8 8.8 %collective-permute-start.26 = (bf16[2,4,64,256]{3,2,1,0:T(8,128)(2,1)S(1)}, bf16[2,4,64,256]{3,2,1,0:T(8,128)(2,1)S(1)}, u32[]{:S(2)}, u32[]{:S(2)}) collective-permute-start(bf16[2,4,64,256]{3,2,1,0:T(8,128)(2,1)S(1)} %get-tuple-element.104.refs_0_), channel_id=1, source_target_pairs={{0,2},{1,3},{2,0},{3,1},{4,6},{5,7},{6,4},{7,5},{8,10},{9,11},{10,... | collective-permute-start | bytes 786440 | tf_op jit(solution)/shard_map/ppermute | solution.py:475
  65.8 15.5 %collective-permute-start.32 = (bf16[18,64,256]{2,1,0:T(8,128)(2,1)S(1)}, bf16[18,64,256]{2,1,0:T(8,128)(2,1)S(1)}, u32[]{:S(2)}, u32[]{:S(2)}) collective-permute-start(bf16[18,64,256]{2,1,0:T(8,128)(2,1)S(1)} %shard_map.90.refs_2_), channel_id=1, source_target_pairs={{0,4},{4,0},{8,12},{12,8},{16,20},{20,16},{24,28},{28,24},{1,5},{5... | collective-permute-start | bytes 1769480 | tf_op jit(solution)/shard_map/ppermute | solution.py:472
  66.3 7.7 %collective-permute-start.24 = (bf16[128,256]{1,0:T(8,128)(2,1)S(1)}, bf16[128,256]{1,0:T(8,128)(2,1)S(1)}, u32[]{:S(2)}, u32[]{:S(2)}) collective-permute-start(bf16[128,256]{1,0:T(8,128)(2,1)S(1)} %get-tuple-element.102), channel_id=1, source_target_pairs={{0,16},{4,20},{8,24},{12,28},{16,0},{20,4},{24,8},{28,12},{1,17},{... | collective-permute-start | bytes 196616 | tf_op jit(solution)/shard_map/ppermute | solution.py:472
  70.8 11.5 %collective-permute-start.31 = (bf16[2,6,64,256]{3,2,1,0:T(8,128)(2,1)S(1)}, bf16[2,6,64,256]{3,2,1,0:T(8,128)(2,1)S(1)}, u32[]{:S(2)}, u32[]{:S(2)}) collective-permute-start(bf16[2,6,64,256]{3,2,1,0:T(8,128)(2,1)S(1)} %get-tuple-element.108.refs_0_), channel_id=1, source_target_pairs={{0,2},{1,3},{2,0},{3,1},{4,6},{5,7},{6,4},{7,5},{8,10},{9,11},{10,... | collective-permute-start | bytes 1179656 | tf_op jit(solution)/shard_map/ppermute | solution.py:475
  75.9 8.0 %collective-permute-start.28 = (bf16[128,256]{1,0:T(8,128)(2,1)S(1)}, bf16[128,256]{1,0:T(8,128)(2,1)S(1)}, u32[]{:S(2)}, u32[]{:S(2)}) collective-permute-start(bf16[128,256]{1,0:T(8,128)(2,1)S(1)} %get-tuple-element.106.refs_1_.refs_4_.refs_5_.refs_9_), channel_id=1, source_target_pairs={{0,8},{4,12},{8,0},{12,4},{16,24},{20,28},{24,16},{28,20},{1,9},{5... | collective-permute-start | bytes 196616 | tf_op jit(solution)/shard_map/ppermute | solution.py:472
  77.0 7.0 %collective-permute-start.29 = (bf16[128,256]{1,0:T(8,128)(2,1)S(1)}, bf16[128,256]{1,0:T(8,128)(2,1)S(1)}, u32[]{:S(2)}, u32[]{:S(2)}) collective-permute-start(bf16[128,256]{1,0:T(8,128)(2,1)S(1)} %get-tuple-element.106.refs_1_.refs_4_.refs_5_.refs_9_), channel_id=1, source_target_pairs={{0,16},{4,20},{8,24},{12,28},{16,0},{20,4},{24,8},{28,12},{1,17},{... | collective-permute-start | bytes 196616 | tf_op jit(solution)/shard_map/ppermute | solution.py:472
  82.5 11.5 %collective-permute-start.37 = (bf16[2,6,64,256]{3,2,1,0:T(8,128)(2,1)S(1)}, bf16[2,6,64,256]{3,2,1,0:T(8,128)(2,1)S(1)}, u32[]{:S(2)}, u32[]{:S(2)}) collective-permute-start(bf16[2,6,64,256]{3,2,1,0:T(8,128)(2,1)S(1)} %get-tuple-element.112.refs_0_), channel_id=1, source_target_pairs={{0,2},{1,3},{2,0},{3,1},{4,6},{5,7},{6,4},{7,5},{8,10},{9,11},{10,... | collective-permute-start | bytes 1179656 | tf_op jit(solution)/shard_map/ppermute | solution.py:475
  85.7 10.5 %collective-permute-start.34 = (bf16[128,256]{1,0:T(8,128)(2,1)S(1)}, bf16[128,256]{1,0:T(8,128)(2,1)S(1)}, u32[]{:S(2)}, u32[]{:S(2)}) collective-permute-start(bf16[128,256]{1,0:T(8,128)(2,1)S(1)} %shard_map.92.refs_4_.refs_1_.refs_5_.refs_3_), channel_id=1, source_target_pairs={{0,8},{4,12},{8,0},{12,4},{16,24},{20,28},{24,16},{28,20},{1,9},{5... | collective-permute-start | bytes 196616 | tf_op jit(solution)/shard_map/ppermute | solution.py:472
  86.3 9.9 %collective-permute-start.35 = (bf16[128,256]{1,0:T(8,128)(2,1)S(1)}, bf16[128,256]{1,0:T(8,128)(2,1)S(1)}, u32[]{:S(2)}, u32[]{:S(2)}) collective-permute-start(bf16[128,256]{1,0:T(8,128)(2,1)S(1)} %shard_map.92.refs_4_.refs_1_.refs_5_.refs_3_), channel_id=1, source_target_pairs={{0,16},{4,20},{8,24},{12,28},{16,0},{20,4},{24,8},{28,12},{1,17},{... | collective-permute-start | bytes 196616 | tf_op jit(solution)/shard_map/ppermute | solution.py:472
  88.3 7.9 %collective-permute-start.36 = (bf16[128,256]{1,0:T(8,128)(2,1)S(1)}, bf16[128,256]{1,0:T(8,128)(2,1)S(1)}, u32[]{:S(2)}, u32[]{:S(2)}) collective-permute-start(bf16[128,256]{1,0:T(8,128)(2,1)S(1)} %shard_map.92.refs_4_.refs_1_.refs_5_.refs_3_), channel_id=1, source_target_pairs={{0,24},{4,28},{8,16},{12,20},{16,8},{20,12},{24,0},{28,4},{1,25},{... | collective-permute-start | bytes 196616 | tf_op jit(solution)/shard_map/ppermute | solution.py:472
  94.2 11.5 %collective-permute-start.42 = (bf16[2,6,64,256]{3,2,1,0:T(8,128)(2,1)S(1)}, bf16[2,6,64,256]{3,2,1,0:T(8,128)(2,1)S(1)}, u32[]{:S(2)}, u32[]{:S(2)}) collective-permute-start(bf16[2,6,64,256]{3,2,1,0:T(8,128)(2,1)S(1)} %get-tuple-element.115.refs_0_), channel_id=1, source_target_pairs={{0,2},{1,3},{2,0},{3,1},{4,6},{5,7},{6,4},{7,5},{8,10},{9,11},{10,... | collective-permute-start | bytes 1179656 | tf_op jit(solution)/shard_map/ppermute | solution.py:475
  97.4 10.9 %collective-permute-start.39 = (bf16[128,256]{1,0:T(8,128)(2,1)S(1)}, bf16[128,256]{1,0:T(8,128)(2,1)S(1)}, u32[]{:S(2)}, u32[]{:S(2)}) collective-permute-start(bf16[128,256]{1,0:T(8,128)(2,1)S(1)} %shard_map.95.refs_4_.refs_1_.refs_2_), channel_id=1, source_target_pairs={{0,8},{4,12},{8,0},{12,4},{16,24},{20,28},{24,16},{28,20},{1,9},{5... | collective-permute-start | bytes 196616 | tf_op jit(solution)/shard_map/ppermute | solution.py:472
  98.0 10.3 %collective-permute-start.40 = (bf16[128,256]{1,0:T(8,128)(2,1)S(1)}, bf16[128,256]{1,0:T(8,128)(2,1)S(1)}, u32[]{:S(2)}, u32[]{:S(2)}) collective-permute-start(bf16[128,256]{1,0:T(8,128)(2,1)S(1)} %shard_map.95.refs_4_.refs_1_.refs_2_), channel_id=1, source_target_pairs={{0,16},{4,20},{8,24},{12,28},{16,0},{20,4},{24,8},{28,12},{1,17},{... | collective-permute-start | bytes 196616 | tf_op jit(solution)/shard_map/ppermute | solution.py:472
  100.0 8.3 %collective-permute-start.41 = (bf16[128,256]{1,0:T(8,128)(2,1)S(1)}, bf16[128,256]{1,0:T(8,128)(2,1)S(1)}, u32[]{:S(2)}, u32[]{:S(2)}) collective-permute-start(bf16[128,256]{1,0:T(8,128)(2,1)S(1)} %shard_map.95.refs_4_.refs_1_.refs_2_), channel_id=1, source_target_pairs={{0,24},{4,28},{8,16},{12,20},{16,8},{20,12},{24,0},{28,4},{1,25},{... | collective-permute-start | bytes 196616 | tf_op jit(solution)/shard_map/ppermute | solution.py:472
  105.9 11.5 %collective-permute-start.47 = (bf16[2,6,64,256]{3,2,1,0:T(8,128)(2,1)S(1)}, bf16[2,6,64,256]{3,2,1,0:T(8,128)(2,1)S(1)}, u32[]{:S(2)}, u32[]{:S(2)}) collective-permute-start(bf16[2,6,64,256]{3,2,1,0:T(8,128)(2,1)S(1)} %get-tuple-element.118.refs_0_), channel_id=1, source_target_pairs={{0,2},{1,3},{2,0},{3,1},{4,6},{5,7},{6,4},{7,5},{8,10},{9,11},{10,... | collective-permute-start | bytes 1179656 | tf_op jit(solution)/shard_map/ppermute | solution.py:475
  109.3 9.2 %collective-permute-start.44 = (bf16[128,256]{1,0:T(8,128)(2,1)S(1)}, bf16[128,256]{1,0:T(8,128)(2,1)S(1)}, u32[]{:S(2)}, u32[]{:S(2)}) collective-permute-start(bf16[128,256]{1,0:T(8,128)(2,1)S(1)} %shard_map.98.refs_2_.refs_1_), channel_id=1, source_target_pairs={{0,8},{4,12},{8,0},{12,4},{16,24},{20,28},{24,16},{28,20},{1,9},{5... | collective-permute-start | bytes 196616 | tf_op jit(solution)/shard_map/ppermute | solution.py:472
  109.7 8.8 %collective-permute-start.45 = (bf16[128,256]{1,0:T(8,128)(2,1)S(1)}, bf16[128,256]{1,0:T(8,128)(2,1)S(1)}, u32[]{:S(2)}, u32[]{:S(2)}) collective-permute-start(bf16[128,256]{1,0:T(8,128)(2,1)S(1)} %shard_map.98.refs_2_.refs_1_), channel_id=1, source_target_pairs={{0,16},{4,20},{8,24},{12,28},{16,0},{20,4},{24,8},{28,12},{1,17},{... | collective-permute-start | bytes 196616 | tf_op jit(solution)/shard_map/ppermute | solution.py:472
  (30 other events, 174.8 us)

commit v4 on v3

--- a/solution.py
+++ b/solution.py
@@ -385,9 +385,9 @@
         at = slice(s * c, (s + 1) * c)
         lanes = slice(s * plan.group_rows, (s + 1) * plan.group_rows)
         whole = jnp.concatenate([p[:, lanes] for p in pulled], axis=1)
-        upper = nn(whole, joined(plan, blocks, part_of["upper"], s, tall))
+        upper = nn(whole, joined(plan, blocks[:2], part_of["upper"], s, tall))
         reduced = (forward_ref[at, :] - upper).astype(BF)
-        solved_ref[at, :] = nt(reduced, joined(plan, blocks, part_of["inv"], s)).astype(BF)
+        solved_ref[at, :] = nt(reduced, joined(plan, blocks[2:], part_of["inv"], s)).astype(BF)
 
 
 def pieces_kernel(plan, *refs):
@@ -497,8 +497,8 @@
         return [(dict(fwd=0, inv=1)[name], (level,))]
 
     names = [[("fwd", level), ("upd", level)] for level in range(top)]
-    names.append([("fwd", top), ("inv", top)])
-    names += [[("upper", level), ("inv", level)] for level in reversed(range(top))]
+    names.append([("fwd", top), ("inv", top), ("inv", top - 1)])
+    names += [[("upper", level), ("inv", level - 1)][: 1 + (level > 0)] for level in reversed(range(top))]
     where, layouts = {}, []
     for number, chunk in enumerate(names):
         layouts.append([])
@@ -664,7 +664,9 @@
                 100 * one_pass * len(froms), 16 * slab_bytes,
             )
         advance(levels + top - level - 2, above)
-        blocks, part_of = matrices(level, ["upper", "inv"])
+        blocks, part_of = matrices(level, ["upper"])
+        inverses, inverse_part = matrices(level, ["inv"])
+        blocks, part_of = blocks + inverses, dict(part_of, **inverse_part)
         args = [keys] + everywhere[level + 1] + list(known) + [forward_out[level]]
         (solutions[level],) = call(
             functools.partial(backward_kernel, plan, level, part_of, bool(froms)),

time: 133 us -> 133 us (level)
    ppermute x18, waiting for transfers between devices: 18.7 us -> 20.9 us  [over_grid(): return lax.ppermute(x, 'grid', [(i, i ^ step) for i in range(plan.groups)])]
    ppermute x28, waiting for transfers between devices: 23.5 us -> 21.8 us  [over_leaf(): return lax.ppermute(x, 'leaf', [(i, i ^ step) for i in range(plan.leaves)])]
  transfers between devices with their start and end apart: 56 -> 56, of which waited for: 22 -> 21; matrix products, arithmetic and copies ran while one was open for 0% -> 0% of each run, Pallas kernels for 11% -> 11%
where the time goes in v4:
time: 133 us
  starting transfers between devices  64.9 us (49%)
  waiting for transfers between devices  45.9 us (35%)
  Pallas kernels  20.4 us (15%)
    ppermute x28, starting transfers between devices, over_leaf(): return lax.ppermute(x, 'leaf', [(i, i ^ step) for i in range(plan.leaves)])  40.2 us
    ppermute x28, waiting for transfers between devices, over_leaf(): return lax.ppermute(x, 'leaf', [(i, i ^ step) for i in range(plan.leaves)])  21.8 us
    ppermute x18, waiting for transfers between devices, over_grid(): return lax.ppermute(x, 'grid', [(i, i ^ step) for i in range(plan.groups)])  20.9 us
    pallas_call x27, Pallas kernels, call(): pl.pallas_call(body, in_specs=specs, out_specs=[VM] * len(outs), out_shap...  20.4 us
    ppermute x18, starting transfers between devices, over_grid(): return lax.ppermute(x, 'grid', [(i, i ^ step) for i in range(plan.groups)])  14.9 us
    ppermute x10, starting transfers between devices, swap(): return lax.ppermute(x, ('leaf', 'grid'), moves)  9.81 us
    ppermute x10, waiting for transfers between devices, swap(): return lax.ppermute(x, ('leaf', 'grid'), moves)  3.08 us
  transfers between devices with their start and end apart: 56, of which 21 were waited for; matrix products, arithmetic and copies ran while one was open for 0% of the time, Pallas kernels for 11%

profile of v4, /device:TPU:0, one launch (start us, length us, event | category | flops | bytes accessed | tf_op | source)
XLA Modules:
  0.0 132.6 jit_solution(3691390573604592825)
XLA Ops:
  0.0 3.5 %shard_map.73 = (bf16[9,64,256]{2,1,0:T(8,128)(2,1)}, bf16[9,64,256]{2,1,0:T(8,128)(2,1)}, bf16[9,64,256]{2,1,0:T(8,128)(2,1)}, bf16[9,64,256]{2,1,0:T(8,128)(2,1)}, bf16[6,64,256]{2,1,0:T(8,128)(2,1)}) custom-call(bf16[5,2,64,256]{3,2,1,0:T(8,128)(2,1)} %refs_0_.3, bf16[5,2,64,256]{3,2,1,0:T(8,128)(2,1)} %refs_1_.3, bf16[4,2,64,512]{3,2,1,0:T(8,128)(2,1)} %refs_2_.3, ...), custom_call_target="tpu_custom_call" | custom-call | flops 1 | bytes 1048576 | tf_op jit(solution)/shard_map/pallas_call | solution.py:435
  3.5 3.0 %collective-permute-start.3 = (bf16[6,64,256]{2,1,0:T(8,128)(2,1)}, bf16[6,64,256]{2,1,0:T(8,128)(2,1)S(1)}, u32[]{:S(2)}, u32[]{:S(2)}) collective-permute-start(bf16[6,64,256]{2,1,0:T(8,128)(2,1)} %get-tuple-element.70.refs_4_), channel_id=1, source_target_pairs={{0,4},{4,0},{8,12},{12,8},{16,20},{20,16},{24,28},{28,24},{1,5},{5... | collective-permute-start | bytes 589832 | tf_op jit(solution)/shard_map/ppermute | solution.py:472
  8.6 2.9 %collective-permute-start.2 = (bf16[9,64,256]{2,1,0:T(8,128)(2,1)}, bf16[9,64,256]{2,1,0:T(8,128)(2,1)S(1)}, u32[]{:S(2)}, u32[]{:S(2)}) collective-permute-start(bf16[9,64,256]{2,1,0:T(8,128)(2,1)} %get-tuple-element.69), channel_id=1, source_target_pairs={{0,6},{1,7},{2,4},{3,5},{4,2},{5,3},{6,0},{7,1},{8,14},{9,15},{10,... | collective-permute-start | bytes 884744 | tf_op jit(solution)/shard_map/ppermute | solution.py:486
  16.1 12.4 %collective-permute-done.6.refs_9_ = bf16[6,64,256]{2,1,0:T(8,128)(2,1)S(1)} collective-permute-done((bf16[6,64,256]{2,1,0:T(8,128)(2,1)S(1)}, bf16[6,64,256]{2,1,0:T(8,128)(2,1)S(1)}, u32[]{:S(2)}, u32[]{:S(2)}) %collective-permute-start.6) | collective-permute-done | bytes 196640 | tf_op jit(solution)/shard_map/ppermute | solution.py:472
  34.1 1.6 %collective-permute-start.8 = (bf16[128,256]{1,0:T(8,128)(2,1)S(1)}, bf16[128,256]{1,0:T(8,128)(2,1)S(1)}, u32[]{:S(2)}, u32[]{:S(2)}) collective-permute-start(bf16[128,256]{1,0:T(8,128)(2,1)S(1)} %get-tuple-element.79), channel_id=1, source_target_pairs={{0,8},{4,12},{8,0},{12,4},{16,24},{20,28},{24,16},{28,20},{1,9},{5... | collective-permute-start | bytes 196616 | tf_op jit(solution)/shard_map/ppermute | solution.py:472
  35.8 2.6 %collective-permute-start.9 = (bf16[128,256]{1,0:T(8,128)(2,1)S(1)}, bf16[128,256]{1,0:T(8,128)(2,1)S(1)}, u32[]{:S(2)}, u32[]{:S(2)}) collective-permute-start(bf16[128,256]{1,0:T(8,128)(2,1)S(1)} %get-tuple-element.80), channel_id=1, source_target_pairs={{0,16},{4,20},{8,24},{12,28},{16,0},{20,4},{24,8},{28,12},{1,17},{... | collective-permute-start | bytes 196616 | tf_op jit(solution)/shard_map/ppermute | solution.py:472
  39.2 4.1 %collective-permute-done.9.refs_4_ = bf16[128,256]{1,0:T(8,128)(2,1)S(1)} collective-permute-done((bf16[128,256]{1,0:T(8,128)(2,1)S(1)}, bf16[128,256]{1,0:T(8,128)(2,1)S(1)}, u32[]{:S(2)}, u32[]{:S(2)}) %collective-permute-start.9) | collective-permute-done | bytes 65568 | tf_op jit(solution)/shard_map/ppermute | solution.py:472
  46.4 1.7 %collective-permute-start.13 = (bf16[128,256]{1,0:T(8,128)(2,1)S(1)}, bf16[128,256]{1,0:T(8,128)(2,1)S(1)}, u32[]{:S(2)}, u32[]{:S(2)}) collective-permute-start(bf16[128,256]{1,0:T(8,128)(2,1)S(1)} %get-tuple-element.86), channel_id=1, source_target_pairs={{0,16},{4,20},{8,24},{12,28},{16,0},{20,4},{24,8},{28,12},{1,17},{... | collective-permute-start | bytes 196616 | tf_op jit(solution)/shard_map/ppermute | solution.py:472
  48.1 1.8 %collective-permute-start.14 = (bf16[128,256]{1,0:T(8,128)(2,1)S(1)}, bf16[128,256]{1,0:T(8,128)(2,1)S(1)}, u32[]{:S(2)}, u32[]{:S(2)}) collective-permute-start(bf16[128,256]{1,0:T(8,128)(2,1)S(1)} %get-tuple-element.87), channel_id=1, source_target_pairs={{0,24},{4,28},{8,16},{12,20},{16,8},{20,12},{24,0},{28,4},{1,25},{... | collective-permute-start | bytes 196616 | tf_op jit(solution)/shard_map/ppermute | solution.py:472
  50.1 1.6 %collective-permute-start.21 = (bf16[2,6,64,256]{3,2,1,0:T(8,128)(2,1)S(1)}, bf16[2,6,64,256]{3,2,1,0:T(8,128)(2,1)S(1)}, u32[]{:S(2)}, u32[]{:S(2)}) collective-permute-start(bf16[2,6,64,256]{3,2,1,0:T(8,128)(2,1)S(1)} %get-tuple-element.97.refs_0_), channel_id=1, source_target_pairs={{0,2},{1,3},{2,0},{3,1},{4,6},{5,7},{6,4},{7,5},{8,10},{9,11},{10,... | collective-permute-start | bytes 1179656 | tf_op jit(solution)/shard_map/ppermute | solution.py:475
  55.2 2.5 %collective-permute-start.19 = (bf16[128,256]{1,0:T(8,128)(2,1)S(1)}, bf16[128,256]{1,0:T(8,128)(2,1)S(1)}, u32[]{:S(2)}, u32[]{:S(2)}) collective-permute-start(bf16[128,256]{1,0:T(8,128)(2,1)S(1)} %get-tuple-element.94), channel_id=1, source_target_pairs={{0,16},{4,20},{8,24},{12,28},{16,0},{20,4},{24,8},{28,12},{1,17},{... | collective-permute-start | bytes 196616 | tf_op jit(solution)/shard_map/ppermute | solution.py:472
  57.7 1.9 %collective-permute-start.20 = (bf16[128,256]{1,0:T(8,128)(2,1)S(1)}, bf16[128,256]{1,0:T(8,128)(2,1)S(1)}, u32[]{:S(2)}, u32[]{:S(2)}) collective-permute-start(bf16[128,256]{1,0:T(8,128)(2,1)S(1)} %get-tuple-element.95), channel_id=1, source_target_pairs={{0,24},{4,28},{8,16},{12,20},{16,8},{20,12},{24,0},{28,4},{1,25},{... | collective-permute-start | bytes 196616 | tf_op jit(solution)/shard_map/ppermute | solution.py:472
  59.6 2.1 %collective-permute-done.21.refs_1_ = bf16[2,6,64,256]{3,2,1,0:T(8,128)(2,1)S(1)} collective-permute-done((bf16[2,6,64,256]{3,2,1,0:T(8,128)(2,1)S(1)}, bf16[2,6,64,256]{3,2,1,0:T(8,128)(2,1)S(1)}, u32[]{:S(2)}, u32[]{:S(2)}) %collective-permute-start.21) | collective-permute-done | bytes 393248 | tf_op jit(solution)/shard_map/ppermute | solution.py:475
  61.8 1.6 %collective-permute-start.26 = (bf16[2,6,64,256]{3,2,1,0:T(8,128)(2,1)S(1)}, bf16[2,6,64,256]{3,2,1,0:T(8,128)(2,1)S(1)}, u32[]{:S(2)}, u32[]{:S(2)}) collective-permute-start(bf16[2,6,64,256]{3,2,1,0:T(8,128)(2,1)S(1)} %get-tuple-element.104.refs_0_), channel_id=1, source_target_pairs={{0,2},{1,3},{2,0},{3,1},{4,6},{5,7},{6,4},{7,5},{8,10},{9,11},{10,... | collective-permute-start | bytes 1179656 | tf_op jit(solution)/shard_map/ppermute | solution.py:475
  66.4 2.5 %collective-permute-start.24 = (bf16[128,256]{1,0:T(8,128)(2,1)S(1)}, bf16[128,256]{1,0:T(8,128)(2,1)S(1)}, u32[]{:S(2)}, u32[]{:S(2)}) collective-permute-start(bf16[128,256]{1,0:T(8,128)(2,1)S(1)} %get-tuple-element.102), channel_id=1, source_target_pairs={{0,16},{4,20},{8,24},{12,28},{16,0},{20,4},{24,8},{28,12},{1,17},{... | collective-permute-start | bytes 196616 | tf_op jit(solution)/shard_map/ppermute | solution.py:472
  68.8 1.8 %collective-permute-start.25 = (bf16[128,256]{1,0:T(8,128)(2,1)S(1)}, bf16[128,256]{1,0:T(8,128)(2,1)S(1)}, u32[]{:S(2)}, u32[]{:S(2)}) collective-permute-start(bf16[128,256]{1,0:T(8,128)(2,1)S(1)} %get-tuple-element.103), channel_id=1, source_target_pairs={{0,24},{4,28},{8,16},{12,20},{16,8},{20,12},{24,0},{28,4},{1,25},{... | collective-permute-start | bytes 196616 | tf_op jit(solution)/shard_map/ppermute | solution.py:472
  70.7 2.7 %collective-permute-done.26.refs_1_ = bf16[2,6,64,256]{3,2,1,0:T(8,128)(2,1)S(1)} collective-permute-done((bf16[2,6,64,256]{3,2,1,0:T(8,128)(2,1)S(1)}, bf16[2,6,64,256]{3,2,1,0:T(8,128)(2,1)S(1)}, u32[]{:S(2)}, u32[]{:S(2)}) %collective-permute-start.26) | collective-permute-done | bytes 393248 | tf_op jit(solution)/shard_map/ppermute | solution.py:475
  73.6 1.6 %collective-permute-start.31 = (bf16[2,6,64,256]{3,2,1,0:T(8,128)(2,1)S(1)}, bf16[2,6,64,256]{3,2,1,0:T(8,128)(2,1)S(1)}, u32[]{:S(2)}, u32[]{:S(2)}) collective-permute-start(bf16[2,6,64,256]{3,2,1,0:T(8,128)(2,1)S(1)} %get-tuple-element.108.refs_0_), channel_id=1, source_target_pairs={{0,2},{1,3},{2,0},{3,1},{4,6},{5,7},{6,4},{7,5},{8,10},{9,11},{10,... | collective-permute-start | bytes 1179656 | tf_op jit(solution)/shard_map/ppermute | solution.py:475
  77.0 2.3 %collective-permute-start.29 = (bf16[128,256]{1,0:T(8,128)(2,1)S(1)}, bf16[128,256]{1,0:T(8,128)(2,1)S(1)}, u32[]{:S(2)}, u32[]{:S(2)}) collective-permute-start(bf16[128,256]{1,0:T(8,128)(2,1)S(1)} %get-tuple-element.106.refs_1_.refs_4_.refs_5_.refs_9_), channel_id=1, source_target_pairs={{0,16},{4,20},{8,24},{12,28},{16,0},{20,4},{24,8},{28,12},{1,17},{... | collective-permute-start | bytes 196616 | tf_op jit(solution)/shard_map/ppermute | solution.py:472
  79.3 1.8 %collective-permute-start.30 = (bf16[128,256]{1,0:T(8,128)(2,1)S(1)}, bf16[128,256]{1,0:T(8,128)(2,1)S(1)}, u32[]{:S(2)}, u32[]{:S(2)}) collective-permute-start(bf16[128,256]{1,0:T(8,128)(2,1)S(1)} %get-tuple-element.106.refs_1_.refs_4_.refs_5_.refs_9_), channel_id=1, source_target_pairs={{0,24},{4,28},{8,16},{12,20},{16,8},{20,12},{24,0},{28,4},{1,25},{... | collective-permute-start | bytes 196616 | tf_op jit(solution)/shard_map/ppermute | solution.py:472
  81.1 3.9 %collective-permute-done.31.refs_1_ = bf16[2,6,64,256]{3,2,1,0:T(8,128)(2,1)S(1)} collective-permute-done((bf16[2,6,64,256]{3,2,1,0:T(8,128)(2,1)S(1)}, bf16[2,6,64,256]{3,2,1,0:T(8,128)(2,1)S(1)}, u32[]{:S(2)}, u32[]{:S(2)}) %collective-permute-start.31) | collective-permute-done | bytes 393248 | tf_op jit(solution)/shard_map/ppermute | solution.py:475
  85.3 1.6 %collective-permute-start.37 = (bf16[2,6,64,256]{3,2,1,0:T(8,128)(2,1)S(1)}, bf16[2,6,64,256]{3,2,1,0:T(8,128)(2,1)S(1)}, u32[]{:S(2)}, u32[]{:S(2)}) collective-permute-start(bf16[2,6,64,256]{3,2,1,0:T(8,128)(2,1)S(1)} %get-tuple-element.112.refs_0_), channel_id=1, source_target_pairs={{0,2},{1,3},{2,0},{3,1},{4,6},{5,7},{6,4},{7,5},{8,10},{9,11},{10,... | collective-permute-start | bytes 1179656 | tf_op jit(solution)/shard_map/ppermute | solution.py:475
  88.5 2.5 %collective-permute-start.35 = (bf16[128,256]{1,0:T(8,128)(2,1)S(1)}, bf16[128,256]{1,0:T(8,128)(2,1)S(1)}, u32[]{:S(2)}, u32[]{:S(2)}) collective-permute-start(bf16[128,256]{1,0:T(8,128)(2,1)S(1)} %shard_map.92.refs_4_.refs_1_.refs_5_.refs_3_), channel_id=1, source_target_pairs={{0,16},{4,20},{8,24},{12,28},{16,0},{20,4},{24,8},{28,12},{1,17},{... | collective-permute-start | bytes 196616 | tf_op jit(solution)/shard_map/ppermute | solution.py:472
  91.0 1.8 %collective-permute-start.36 = (bf16[128,256]{1,0:T(8,128)(2,1)S(1)}, bf16[128,256]{1,0:T(8,128)(2,1)S(1)}, u32[]{:S(2)}, u32[]{:S(2)}) collective-permute-start(bf16[128,256]{1,0:T(8,128)(2,1)S(1)} %shard_map.92.refs_4_.refs_1_.refs_5_.refs_3_), channel_id=1, source_target_pairs={{0,24},{4,28},{8,16},{12,20},{16,8},{20,12},{24,0},{28,4},{1,25},{... | collective-permute-start | bytes 196616 | tf_op jit(solution)/shard_map/ppermute | solution.py:472
  92.8 3.9 %collective-permute-done.37.refs_1_ = bf16[2,6,64,256]{3,2,1,0:T(8,128)(2,1)S(1)} collective-permute-done((bf16[2,6,64,256]{3,2,1,0:T(8,128)(2,1)S(1)}, bf16[2,6,64,256]{3,2,1,0:T(8,128)(2,1)S(1)}, u32[]{:S(2)}, u32[]{:S(2)}) %collective-permute-start.37) | collective-permute-done | bytes 393248 | tf_op jit(solution)/shard_map/ppermute | solution.py:475
  100.2 2.5 %collective-permute-start.40 = (bf16[128,256]{1,0:T(8,128)(2,1)S(1)}, bf16[128,256]{1,0:T(8,128)(2,1)S(1)}, u32[]{:S(2)}, u32[]{:S(2)}) collective-permute-start(bf16[128,256]{1,0:T(8,128)(2,1)S(1)} %shard_map.95.refs_4_.refs_1_.refs_2_), channel_id=1, source_target_pairs={{0,16},{4,20},{8,24},{12,28},{16,0},{20,4},{24,8},{28,12},{1,17},{... | collective-permute-start | bytes 196616 | tf_op jit(solution)/shard_map/ppermute | solution.py:472
  102.7 1.8 %collective-permute-start.41 = (bf16[128,256]{1,0:T(8,128)(2,1)S(1)}, bf16[128,256]{1,0:T(8,128)(2,1)S(1)}, u32[]{:S(2)}, u32[]{:S(2)}) collective-permute-start(bf16[128,256]{1,0:T(8,128)(2,1)S(1)} %shard_map.95.refs_4_.refs_1_.refs_2_), channel_id=1, source_target_pairs={{0,24},{4,28},{8,16},{12,20},{16,8},{20,12},{24,0},{28,4},{1,25},{... | collective-permute-start | bytes 196616 | tf_op jit(solution)/shard_map/ppermute | solution.py:472
  104.6 3.9 %collective-permute-done.42.refs_1_ = bf16[2,6,64,256]{3,2,1,0:T(8,128)(2,1)S(1)} collective-permute-done((bf16[2,6,64,256]{3,2,1,0:T(8,128)(2,1)S(1)}, bf16[2,6,64,256]{3,2,1,0:T(8,128)(2,1)S(1)}, u32[]{:S(2)}, u32[]{:S(2)}) %collective-permute-start.42) | collective-permute-done | bytes 393248 | tf_op jit(solution)/shard_map/ppermute | solution.py:475
  112.1 2.5 %collective-permute-start.45 = (bf16[128,256]{1,0:T(8,128)(2,1)S(1)}, bf16[128,256]{1,0:T(8,128)(2,1)S(1)}, u32[]{:S(2)}, u32[]{:S(2)}) collective-permute-start(bf16[128,256]{1,0:T(8,128)(2,1)S(1)} %shard_map.98.refs_2_.refs_1_), channel_id=1, source_target_pairs={{0,16},{4,20},{8,24},{12,28},{16,0},{20,4},{24,8},{28,12},{1,17},{... | collective-permute-start | bytes 196616 | tf_op jit(solution)/shard_map/ppermute | solution.py:472
  114.7 1.8 %collective-permute-start.46 = (bf16[128,256]{1,0:T(8,128)(2,1)S(1)}, bf16[128,256]{1,0:T(8,128)(2,1)S(1)}, u32[]{:S(2)}, u32[]{:S(2)}) collective-permute-start(bf16[128,256]{1,0:T(8,128)(2,1)S(1)} %shard_map.98.refs_2_.refs_1_), channel_id=1, source_target_pairs={{0,24},{4,28},{8,16},{12,20},{16,8},{20,12},{24,0},{28,4},{1,25},{... | collective-permute-start | bytes 196616 | tf_op jit(solution)/shard_map/ppermute | solution.py:472
  118.4 2.5 %collective-permute-done.45.refs_3_ = bf16[128,256]{1,0:T(8,128)(2,1)S(1)} collective-permute-done((bf16[128,256]{1,0:T(8,128)(2,1)S(1)}, bf16[128,256]{1,0:T(8,128)(2,1)S(1)}, u32[]{:S(2)}, u32[]{:S(2)}) %collective-permute-start.45) | collective-permute-done | bytes 65568 | tf_op jit(solution)/shard_map/ppermute | solution.py:472
  128.7 1.9 %collective-permute-done.54.refs_6_ = bf16[3,64,128]{2,1,0:T(8,128)(2,1)S(1)} collective-permute-done((bf16[3,64,128]{2,1,0:T(8,128)(2,1)S(1)}, bf16[3,64,128]{2,1,0:T(8,128)(2,1)S(1)}, u32[]{:S(2)}, u32[]{:S(2)}) %collective-permute-start.54) | collective-permute-done | bytes 49184 | tf_op jit(solution)/shard_map/ppermute | solution.py:486
  (123 shorter events, 45.2 us)
Async XLA Ops:
  3.5 10.2 %collective-permute-start.3 = (bf16[6,64,256]{2,1,0:T(8,128)(2,1)}, bf16[6,64,256]{2,1,0:T(8,128)(2,1)S(1)}, u32[]{:S(2)}, u32[]{:S(2)}) collective-permute-start(bf16[6,64,256]{2,1,0:T(8,128)(2,1)} %get-tuple-element.70.refs_4_), channel_id=1, source_target_pairs={{0,4},{4,0},{8,12},{12,8},{16,20},{20,16},{24,28},{28,24},{1,5},{5... | collective-permute-start | bytes 589832 | tf_op jit(solution)/shard_map/ppermute | solution.py:472
  6.5 8.0 %collective-permute-start.4 = (bf16[6,64,256]{2,1,0:T(8,128)(2,1)}, bf16[6,64,256]{2,1,0:T(8,128)(2,1)S(1)}, u32[]{:S(2)}, u32[]{:S(2)}) collective-permute-start(bf16[6,64,256]{2,1,0:T(8,128)(2,1)} %get-tuple-element.70.refs_4_), channel_id=1, source_target_pairs={{0,2},{1,3},{2,0},{3,1},{4,6},{5,7},{6,4},{7,5},{8,10},{9,11},{10,... | collective-permute-start | bytes 589832 | tf_op jit(solution)/shard_map/ppermute | solution.py:475
  8.0 20.5 %collective-permute-start = (bf16[9,64,256]{2,1,0:T(8,128)(2,1)}, bf16[9,64,256]{2,1,0:T(8,128)(2,1)S(1)}, u32[]{:S(2)}, u32[]{:S(2)}) collective-permute-start(bf16[9,64,256]{2,1,0:T(8,128)(2,1)} %get-tuple-element.67), channel_id=1, source_target_pairs={{0,4},{1,5},{2,6},{3,7},{4,0},{5,1},{6,2},{7,3},{8,12},{9,13},{10,... | collective-permute-start | bytes 884744 | tf_op jit(solution)/shard_map/ppermute | solution.py:486
  8.5 20.0 %collective-permute-start.1 = (bf16[9,64,256]{2,1,0:T(8,128)(2,1)}, bf16[9,64,256]{2,1,0:T(8,128)(2,1)S(1)}, u32[]{:S(2)}, u32[]{:S(2)}) collective-permute-start(bf16[9,64,256]{2,1,0:T(8,128)(2,1)} %get-tuple-element.68), channel_id=1, source_target_pairs={{0,2},{1,3},{2,0},{3,1},{4,6},{5,7},{6,4},{7,5},{8,10},{9,11},{10,... | collective-permute-start | bytes 884744 | tf_op jit(solution)/shard_map/ppermute | solution.py:486
  8.6 19.9 %collective-permute-start.2 = (bf16[9,64,256]{2,1,0:T(8,128)(2,1)}, bf16[9,64,256]{2,1,0:T(8,128)(2,1)S(1)}, u32[]{:S(2)}, u32[]{:S(2)}) collective-permute-start(bf16[9,64,256]{2,1,0:T(8,128)(2,1)} %get-tuple-element.69), channel_id=1, source_target_pairs={{0,6},{1,7},{2,4},{3,5},{4,2},{5,3},{6,0},{7,1},{8,14},{9,15},{10,... | collective-permute-start | bytes 884744 | tf_op jit(solution)/shard_map/ppermute | solution.py:486
  13.7 14.8 %collective-permute-start.6 = (bf16[6,64,256]{2,1,0:T(8,128)(2,1)S(1)}, bf16[6,64,256]{2,1,0:T(8,128)(2,1)S(1)}, u32[]{:S(2)}, u32[]{:S(2)}) collective-permute-start(bf16[6,64,256]{2,1,0:T(8,128)(2,1)S(1)} %get-tuple-element.71.refs_8_), channel_id=1, source_target_pairs={{0,4},{4,0},{8,12},{12,8},{16,20},{20,16},{24,28},{28,24},{1,5},{5... | collective-permute-start | bytes 589832 | tf_op jit(solution)/shard_map/ppermute | solution.py:472
  14.6 15.4 %collective-permute-start.5 = (bf16[6,64,256]{2,1,0:T(8,128)(2,1)S(1)}, bf16[6,64,256]{2,1,0:T(8,128)(2,1)S(1)}, u32[]{:S(2)}, u32[]{:S(2)}) collective-permute-start(bf16[6,64,256]{2,1,0:T(8,128)(2,1)S(1)} %collective-permute-done.3.refs_5_), channel_id=1, source_target_pairs={{0,2},{1,3},{2,0},{3,1},{4,6},{5,7},{6,4},{7,5},{8,10},{9,11},{10,... | collective-permute-start | bytes 589832 | tf_op jit(solution)/shard_map/ppermute | solution.py:475
  30.3 8.1 %collective-permute-start.11 = (bf16[2,2,6,64,256]{4,3,2,1,0:T(8,128)(2,1)S(1)}, bf16[2,2,6,64,256]{4,3,2,1,0:T(8,128)(2,1)S(1)}, u32[]{:S(2)}, u32[]{:S(2)}) collective-permute-start(bf16[2,2,6,64,256]{4,3,2,1,0:T(8,128)(2,1)S(1)} %get-tuple-element.83.refs_7_), channel_id=1, source_target_pairs={{0,1},{1,0},{2,3},{3,2},{4,5},{5,4},{6,7},{7,6},{8,9},{9,8},{10,11... | collective-permute-start | bytes 2359304 | tf_op jit(solution)/shard_map/ppermute | solution.py:475
  30.7 19.2 %collective-permute-start.15 = (bf16[2,6,64,256]{3,2,1,0:T(8,128)(2,1)S(1)}, bf16[2,6,64,256]{3,2,1,0:T(8,128)(2,1)S(1)}, u32[]{:S(2)}, u32[]{:S(2)}) collective-permute-start(bf16[2,6,64,256]{3,2,1,0:T(8,128)(2,1)S(1)} %get-tuple-element.89.refs_1_.refs_0_), channel_id=1, source_target_pairs={{0,2},{1,3},{2,0},{3,1},{4,6},{5,7},{6,4},{7,5},{8,10},{9,11},{10,... | collective-permute-start | bytes 1179656 | tf_op jit(solution)/shard_map/ppermute | solution.py:475
  32.2 17.7 %collective-permute-start.16 = (bf16[18,64,256]{2,1,0:T(8,128)(2,1)S(1)}, bf16[18,64,256]{2,1,0:T(8,128)(2,1)S(1)}, u32[]{:S(2)}, u32[]{:S(2)}) collective-permute-start(bf16[18,64,256]{2,1,0:T(8,128)(2,1)S(1)} %shard_map.80.refs_2_), channel_id=1, source_target_pairs={{0,4},{4,0},{8,12},{12,8},{16,20},{20,16},{24,28},{28,24},{1,5},{5... | collective-permute-start | bytes 1769480 | tf_op jit(solution)/shard_map/ppermute | solution.py:472
  35.8 7.5 %collective-permute-start.9 = (bf16[128,256]{1,0:T(8,128)(2,1)S(1)}, bf16[128,256]{1,0:T(8,128)(2,1)S(1)}, u32[]{:S(2)}, u32[]{:S(2)}) collective-permute-start(bf16[128,256]{1,0:T(8,128)(2,1)S(1)} %get-tuple-element.80), channel_id=1, source_target_pairs={{0,16},{4,20},{8,24},{12,28},{16,0},{20,4},{24,8},{28,12},{1,17},{... | collective-permute-start | bytes 196616 | tf_op jit(solution)/shard_map/ppermute | solution.py:472
  50.1 11.5 %collective-permute-start.21 = (bf16[2,6,64,256]{3,2,1,0:T(8,128)(2,1)S(1)}, bf16[2,6,64,256]{3,2,1,0:T(8,128)(2,1)S(1)}, u32[]{:S(2)}, u32[]{:S(2)}) collective-permute-start(bf16[2,6,64,256]{3,2,1,0:T(8,128)(2,1)S(1)} %get-tuple-element.97.refs_0_), channel_id=1, source_target_pairs={{0,2},{1,3},{2,0},{3,1},{4,6},{5,7},{6,4},{7,5},{8,10},{9,11},{10,... | collective-permute-start | bytes 1179656 | tf_op jit(solution)/shard_map/ppermute | solution.py:475
  55.1 9.5 %collective-permute-start.18 = (bf16[128,256]{1,0:T(8,128)(2,1)S(1)}, bf16[128,256]{1,0:T(8,128)(2,1)S(1)}, u32[]{:S(2)}, u32[]{:S(2)}) collective-permute-start(bf16[128,256]{1,0:T(8,128)(2,1)S(1)} %get-tuple-element.93), channel_id=1, source_target_pairs={{0,8},{4,12},{8,0},{12,4},{16,24},{20,28},{24,16},{28,20},{1,9},{5... | collective-permute-start | bytes 196616 | tf_op jit(solution)/shard_map/ppermute | solution.py:472
  55.2 9.5 %collective-permute-start.19 = (bf16[128,256]{1,0:T(8,128)(2,1)S(1)}, bf16[128,256]{1,0:T(8,128)(2,1)S(1)}, u32[]{:S(2)}, u32[]{:S(2)}) collective-permute-start(bf16[128,256]{1,0:T(8,128)(2,1)S(1)} %get-tuple-element.94), channel_id=1, source_target_pairs={{0,16},{4,20},{8,24},{12,28},{16,0},{20,4},{24,8},{28,12},{1,17},{... | collective-permute-start | bytes 196616 | tf_op jit(solution)/shard_map/ppermute | solution.py:472
  61.8 11.5 %collective-permute-start.26 = (bf16[2,6,64,256]{3,2,1,0:T(8,128)(2,1)S(1)}, bf16[2,6,64,256]{3,2,1,0:T(8,128)(2,1)S(1)}, u32[]{:S(2)}, u32[]{:S(2)}) collective-permute-start(bf16[2,6,64,256]{3,2,1,0:T(8,128)(2,1)S(1)} %get-tuple-element.104.refs_0_), channel_id=1, source_target_pairs={{0,2},{1,3},{2,0},{3,1},{4,6},{5,7},{6,4},{7,5},{8,10},{9,11},{10,... | collective-permute-start | bytes 1179656 | tf_op jit(solution)/shard_map/ppermute | solution.py:475
  65.7 7.9 %collective-permute-start.23 = (bf16[128,256]{1,0:T(8,128)(2,1)S(1)}, bf16[128,256]{1,0:T(8,128)(2,1)S(1)}, u32[]{:S(2)}, u32[]{:S(2)}) collective-permute-start(bf16[128,256]{1,0:T(8,128)(2,1)S(1)} %get-tuple-element.101), channel_id=1, source_target_pairs={{0,8},{4,12},{8,0},{12,4},{16,24},{20,28},{24,16},{28,20},{1,9},{5... | collective-permute-start | bytes 196616 | tf_op jit(solution)/shard_map/ppermute | solution.py:472
  65.8 15.4 %collective-permute-start.32 = (bf16[16,64,256]{2,1,0:T(8,128)(2,1)S(1)}, bf16[16,64,256]{2,1,0:T(8,128)(2,1)S(1)}, u32[]{:S(2)}, u32[]{:S(2)}) collective-permute-start(bf16[16,64,256]{2,1,0:T(8,128)(2,1)S(1)} %shard_map.90.refs_2_), channel_id=1, source_target_pairs={{0,4},{4,0},{8,12},{12,8},{16,20},{20,16},{24,28},{28,24},{1,5},{5... | collective-permute-start | bytes 1572872 | tf_op jit(solution)/shard_map/ppermute | solution.py:472
  66.4 8.8 %collective-permute-start.24 = (bf16[128,256]{1,0:T(8,128)(2,1)S(1)}, bf16[128,256]{1,0:T(8,128)(2,1)S(1)}, u32[]{:S(2)}, u32[]{:S(2)}) collective-permute-start(bf16[128,256]{1,0:T(8,128)(2,1)S(1)} %get-tuple-element.102), channel_id=1, source_target_pairs={{0,16},{4,20},{8,24},{12,28},{16,0},{20,4},{24,8},{28,12},{1,17},{... | collective-permute-start | bytes 196616 | tf_op jit(solution)/shard_map/ppermute | solution.py:472
  73.6 11.5 %collective-permute-start.31 = (bf16[2,6,64,256]{3,2,1,0:T(8,128)(2,1)S(1)}, bf16[2,6,64,256]{3,2,1,0:T(8,128)(2,1)S(1)}, u32[]{:S(2)}, u32[]{:S(2)}) collective-permute-start(bf16[2,6,64,256]{3,2,1,0:T(8,128)(2,1)S(1)} %get-tuple-element.108.refs_0_), channel_id=1, source_target_pairs={{0,2},{1,3},{2,0},{3,1},{4,6},{5,7},{6,4},{7,5},{8,10},{9,11},{10,... | collective-permute-start | bytes 1179656 | tf_op jit(solution)/shard_map/ppermute | solution.py:475
  76.8 10.1 %collective-permute-start.28 = (bf16[128,256]{1,0:T(8,128)(2,1)S(1)}, bf16[128,256]{1,0:T(8,128)(2,1)S(1)}, u32[]{:S(2)}, u32[]{:S(2)}) collective-permute-start(bf16[128,256]{1,0:T(8,128)(2,1)S(1)} %get-tuple-element.106.refs_1_.refs_4_.refs_5_.refs_9_), channel_id=1, source_target_pairs={{0,8},{4,12},{8,0},{12,4},{16,24},{20,28},{24,16},{28,20},{1,9},{5... | collective-permute-start | bytes 196616 | tf_op jit(solution)/shard_map/ppermute | solution.py:472
  77.0 9.8 %collective-permute-start.29 = (bf16[128,256]{1,0:T(8,128)(2,1)S(1)}, bf16[128,256]{1,0:T(8,128)(2,1)S(1)}, u32[]{:S(2)}, u32[]{:S(2)}) collective-permute-start(bf16[128,256]{1,0:T(8,128)(2,1)S(1)} %get-tuple-element.106.refs_1_.refs_4_.refs_5_.refs_9_), channel_id=1, source_target_pairs={{0,16},{4,20},{8,24},{12,28},{16,0},{20,4},{24,8},{28,12},{1,17},{... | collective-permute-start | bytes 196616 | tf_op jit(solution)/shard_map/ppermute | solution.py:472
  79.3 7.5 %collective-permute-start.30 = (bf16[128,256]{1,0:T(8,128)(2,1)S(1)}, bf16[128,256]{1,0:T(8,128)(2,1)S(1)}, u32[]{:S(2)}, u32[]{:S(2)}) collective-permute-start(bf16[128,256]{1,0:T(8,128)(2,1)S(1)} %get-tuple-element.106.refs_1_.refs_4_.refs_5_.refs_9_), channel_id=1, source_target_pairs={{0,24},{4,28},{8,16},{12,20},{16,8},{20,12},{24,0},{28,4},{1,25},{... | collective-permute-start | bytes 196616 | tf_op jit(solution)/shard_map/ppermute | solution.py:472
  85.3 11.5 %collective-permute-start.37 = (bf16[2,6,64,256]{3,2,1,0:T(8,128)(2,1)S(1)}, bf16[2,6,64,256]{3,2,1,0:T(8,128)(2,1)S(1)}, u32[]{:S(2)}, u32[]{:S(2)}) collective-permute-start(bf16[2,6,64,256]{3,2,1,0:T(8,128)(2,1)S(1)} %get-tuple-element.112.refs_0_), channel_id=1, source_target_pairs={{0,2},{1,3},{2,0},{3,1},{4,6},{5,7},{6,4},{7,5},{8,10},{9,11},{10,... | collective-permute-start | bytes 1179656 | tf_op jit(solution)/shard_map/ppermute | solution.py:475
  88.4 10.6 %collective-permute-start.34 = (bf16[128,256]{1,0:T(8,128)(2,1)S(1)}, bf16[128,256]{1,0:T(8,128)(2,1)S(1)}, u32[]{:S(2)}, u32[]{:S(2)}) collective-permute-start(bf16[128,256]{1,0:T(8,128)(2,1)S(1)} %shard_map.92.refs_4_.refs_1_.refs_5_.refs_3_), channel_id=1, source_target_pairs={{0,8},{4,12},{8,0},{12,4},{16,24},{20,28},{24,16},{28,20},{1,9},{5... | collective-permute-start | bytes 196616 | tf_op jit(solution)/shard_map/ppermute | solution.py:472
  88.5 10.5 %collective-permute-start.35 = (bf16[128,256]{1,0:T(8,128)(2,1)S(1)}, bf16[128,256]{1,0:T(8,128)(2,1)S(1)}, u32[]{:S(2)}, u32[]{:S(2)}) collective-permute-start(bf16[128,256]{1,0:T(8,128)(2,1)S(1)} %shard_map.92.refs_4_.refs_1_.refs_5_.refs_3_), channel_id=1, source_target_pairs={{0,16},{4,20},{8,24},{12,28},{16,0},{20,4},{24,8},{28,12},{1,17},{... | collective-permute-start | bytes 196616 | tf_op jit(solution)/shard_map/ppermute | solution.py:472
  91.0 8.0 %collective-permute-start.36 = (bf16[128,256]{1,0:T(8,128)(2,1)S(1)}, bf16[128,256]{1,0:T(8,128)(2,1)S(1)}, u32[]{:S(2)}, u32[]{:S(2)}) collective-permute-start(bf16[128,256]{1,0:T(8,128)(2,1)S(1)} %shard_map.92.refs_4_.refs_1_.refs_5_.refs_3_), channel_id=1, source_target_pairs={{0,24},{4,28},{8,16},{12,20},{16,8},{20,12},{24,0},{28,4},{1,25},{... | collective-permute-start | bytes 196616 | tf_op jit(solution)/shard_map/ppermute | solution.py:472
  97.0 11.5 %collective-permute-start.42 = (bf16[2,6,64,256]{3,2,1,0:T(8,128)(2,1)S(1)}, bf16[2,6,64,256]{3,2,1,0:T(8,128)(2,1)S(1)}, u32[]{:S(2)}, u32[]{:S(2)}) collective-permute-start(bf16[2,6,64,256]{3,2,1,0:T(8,128)(2,1)S(1)} %get-tuple-element.115.refs_0_), channel_id=1, source_target_pairs={{0,2},{1,3},{2,0},{3,1},{4,6},{5,7},{6,4},{7,5},{8,10},{9,11},{10,... | collective-permute-start | bytes 1179656 | tf_op jit(solution)/shard_map/ppermute | solution.py:475
  100.1 11.0 %collective-permute-start.39 = (bf16[128,256]{1,0:T(8,128)(2,1)S(1)}, bf16[128,256]{1,0:T(8,128)(2,1)S(1)}, u32[]{:S(2)}, u32[]{:S(2)}) collective-permute-start(bf16[128,256]{1,0:T(8,128)(2,1)S(1)} %shard_map.95.refs_4_.refs_1_.refs_2_), channel_id=1, source_target_pairs={{0,8},{4,12},{8,0},{12,4},{16,24},{20,28},{24,16},{28,20},{1,9},{5... | collective-permute-start | bytes 196616 | tf_op jit(solution)/shard_map/ppermute | solution.py:472
  100.2 11.0 %collective-permute-start.40 = (bf16[128,256]{1,0:T(8,128)(2,1)S(1)}, bf16[128,256]{1,0:T(8,128)(2,1)S(1)}, u32[]{:S(2)}, u32[]{:S(2)}) collective-permute-start(bf16[128,256]{1,0:T(8,128)(2,1)S(1)} %shard_map.95.refs_4_.refs_1_.refs_2_), channel_id=1, source_target_pairs={{0,16},{4,20},{8,24},{12,28},{16,0},{20,4},{24,8},{28,12},{1,17},{... | collective-permute-start | bytes 196616 | tf_op jit(solution)/shard_map/ppermute | solution.py:472
  102.7 8.4 %collective-permute-start.41 = (bf16[128,256]{1,0:T(8,128)(2,1)S(1)}, bf16[128,256]{1,0:T(8,128)(2,1)S(1)}, u32[]{:S(2)}, u32[]{:S(2)}) collective-permute-start(bf16[128,256]{1,0:T(8,128)(2,1)S(1)} %shard_map.95.refs_4_.refs_1_.refs_2_), channel_id=1, source_target_pairs={{0,24},{4,28},{8,16},{12,20},{16,8},{20,12},{24,0},{28,4},{1,25},{... | collective-permute-start | bytes 196616 | tf_op jit(solution)/shard_map/ppermute | solution.py:472
  108.7 8.7 %collective-permute-start.47 = (bf16[2,4,64,256]{3,2,1,0:T(8,128)(2,1)S(1)}, bf16[2,4,64,256]{3,2,1,0:T(8,128)(2,1)S(1)}, u32[]{:S(2)}, u32[]{:S(2)}) collective-permute-start(bf16[2,4,64,256]{3,2,1,0:T(8,128)(2,1)S(1)} %get-tuple-element.118.refs_0_), channel_id=1, source_target_pairs={{0,2},{1,3},{2,0},{3,1},{4,6},{5,7},{6,4},{7,5},{8,10},{9,11},{10,... | collective-permute-start | bytes 786440 | tf_op jit(solution)/shard_map/ppermute | solution.py:475
  112.1 8.7 %collective-permute-start.45 = (bf16[128,256]{1,0:T(8,128)(2,1)S(1)}, bf16[128,256]{1,0:T(8,128)(2,1)S(1)}, u32[]{:S(2)}, u32[]{:S(2)}) collective-permute-start(bf16[128,256]{1,0:T(8,128)(2,1)S(1)} %shard_map.98.refs_2_.refs_1_), channel_id=1, source_target_pairs={{0,16},{4,20},{8,24},{12,28},{16,0},{20,4},{24,8},{28,12},{1,17},{... | collective-permute-start | bytes 196616 | tf_op jit(solution)/shard_map/ppermute | solution.py:472
  (30 other events, 175.7 us)
